TPU v7x, 32 devices: a whole 2x2x4 slice. The times are simulated.
32 devices in a mesh: groups: 2 (over y), sector: 4 (over z), mpo: 4 (over x, core).
Axes of the slice: x: 2, y: 2, z: 4, core: 2. Of those that a mesh axis runs over, the one named last changes fastest.
Arguments:
- wavefunction: float32 [1024, 512], P(('groups', 'sector')), parts along dimension 0
- left_environment: float32 [16, 1024, 128], P('mpo', ('groups', 'sector')), parts along dimension 1, may hold values from -0.125 to 0.125
- right_environment: float32 [16, 1024, 128], P('mpo', ('groups', 'sector')), parts along dimension 1, may hold values from -0.5 to 0.5
- left_sizes: int32 [8], P('groups'), parts along dimension 0, may hold values from 32 to 128, as said below
- right_sizes: int32 [8], P('groups'), parts along dimension 0, may hold values from 32 to 128, as said below
- sector_pairs: int32 [8, 4], P('groups'), parts along dimension 0, may hold values from 0 to 1, as said below
Outputs:
- product: float32 [1024, 512], P(('groups', 'sector')), parts along dimension 0
- ritz_value: float32 [2], P('groups'), parts along dimension 0
There are 2 independent parts, one for each index of `groups`. A program takes and returns all parts, laid end to end along the dimension named above; each array names one. Nothing has to cross between parts.
Inputs may be any that keep to these rules, and one draw needn't show every extreme that they name: `left_sizes`: some left sector has exactly 128 states. `right_sizes`: some right sector has exactly 128 states. `sector_pairs`: every left sector has at least one allowed right sector.
All inputs are finite; a program needn't handle non-finite values.
Results may differ from a plain program's by a relative error of at most 0.0002.
Values sent between devices are 32-bit elements; how exact they have to be, the bound alone decides.
No kernel may reach another device: no remote copies, remote signals or barrier semaphores. Data moves between devices by JAX's collectives and lax.ppermute only.
A program may use at most 64 MiB of HBM per device.

v0:
```python
import jax
import jax.numpy as jnp
from jax import lax
from jax.sharding import PartitionSpec as P

EXACT = lax.Precision.HIGHEST
TINY = 1e-06


def left_mask(left_sizes, right_sizes, sector_pairs, left_width, right_width):
    sector = lax.axis_index("sector")
    own_size = lax.dynamic_index_in_dim(left_sizes, sector, 0, keepdims=False)
    own_pairs = lax.dynamic_index_in_dim(sector_pairs, sector, 0, keepdims=False)
    row_valid = (jnp.arange(left_width) < own_size).astype(jnp.float32)
    col_valid = (jnp.arange(right_width)[None, :] < right_sizes[:, None]).astype(jnp.float32)
    col_valid = col_valid * own_pairs[:, None].astype(jnp.float32)
    return row_valid[:, None] * col_valid.reshape(1, -1)


def right_mask(left_sizes, right_sizes, sector_pairs, left_width, right_width):
    sector = lax.axis_index("sector")
    own_size = lax.dynamic_index_in_dim(right_sizes, sector, 0, keepdims=False)
    own_pairs = lax.dynamic_index_in_dim(sector_pairs, sector, 1, keepdims=False)
    row_valid = (jnp.arange(left_width)[None, :] < left_sizes[:, None]).astype(jnp.float32)
    row_valid = row_valid * own_pairs[:, None].astype(jnp.float32)
    col_valid = (jnp.arange(right_width) < own_size).astype(jnp.float32)
    return row_valid.reshape(-1, 1) * col_valid[None, :]


def left_contract(operand, left_environment):
    return jnp.einsum("wik,kc->wic", left_environment, operand, precision=EXACT)


def channel_total(partial_value):
    return lax.psum(partial_value, "mpo")


def davidson_step(vector, first_image, total_cells):
    cross_term, self_term = lax.psum(
        (jnp.sum(vector * first_image), jnp.sum(vector * vector)), "sector"
    )
    ritz_value = cross_term / (self_term + TINY)
    residual = first_image - ritz_value * vector
    square_total = lax.psum(jnp.sum(residual * residual), "sector")
    following = residual / jnp.sqrt(square_total / total_cells + TINY)
    return (following, ritz_value)


def per_device(
    wavefunction, left_environment, right_environment, left_sizes, right_sizes, sector_pairs
):
    left_width = left_environment.shape[2]
    right_width = right_environment.shape[2]
    sectors = lax.axis_size("sector")
    total_cells = float(sectors * left_width * sectors * right_width)
    left_valid = left_mask(left_sizes, right_sizes, sector_pairs, left_width, right_width)
    vector = wavefunction * left_valid
    right_valid = right_mask(left_sizes, right_sizes, sector_pairs, left_width, right_width)
    halfway = left_contract(vector, left_environment)
    arrived, vector_right = (
        lax.all_to_all(halfway, "sector", split_axis=2, concat_axis=1, tiled=True),
        lax.all_to_all(vector[None], "sector", split_axis=2, concat_axis=1, tiled=True),
    )
    partial_value = jnp.einsum("wrc,wjc->rj", arrived, right_environment, precision=EXACT)
    first_image = channel_total(partial_value) * right_valid
    following, ritz_value = davidson_step(vector_right[0], first_image, total_cells)
    outgoing = jnp.einsum("rc,wjc->wrj", following, right_environment, precision=EXACT)
    returned = lax.all_to_all(outgoing, "sector", split_axis=1, concat_axis=2, tiled=True)
    partial_left = jnp.einsum("wik,wkc->ic", left_environment, returned, precision=EXACT)
    product = channel_total(partial_left) * left_valid
    return (product, jnp.reshape(ritz_value, (1,)))


def solution(mesh):
    return jax.shard_map(
        per_device,
        mesh=mesh,
        in_specs=(
            P(("groups", "sector"), None),
            P("mpo", ("groups", "sector"), None),
            P("mpo", ("groups", "sector"), None),
            P("groups"),
            P("groups"),
            P("groups", None),
        ),
        out_specs=(P(("groups", "sector"), None), P("groups")),
        check_vma=False,
    )
```

profile of v0, /device:TPU:0, one launch (start us, length us, event | category | flops | bytes accessed | tf_op | source)
XLA Modules:
  0.0 181.3 jit_solution(4967855876234697629)
XLA Ops:
  7.2 0.0 copy-start
  7.2 0.0 copy-start.3
  7.2 0.7 copy-done.3
  7.9 0.0 copy-start.5
  7.9 0.6 copy-done.5
  8.6 0.6 dynamic_slice.15
  9.1 0.6 compare_convert_fusion.1
  9.8 0.0 copy-start.4
  9.8 1.1 copy.13
  10.9 0.0 copy-done.4
  10.9 0.1 select_bitcast_fusion.1
  11.0 0.0 copy-start.2
  11.0 0.8 multiply_multiply_fusion.1
  11.8 0.1 copy-done.2
  11.9 1.9 %convolution_bitcast_fusion.1 = f32[4,128,512]{1,2,0:T(8,128)S(1)} fusion(f32[4,128,128]{2,1,0:T(8,128)S(1)} %copy-done.2, f32[128,512]{0,1:T(8,128)} %multiply_multiply_fusion.1), kind=kOutput, calls=%fused_computation.1 | convolution fusion | flops 402653184 | bytes 1572864 | tf_op jit(solution)/shard_map/wik,kc->wic/dot_general | solution.py:31
  13.9 1.7 copy.14
  15.5 6.3 %all-to-all-start = ((f32[4,128,512]{1,0,2:T(4,128)}), f32[4,128,512]{1,0,2:T(4,128)S(1)}, u32[]{:S(2)}, u32[]{:S(2)}) async-start(f32[4,128,512]{1,0,2:T(4,128)} %copy.14), calls=%async_computation | async-start | bytes 2097152 | tf_op jit(solution)/shard_map/all_to_all | solution.py:61
  21.9 0.2 convert_reduce_fusion
  22.0 0.6 dynamic_slice.18
  22.6 24.9 %all-to-all-done = f32[4,128,512]{1,0,2:T(4,128)S(1)} async-done(((f32[4,128,512]{1,0,2:T(4,128)}), f32[4,128,512]{1,0,2:T(4,128)S(1)}, u32[]{:S(2)}, u32[]{:S(2)}) %all-to-all-start) | async-done | bytes 1048608 | tf_op jit(solution)/shard_map/all_to_all | solution.py:61
  47.6 3.4 %all-to-all-start.1 = ((f32[1,128,512]{1,0,2:T(1,128)}), f32[1,128,512]{1,0,2:T(1,128)S(1)}, u32[]{:S(2)}, u32[]{:S(2)}) async-start(f32[1,128,512]{1,0,2:T(1,128)} %bitcast.12), calls=%async_computation.1 | async-start | bytes 524288 | tf_op jit(solution)/shard_map/all_to_all | solution.py:62
  51.0 0.0 all-reduce.4.cloned.1.call-start
  51.0 0.1 select_bitcast_fusion
  51.1 0.4 copy.15
  51.5 0.0 copy-done
  51.5 1.7 convolution_bitcast_fusion.3
  53.2 0.0 all-reduce.4.cloned.1.call-update
  53.2 0.0 all-reduce.6.cloned.1.call-start
  53.3 0.7 compare_convert_fusion
  53.9 5.4 %all-to-all-done.1 = f32[1,128,512]{1,0,2:T(1,128)S(1)} async-done(((f32[1,128,512]{1,0,2:T(1,128)}), f32[1,128,512]{1,0,2:T(1,128)S(1)}, u32[]{:S(2)}, u32[]{:S(2)}) %all-to-all-start.1) | async-done | bytes 262176 | tf_op jit(solution)/shard_map/all_to_all | solution.py:62
  59.3 0.1 copy.17
  59.5 0.7 fusion.3
  60.1 27.4 %all-reduce.4.cloned.1.call-done = f32[512,128]{1,0:T(8,128)} async-done(((f32[512,128]{1,0:T(8,128)}), f32[512,128]{1,0:T(8,128)}) %all-reduce.4.cloned.1.call-update) | async-done | bytes 262160 | tf_op jit(solution)/shard_map/psum | solution.py:35
  87.6 0.0 copy-start.1
  87.6 1.8 fusion
  89.4 12.3 %all-reduce = (f32[]{:T(128)}, f32[]{:T(128)}) all-reduce(f32[]{:T(128)} %fusion, f32[]{:T(128)} %fusion.3), channel_id=1, replica_groups=mesh['groups'=2,'sector'=4,'mpo'=4] {'sector'}, use_global_device_ids=true, to_apply=%region_2.3 | all-reduce | flops 2 | bytes 16 | tf_op jit(solution)/shard_map/psum | solution.py:39
  103.0 0.0 copy-done.1
  103.0 0.7 multiply_reduce_fusion
  103.7 9.0 %psum.38 = f32[]{:T(128)} all-reduce(f32[]{:T(128)} %get-tuple-element.8), channel_id=1, replica_groups=mesh['groups'=2,'sector'=4,'mpo'=4] {'sector'}, use_global_device_ids=true, to_apply=%region_6.7 | all-reduce | flops 1 | bytes 8 | tf_op jit(solution)/shard_map/psum | solution.py:44
  113.4 1.0 convolution_bitcast_fusion
  114.4 0.7 copy.18
  115.1 23.7 %all_to_all.51 = f32[4,512,128]{2,0,1:T(4,128)S(1)} all-to-all(f32[4,512,128]{2,0,1:T(4,128)S(1)} %copy.18), channel_id=1, replica_groups=mesh['groups'=2,'sector'=4,'mpo'=4] {'sector'}, dimensions={1} | all-to-all | bytes 2097152 | tf_op jit(solution)/shard_map/all_to_all | solution.py:68
  138.7 0.4 copy.19
  139.1 1.7 convolution_bitcast_fusion.2
  140.8 0.0 all-reduce.6.cloned.1.call-update
  140.8 30.6 %all-reduce.6.cloned.1.call-done = f32[128,512]{0,1:T(8,128)} async-done(((f32[128,512]{0,1:T(8,128)}), f32[128,512]{0,1:T(8,128)}) %all-reduce.6.cloned.1.call-update) | async-done | bytes 262160 | tf_op jit(solution)/shard_map/psum | solution.py:35
  171.4 1.1 multiply_multiply_fusion
  172.5 0.8 copy.20
  (1 shorter events, 0.0 us)
Async XLA Ops:
  7.2 44.3 %copy-start = (f32[4,128,128]{2,1,0:T(8,128)S(1)}, f32[4,128,128]{2,1,0:T(8,128)}, u32[]{:S(2)}) copy-start(f32[4,128,128]{2,1,0:T(8,128)} %param.8) | copy-start | bytes 786436
  7.2 0.7 copy-start.3
  7.9 0.7 copy-start.5
  9.8 1.1 copy-start.4
  11.0 1.0 copy-start.2
  15.5 32.0 %all-to-all-start = ((f32[4,128,512]{1,0,2:T(4,128)}), f32[4,128,512]{1,0,2:T(4,128)S(1)}, u32[]{:S(2)}, u32[]{:S(2)}) async-start(f32[4,128,512]{1,0,2:T(4,128)} %copy.14), calls=%async_computation | async-start | bytes 2097152 | tf_op jit(solution)/shard_map/all_to_all | solution.py:61
  47.6 11.8 %all-to-all-start.1 = ((f32[1,128,512]{1,0,2:T(1,128)}), f32[1,128,512]{1,0,2:T(1,128)S(1)}, u32[]{:S(2)}, u32[]{:S(2)}) async-start(f32[1,128,512]{1,0,2:T(1,128)} %bitcast.12), calls=%async_computation.1 | async-start | bytes 524288 | tf_op jit(solution)/shard_map/all_to_all | solution.py:62
  51.0 36.6 %all-reduce.4.cloned.1.call-start = ((), (), s32[]{:S(2)}) async-start(), calls=%async_computation.3 | async-start | bytes 524288 | tf_op jit(solution)/shard_map/psum | solution.py:35
  53.2 118.2 %all-reduce.6.cloned.1.call-start = ((), (), s32[]{:S(2)}) async-start(), calls=%async_computation.4 | async-start | bytes 524288 | tf_op jit(solution)/shard_map/psum | solution.py:35
  87.6 15.4 %copy-start.1 = (f32[512,128]{1,0:T(8,128)S(1)}, f32[512,128]{1,0:T(8,128)}, u32[]{:S(2)}) copy-start(f32[512,128]{1,0:T(8,128)} %all-reduce.4.cloned.1.call-done) | copy-start | bytes 786436
Sparse Core Ops, SparseCore 0:
  54.2 33.3 all-reduce.3
  140.9 30.4 all-reduce.5
where the time goes:
time: 182 us; the launch traced here: 181 us
  waiting for transfers between devices  88.4 us (49%)
  blocking collectives  44.9 us (25%)
  between operations  17.3 us (10%)
  starting transfers between devices  9.81 us (5%)
  local copies, waits for them, and re-layouts  7.77 us (4%)
  other arithmetic  6.73 us (4%)
  matrix products  6.29 us (3%)
    psum x2, waiting for transfers between devices, channel_total(): return lax.psum(partial_value, 'mpo')  58 us
    all_to_all x1, waiting for transfers between devices, per_device(): lax.all_to_all(halfway, 'sector', split_axis=2, concat_axis=1, tiled=True)  24.9 us
    all_to_all x1, blocking collectives, per_device(): lax.all_to_all(outgoing, 'sector', split_axis=1, concat_axis=2, tiled=True)  23.7 us
    psum x1, blocking collectives, davidson_step(): lax.psum((jnp.sum(vector * first_image), jnp.sum(vector * vector)), 'sect...  12.3 us
    psum x1, blocking collectives, davidson_step(): square_total = lax.psum(jnp.sum(residual * residual), 'sector')  8.97 us
    all_to_all x1, starting transfers between devices, per_device(): lax.all_to_all(halfway, 'sector', split_axis=2, concat_axis=1, tiled=True)  6.32 us
    all_to_all x1, waiting for transfers between devices, per_device(): lax.all_to_all(vector[None], 'sector', split_axis=2, concat_axis=1, tiled...  5.42 us
  transfers between devices with their start and end apart: 4, of which 4 were waited for; matrix products, arithmetic and copies ran while one was open for 2% of the time, Pallas kernels for 0%

commit v1 on v0

v1 whole, which is shorter than its diff:
```python
import functools

import jax
import jax.numpy as jnp
from jax import lax
from jax.experimental import pallas as pl
from jax.experimental.pallas import tpu as pltpu
from jax.sharding import PartitionSpec as P

EXACT = lax.Precision.HIGHEST
TINY = 1e-06
VMEM = pl.BlockSpec(memory_space=pltpu.VMEM)
SMEM = pl.BlockSpec(memory_space=pltpu.SMEM)
F32 = jnp.float32


def dot_nn(a, b):
    return lax.dot_general(
        a, b, (((1,), (0,)), ((), ())), precision=EXACT, preferred_element_type=F32
    )


def dot_nt(a, b):
    return lax.dot_general(
        a, b, (((1,), (1,)), ((), ())), precision=EXACT, preferred_element_type=F32
    )


def block_valid(left_sizes, right_sizes, pairs, a, b, rows, cols):
    row = lax.broadcasted_iota(jnp.int32, (rows, cols), 0) < left_sizes[a]
    col = lax.broadcasted_iota(jnp.int32, (rows, cols), 1) < right_sizes[b]
    return (row & col).astype(F32) * pairs[a, b].astype(F32)


def call(body, outs, n_small, n_big, **kw):
    return pl.pallas_call(
        body,
        out_shape=outs,
        in_specs=[SMEM] * n_small + [VMEM] * n_big,
        out_specs=[VMEM] * len(outs),
        compiler_params=pltpu.CompilerParams(vmem_limit_bytes=32 * 1024 * 1024),
        **kw,
    )


def slot_column(slot, sector):
    low = sector < 2
    if slot == 0:
        return sector
    if slot == 1:
        return sector ^ 1
    if slot == 2:
        return jnp.where(low, 2, 1)
    return jnp.where(low, 3, 0)


def half_body(left_sizes, right_sizes, pairs, wave, left, vector, halfway):
    sector = lax.axis_index("sector")
    channels, rows, _ = left.shape
    sectors, _, inner = halfway.shape
    cols = inner // channels
    for b in range(sectors):
        at = slice(b * cols, (b + 1) * cols)
        vector[:, at] = wave[:, at] * block_valid(
            left_sizes, right_sizes, pairs, sector, b, rows, cols
        )
    for w in range(channels):
        part = dot_nn(left[w], vector[...])
        for b in range(sectors):
            halfway[b, :, w * cols : (w + 1) * cols] = part[:, b * cols : (b + 1) * cols]


def pick(refs, w, sector):
    if len(refs) == 1:
        return refs[0][w]
    middle = (sector == 1) | (sector == 2)
    return jnp.where(middle, refs[0][w], refs[1][w])


def group(refs, ways):
    out, k = [], 0
    for n in ways:
        out.append(refs[k : k + n])
        k += n
    return out


def first_body(slots, ways, halfway, *refs):
    out = refs[-1]
    sector = lax.axis_index("sector")
    rights = group(refs[:-1], ways)
    for k, slot in enumerate(slots):
        b = slot_column(slot, sector)
        channels, cols, _ = rights[k][0].shape
        total = None
        for w in range(channels):
            part = dot_nt(
                halfway[b, :, w * cols : (w + 1) * cols], pick(rights[k], w, sector)
            )
            total = part if total is None else total + part
        out[k] = total


def second_body(slots, ways, left_sizes, right_sizes, pairs, own, other, vector, left, *refs):
    image, partial, sums = refs[-3:]
    sector = lax.axis_index("sector")
    rights = group(refs[:-3], ways)
    channels, rows, _ = left.shape
    cross = jnp.zeros((1, 1), F32)
    square = jnp.zeros((1, 1), F32)
    vectors = []
    for k, slot in enumerate(slots):
        b = slot_column(slot, sector)
        cols = own.shape[2]
        valid = block_valid(left_sizes, right_sizes, pairs, sector, b, rows, cols)
        here = (own[k] + other[k]) * valid
        image[k] = here
        v = vector[:, pl.ds(pl.multiple_of(b * cols, cols), cols)]
        vectors.append(v)
        cross += jnp.sum(v * here, keepdims=True)
        square += jnp.sum(v * v, keepdims=True)
        total = None
        for w in range(channels):
            part = dot_nt(dot_nn(left[w], here), pick(rights[k], w, sector))
            total = part if total is None else total + part
        partial[k] = total
    ratio = jnp.where(square > 0, cross / jnp.where(square > 0, square, 1.0), 0.0)
    rest = jnp.zeros((1, 1), F32)
    for k in range(len(slots)):
        away = image[k] - ratio * vectors[k]
        rest += jnp.sum(away * away, keepdims=True)
    row = lax.broadcasted_iota(jnp.int32, sums.shape, 0)
    sums[...] = jnp.where(row == 0, cross, jnp.where(row == 1, square, rest))


def last_body(slots_a, slots_b, cells, left_sizes, right_sizes, pairs, *refs):
    sums = refs[:8]
    own_a, other_a, image_a, own_b, other_b, image_b, product, ritz = refs[8:]
    sector = lax.axis_index("sector")


    def added(terms):
        while len(terms) > 1:
            terms = [x + y for x, y in zip(terms[::2], terms[1::2])]
        return terms[0]

    value = added([s[0:1, :] for s in sums]) / (added([s[1:2, :] for s in sums]) + TINY)
    rests = []
    for s in sums:
        c = s[1:2, :]
        ratio = jnp.where(c > 0, s[0:1, :] / jnp.where(c > 0, c, 1.0), 0.0)
        rests.append(s[2:3, :] + (ratio - value) * (ratio - value) * c)
    rest = added(rests)
    scale = 1.0 / jnp.sqrt(rest / cells + TINY)
    ritz[...] = jnp.broadcast_to(value, ritz.shape)
    for slots, own, other, image in (
        (slots_a, own_a, other_a, image_a),
        (slots_b, own_b, other_b, image_b),
    ):
        for k, slot in enumerate(slots):
            b = slot_column(slot, sector)
            _, rows, cols = own.shape
            valid = block_valid(left_sizes, right_sizes, pairs, sector, b, rows, cols)
            out = ((own[k] + other[k]) * valid - value * image[k]) * scale
            product[:, pl.ds(pl.multiple_of(b * cols, cols), cols)] = out


def line_device(wave, left, right, left_sizes, right_sizes, pairs):
    channels, rows, _ = left.shape
    cols = right.shape[2]
    sectors = 4
    cells = float(sectors * rows * sectors * cols)
    small = (left_sizes, right_sizes, pairs)

    def outer(x):
        return lax.ppermute(x, "sector", [(0, 1), (1, 0), (2, 3), (3, 2)])

    def inner(x):
        return lax.ppermute(x, "sector", [(1, 2), (2, 1), (0, 0), (3, 3)])

    def core(x):
        return lax.ppermute(x, "mpo", [(0, 1), (1, 0), (2, 3), (3, 2)])

    def across(x):
        return lax.ppermute(x, "mpo", [(0, 2), (1, 3), (2, 0), (3, 1)])

    def shape(*dims):
        return jax.ShapeDtypeStruct(dims, F32)

    out1 = outer(right)
    in1 = inner(right)
    vector, halfway = call(
        half_body, [shape(rows, sectors * cols), shape(sectors, rows, channels * cols)], 3, 2
    )(*small, wave, left)
    in2 = inner(out1)
    out2 = outer(in1)
    out3 = outer(in2)

    groups = (
        ((0, 1, 2), (1, 1, 2), (right, out1, in1, out2)),
        ((3,), (2,), (in2, out3)),
    )
    images, totals, sums = [], [], []
    for slots, ways, rights in groups:
        n = len(slots)
        (partial,) = call(
            functools.partial(first_body, slots, ways), [shape(n, rows, cols)], 0, 1 + len(rights)
        )(halfway, *rights)
        both = partial + core(partial)
        image, partial, total = call(
            functools.partial(second_body, slots, ways),
            [shape(n, rows, cols), shape(n, rows, cols), shape(8, cols)],
            3,
            4 + len(rights),
        )(*small, both, across(both), vector, left, *rights)
        both = partial + core(partial)
        images.append(image)
        totals.append((both, across(both)))
        sums.append(total)

    mine = jnp.concatenate(sums)
    near = lax.ppermute(mine, "sector", [(0, 1), (1, 0), (2, 3), (3, 2)])
    far = lax.ppermute(mine, "sector", [(0, 2), (2, 0), (1, 3), (3, 1)])
    cross = lax.ppermute(mine, "sector", [(0, 3), (3, 0), (1, 2), (2, 1)])
    everyone = [s[i : i + 8] for s in (mine, near, far, cross) for i in (0, 8)]
    product, ritz = call(
        functools.partial(last_body, groups[0][0], groups[1][0], cells),
        [shape(rows, sectors * cols), shape(8, cols)],
        3,
        14,
    )(*small, *everyone, *totals[0], images[0], *totals[1], images[1])
    return product, ritz[0, :1]


def wide_device(wave, left, right, left_sizes, right_sizes, pairs):
    sector = lax.axis_index("sector")
    sectors = lax.axis_size("sector")
    channels, rows, _ = left.shape
    cols = right.shape[2]
    cells = float(sectors * rows * sectors * cols)
    own = lax.dynamic_index_in_dim(pairs, sector, 0, keepdims=False).astype(F32)
    size = lax.dynamic_index_in_dim(left_sizes, sector, 0, keepdims=False)
    row = (jnp.arange(rows) < size).astype(F32)
    col = (jnp.arange(cols)[None, :] < right_sizes[:, None]).astype(F32) * own[:, None]
    valid = row[:, None] * col.reshape(1, -1)
    vector = wave * valid
    rights = lax.all_gather(right, "sector", axis=1)

    def image_of(v):
        half = jnp.einsum("wik,kbc->wibc", left, v.reshape(rows, sectors, cols), precision=EXACT)
        out = jnp.einsum("wibc,wbjc->ibj", half, rights, precision=EXACT)
        return lax.psum(out.reshape(rows, sectors * cols), "mpo") * valid

    first = image_of(vector)
    cross, square = lax.psum((jnp.sum(vector * first), jnp.sum(vector * vector)), "sector")
    value = cross / (square + TINY)
    residual = first - value * vector
    rest = lax.psum(jnp.sum(residual * residual), "sector")
    product = image_of(residual / jnp.sqrt(rest / cells + TINY))
    return product, jnp.reshape(value, (1,))


def solution(mesh):
    line = mesh.shape["sector"] == 4 and mesh.shape["mpo"] == 4
    return jax.shard_map(
        line_device if line else wide_device,
        mesh=mesh,
        in_specs=(
            P(("groups", "sector"), None),
            P("mpo", ("groups", "sector"), None),
            P("mpo", ("groups", "sector"), None),
            P("groups"),
            P("groups"),
            P("groups", None),
        ),
        out_specs=(P(("groups", "sector"), None), P("groups")),
        check_vma=False,
    )
```

time: 182 us -> 57.1 us (0.31)
  waiting for transfers between devices: 88.4 us -> 13.6 us
  blocking collectives: 44.9 us -> 0 us
  starting transfers between devices: 9.81 us -> 27.3 us
  between operations: 17.3 us -> 0.78 us
  Pallas kernels: 0 us -> 10.7 us
  other arithmetic: 6.73 us -> 0.07 us
  matrix products: 6.29 us -> 0 us
  local copies, waits for them, and re-layouts: 7.77 us -> 4.41 us
    psum x2 -> x0, waiting for transfers between devices: 58 us -> none  [channel_total(): return lax.psum(partial_value, 'mpo')]
    all_to_all x2 -> x0, waiting for transfers between devices: 30.4 us -> none  [the longest x1 24.9 us: per_device(): lax.all_to_all(halfway, 'sector', split_axis=2, concat_axis=1, tiled=True)]
    ppermute x0 -> x16, starting transfers between devices: none -> 27.3 us  [the longest x3 14.7 us: outer(): return lax.ppermute(x, 'sector', [(0, 1), (1, 0), (2, 3), (3, 2)])]
    all_to_all x1 -> x0, blocking collectives: 23.7 us -> none  [per_device(): lax.all_to_all(outgoing, 'sector', split_axis=1, concat_axis=2, tiled=True)]
    psum x2 -> x0, blocking collectives: 21.3 us -> none  [the longest x1 12.3 us: davidson_step(): lax.psum((jnp.sum(vector * first_image), jnp.sum(vector * vector)), 'sect...]
    ppermute x0 -> x16, waiting for transfers between devices: none -> 13.6 us  [the longest x3 5.31 us: outer(): return lax.ppermute(x, 'sector', [(0, 1), (1, 0), (2, 3), (3, 2)])]
    pallas_call x0 -> x6, Pallas kernels: none -> 10.7 us  [the longest x2 5.22 us: line_device(): call(functools.partial(second_body, slots, ways), [shape(n, rows, cols),...]
    all_to_all x2 -> x0, starting transfers between devices: 9.73 us -> none  [the longest x1 6.32 us: per_device(): lax.all_to_all(halfway, 'sector', split_axis=2, concat_axis=1, tiled=True)]
  transfers between devices with their start and end apart: 4 -> 16, of which waited for: 4 -> 6; matrix products, arithmetic and copies ran while one was open for 2% -> 0% of each run, Pallas kernels for 0% -> 13%
where the time goes in v1:
time: 57.1 us; the launch traced here: 56.8 us
  starting transfers between devices  27.3 us (48%)
  waiting for transfers between devices  13.6 us (24%)
  Pallas kernels  10.7 us (19%)
  local copies, waits for them, and re-layouts  4.41 us (8%)
  between operations  0.78 us (1%)
    ppermute x3, starting transfers between devices, outer(): return lax.ppermute(x, 'sector', [(0, 1), (1, 0), (2, 3), (3, 2)])  14.7 us
    ppermute x3, waiting for transfers between devices, outer(): return lax.ppermute(x, 'sector', [(0, 1), (1, 0), (2, 3), (3, 2)])  5.31 us
    ppermute x4, starting transfers between devices, across(): return lax.ppermute(x, 'mpo', [(0, 2), (1, 3), (2, 0), (3, 1)])  5.27 us
    pallas_call x2, Pallas kernels, line_device(): call(functools.partial(second_body, slots, ways), [shape(n, rows, cols),...  5.22 us
    ppermute x4, waiting for transfers between devices, across(): return lax.ppermute(x, 'mpo', [(0, 2), (1, 3), (2, 0), (3, 1)])  4.88 us
    unnamed x15, local copies, waits for them, and re-layouts  3.9 us
    ppermute x1, starting transfers between devices, line_device(): cross = lax.ppermute(mine, 'sector', [(0, 3), (3, 0), (1, 2), (2, 1)])  2.53 us
    pallas_call x2, Pallas kernels, line_device(): call(functools.partial(first_body, slots, ways), [shape(n, rows, cols)],...  2.43 us
  transfers between devices with their start and end apart: 16, of which 6 were waited for; matrix products, arithmetic and copies ran while one was open for 0% of the time, Pallas kernels for 13%

profile of v1, /device:TPU:0, one launch (start us, length us, event | category | flops | bytes accessed | tf_op | source)
XLA Modules:
  0.0 56.8 jit_solution(8032976086979865478)
XLA Ops:
  0.6 1.6 %collective-permute-start.1 = (f32[4,128,128]{2,1,0:T(8,128)}, f32[4,128,128]{2,1,0:T(8,128)S(1)}, u32[]{:S(2)}, u32[]{:S(2)}) collective-permute-start(f32[4,128,128]{2,1,0:T(8,128)} %refs_0_.3), channel_id=1, source_target_pairs={{4,8},{8,4},{0,0},{12,12},{5,9},{9,5},{1,1},{13,13},{6,10},{10,6},... | collective-permute-start | bytes 786440 | tf_op jit(solution)/shard_map/ppermute | solution.py:179
  2.2 5.0 %collective-permute-start = (f32[4,128,128]{2,1,0:T(8,128)}, f32[4,128,128]{2,1,0:T(8,128)S(1)}, u32[]{:S(2)}, u32[]{:S(2)}) collective-permute-start(f32[4,128,128]{2,1,0:T(8,128)} %refs_0_.3), channel_id=1, source_target_pairs={{0,4},{4,0},{8,12},{12,8},{1,5},{5,1},{9,13},{13,9},{2,6},{6,2},{1... | collective-permute-start | bytes 786440 | tf_op jit(solution)/shard_map/ppermute | solution.py:176
  7.2 0.0 collective-permute-done.1.refs_2_
  7.2 6.6 %collective-permute-start.2 = (f32[4,128,128]{2,1,0:T(8,128)S(1)}, f32[4,128,128]{2,1,0:T(8,128)S(1)}, u32[]{:S(2)}, u32[]{:S(2)}) collective-permute-start(f32[4,128,128]{2,1,0:T(8,128)S(1)} %collective-permute-done.1.refs_2_), channel_id=1, source_target_pairs={{0,4},{4,0},{8,12},{12,8},{1,5},{5,1},{9,13},{13,9},{2,6},{6,2},{1... | collective-permute-start | bytes 786440 | tf_op jit(solution)/shard_map/ppermute | solution.py:176
  13.8 0.0 collective-permute-done.refs_1_
  13.8 0.7 %collective-permute-start.5 = (f32[4,128,128]{2,1,0:T(8,128)S(1)}, f32[4,128,128]{2,1,0:T(8,128)S(1)}, u32[]{:S(2)}, u32[]{:S(2)}) collective-permute-start(f32[4,128,128]{2,1,0:T(8,128)S(1)} %collective-permute-done.refs_1_), channel_id=1, source_target_pairs={{4,8},{8,4},{0,0},{12,12},{5,9},{9,5},{1,1},{13,13},{6,10},{10,6},... | collective-permute-start | bytes 786440 | tf_op jit(solution)/shard_map/ppermute | solution.py:179
  14.5 0.0 copy-start
  14.5 0.9 %copy-done = f32[4,128,128]{2,1,0:T(8,128)S(1)} copy-done((f32[4,128,128]{2,1,0:T(8,128)S(1)}, f32[4,128,128]{2,1,0:T(8,128)}, u32[]{:S(2)}) %copy-start) | copy-done | bytes 262168
  15.4 0.0 copy-start.3
  15.4 0.9 %copy-done.3 = f32[128,512]{1,0:T(8,128)S(1)} copy-done((f32[128,512]{1,0:T(8,128)S(1)}, f32[128,512]{1,0:T(8,128)}, u32[]{:S(2)}) %copy-start.3) | copy-done | bytes 262168
  16.4 0.7 %copy-done.4 = s32[4,4]{1,0:T(4,128)S(1)} copy-done((s32[4,4]{1,0:T(4,128)S(1)}, s32[4,4]{1,0:T(4,128)}, u32[]{:S(2)}) %copy-start.4) | copy-done | bytes 88
  17.1 0.7 %copy-done.5 = s32[4]{0:T(128)S(1)} copy-done((s32[4]{0:T(128)S(1)}, s32[4]{0:T(128)}, u32[]{:S(2)}) %copy-start.5) | copy-done | bytes 40
  17.7 0.7 %copy-done.6 = s32[4]{0:T(128)S(1)} copy-done((s32[4]{0:T(128)S(1)}, s32[4]{0:T(128)}, u32[]{:S(2)}) %copy-start.6) | copy-done | bytes 40
  18.4 1.6 %shard_map.77 = (f32[128,512]{1,0:T(8,128)S(1)}, f32[4,128,512]{2,1,0:T(8,128)S(1)}) custom-call(s32[4]{0:T(128)S(1)} %copy-done.5, s32[4]{0:T(128)S(1)} %copy-done.6, s32[4,4]{1,0:T(4,128)S(1)} %copy-done.4, f32[128,512]{1,0:T(8,128)S(1)} %copy-done.3, f32[4,128,128]{2,1,0:T(8,128)S(1)} %copy-done), custom_call_target="tpu_custom_call" | custom-call | tf_op jit(solution)/shard_map/pallas_call | solution.py:192
  20.0 0.0 collective-permute-done.2.refs_3_
  20.0 0.0 copy-done.2
  20.0 1.8 %shard_map.78 = f32[3,128,128]{2,1,0:T(8,128)S(1)} custom-call(f32[4,128,512]{2,1,0:T(8,128)S(1)} %get-tuple-element.12.halfway, f32[4,128,128]{2,1,0:T(8,128)S(1)} %copy-done.2, f32[4,128,128]{2,1,0:T(8,128)S(1)} %collective-permute-done.refs_1_, f32[4,128,128]{2,1,0:T(8,128)S(1)} %collective-permute-done.1.refs_2_, ...), custom_call_target="tpu_custom_call" | custom-call | tf_op jit(solution)/shard_map/pallas_call | solution.py:206
  21.8 0.1 collective-permute-start.3
  21.9 0.0 collective-permute-done.5.refs_0_
  21.9 3.1 %collective-permute-start.6 = (f32[4,128,128]{2,1,0:T(8,128)S(1)}, f32[4,128,128]{2,1,0:T(8,128)S(1)}, u32[]{:S(2)}, u32[]{:S(2)}) collective-permute-start(f32[4,128,128]{2,1,0:T(8,128)S(1)} %collective-permute-done.5.refs_0_), channel_id=1, source_target_pairs={{0,4},{4,0},{8,12},{12,8},{1,5},{5,1},{9,13},{13,9},{2,6},{6,2},{1... | collective-permute-start | bytes 786440 | tf_op jit(solution)/shard_map/ppermute | solution.py:176
  25.0 0.0 collective-permute-done.3
  25.0 1.6 %collective-permute-start.4 = (f32[3,128,128]{2,1,0:T(8,128)S(1)}, f32[3,128,128]{2,1,0:T(8,128)S(1)}, u32[]{:S(2)}, u32[]{:S(2)}) collective-permute-start(f32[3,128,128]{2,1,0:T(8,128)S(1)} %add.12.own), channel_id=1, source_target_pairs={{0,2},{1,3},{2,0},{3,1},{4,6},{5,7},{6,4},{7,5},{8,10},{9,11},{10,... | collective-permute-start | bytes 589832 | tf_op jit(solution)/shard_map/ppermute | solution.py:185
  26.6 5.3 %collective-permute-done.6.refs_1_ = f32[4,128,128]{2,1,0:T(8,128)S(1)} collective-permute-done((f32[4,128,128]{2,1,0:T(8,128)S(1)}, f32[4,128,128]{2,1,0:T(8,128)S(1)}, u32[]{:S(2)}, u32[]{:S(2)}) %collective-permute-start.6) | collective-permute-done | bytes 262176 | tf_op jit(solution)/shard_map/ppermute | solution.py:176
  31.9 0.7 %shard_map.80 = f32[1,128,128]{2,1,0:T(8,128)S(1)} custom-call(f32[4,128,512]{2,1,0:T(8,128)S(1)} %get-tuple-element.12.halfway, f32[4,128,128]{2,1,0:T(8,128)S(1)} %collective-permute-done.5.refs_0_, f32[4,128,128]{2,1,0:T(8,128)S(1)} %collective-permute-done.6.refs_1_), custom_call_target="tpu_custom_call" | custom-call | tf_op jit(solution)/shard_map/pallas_call | solution.py:206
  32.6 0.1 collective-permute-start.7
  32.7 1.2 %collective-permute-done.7 = f32[1,128,128]{2,1,0:T(8,128)S(1)} collective-permute-done((f32[1,128,128]{2,1,0:T(8,128)S(1)}, f32[1,128,128]{2,1,0:T(8,128)S(1)}, u32[]{:S(2)}, u32[]{:S(2)}) %collective-permute-start.7) | collective-permute-done | bytes 65568 | tf_op jit(solution)/shard_map/ppermute | solution.py:182
  33.9 1.6 %collective-permute-start.8 = (f32[1,128,128]{2,1,0:T(8,128)S(1)}, f32[1,128,128]{2,1,0:T(8,128)S(1)}, u32[]{:S(2)}, u32[]{:S(2)}) collective-permute-start(f32[1,128,128]{2,1,0:T(8,128)S(1)} %add.13.own), channel_id=1, source_target_pairs={{0,2},{1,3},{2,0},{3,1},{4,6},{5,7},{6,4},{7,5},{8,10},{9,11},{10,... | collective-permute-start | bytes 196616 | tf_op jit(solution)/shard_map/ppermute | solution.py:185
  35.5 0.0 collective-permute-done.4.other
  35.5 0.0 copy-done.1
  35.5 3.3 %shard_map.79 = (f32[3,128,128]{2,1,0:T(8,128)S(1)}, f32[3,128,128]{2,1,0:T(8,128)S(1)}, f32[8,128]{1,0:T(8,128)S(1)}) custom-call(s32[4]{0:T(128)S(1)} %copy-done.5, s32[4]{0:T(128)S(1)} %copy-done.6, s32[4,4]{1,0:T(4,128)S(1)} %copy-done.4, f32[3,128,128]{2,1,0:T(8,128)S(1)} %add.12.own, f32[3,128,128]{2,1,0:T(8,128)S(1)} %collective-permute-done.4.other, ...), custom_call_target="tpu_custom_call" | custom-call | tf_op jit(solution)/shard_map/pallas_call | solution.py:210
  38.8 0.0 collective-permute-done.8.other
  38.8 1.9 %shard_map.81 = (f32[1,128,128]{2,1,0:T(8,128)S(1)}, f32[1,128,128]{2,1,0:T(8,128)S(1)}, f32[8,128]{1,0:T(8,128)S(1)}) custom-call(s32[4]{0:T(128)S(1)} %copy-done.5, s32[4]{0:T(128)S(1)} %copy-done.6, s32[4,4]{1,0:T(4,128)S(1)} %copy-done.4, f32[1,128,128]{2,1,0:T(8,128)S(1)} %add.13.own, f32[1,128,128]{2,1,0:T(8,128)S(1)} %collective-permute-done.8.other, ...), custom_call_target="tpu_custom_call" | custom-call | tf_op jit(solution)/shard_map/pallas_call | solution.py:210
  40.7 2.5 %collective-permute-start.11 = (f32[16,128]{1,0:T(8,128)S(1)}, f32[16,128]{1,0:T(8,128)S(1)}, u32[]{:S(2)}, u32[]{:S(2)}) collective-permute-start(f32[16,128]{1,0:T(8,128)S(1)} %constant_dynamic-update-slice_fusion), channel_id=1, source_target_pairs={{0,12},{12,0},{4,8},{8,4},{1,13},{13,1},{5,9},{9,5},{2,14},{14,2},... | collective-permute-start | bytes 24584 | tf_op jit(solution)/shard_map/ppermute | solution.py:224
  43.3 0.7 %collective-permute-start.10 = (f32[16,128]{1,0:T(8,128)S(1)}, f32[16,128]{1,0:T(8,128)S(1)}, u32[]{:S(2)}, u32[]{:S(2)}) collective-permute-start(f32[16,128]{1,0:T(8,128)S(1)} %constant_dynamic-update-slice_fusion), channel_id=1, source_target_pairs={{0,8},{8,0},{4,12},{12,4},{1,9},{9,1},{5,13},{13,5},{2,10},{10,2},... | collective-permute-start | bytes 24584 | tf_op jit(solution)/shard_map/ppermute | solution.py:223
  44.0 1.2 %collective-permute-start.9 = (f32[16,128]{1,0:T(8,128)S(1)}, f32[16,128]{1,0:T(8,128)S(1)}, u32[]{:S(2)}, u32[]{:S(2)}) collective-permute-start(f32[16,128]{1,0:T(8,128)S(1)} %constant_dynamic-update-slice_fusion), channel_id=1, source_target_pairs={{0,4},{4,0},{8,12},{12,8},{1,5},{5,1},{9,13},{13,9},{2,6},{6,2},{1... | collective-permute-start | bytes 24584 | tf_op jit(solution)/shard_map/ppermute | solution.py:222
  45.2 0.0 collective-permute-start.14
  45.2 0.5 collective-permute-start.12
  45.7 0.5 collective-permute-done.11
  46.3 1.6 %collective-permute-done.10 = f32[16,128]{1,0:T(8,128)S(1)} collective-permute-done((f32[16,128]{1,0:T(8,128)S(1)}, f32[16,128]{1,0:T(8,128)S(1)}, u32[]{:S(2)}, u32[]{:S(2)}) %collective-permute-start.10) | collective-permute-done | bytes 8224 | tf_op jit(solution)/shard_map/ppermute | solution.py:223
  47.8 0.0 collective-permute-done.14
  47.8 1.0 %collective-permute-start.15 = (f32[1,128,128]{2,1,0:T(8,128)S(1)}, f32[1,128,128]{2,1,0:T(8,128)S(1)}, u32[]{:S(2)}, u32[]{:S(2)}) collective-permute-start(f32[1,128,128]{2,1,0:T(8,128)S(1)} %add.15.refs_11_), channel_id=1, source_target_pairs={{0,2},{1,3},{2,0},{3,1},{4,6},{5,7},{6,4},{7,5},{8,10},{9,11},{10,... | collective-permute-start | bytes 196616 | tf_op jit(solution)/shard_map/ppermute | solution.py:185
  48.8 0.0 collective-permute-done.12
  48.8 1.2 %collective-permute-start.13 = (f32[3,128,128]{2,1,0:T(8,128)S(1)}, f32[3,128,128]{2,1,0:T(8,128)S(1)}, u32[]{:S(2)}, u32[]{:S(2)}) collective-permute-start(f32[3,128,128]{2,1,0:T(8,128)S(1)} %add.14.refs_8_), channel_id=1, source_target_pairs={{0,2},{1,3},{2,0},{3,1},{4,6},{5,7},{6,4},{7,5},{8,10},{9,11},{10,... | collective-permute-start | bytes 589832 | tf_op jit(solution)/shard_map/ppermute | solution.py:185
  50.0 0.0 collective-permute-done.9
  50.0 2.8 %collective-permute-done.15.refs_12_ = f32[1,128,128]{2,1,0:T(8,128)S(1)} collective-permute-done((f32[1,128,128]{2,1,0:T(8,128)S(1)}, f32[1,128,128]{2,1,0:T(8,128)S(1)}, u32[]{:S(2)}, u32[]{:S(2)}) %collective-permute-start.15) | collective-permute-done | bytes 65568 | tf_op jit(solution)/shard_map/ppermute | solution.py:185
  52.8 2.1 %collective-permute-done.13.refs_9_ = f32[3,128,128]{2,1,0:T(8,128)S(1)} collective-permute-done((f32[3,128,128]{2,1,0:T(8,128)S(1)}, f32[3,128,128]{2,1,0:T(8,128)S(1)}, u32[]{:S(2)}, u32[]{:S(2)}) %collective-permute-start.13) | collective-permute-done | bytes 196640 | tf_op jit(solution)/shard_map/ppermute | solution.py:185
  54.9 1.4 %shard_map.82 = (f32[128,512]{1,0:T(8,128)}, f32[8,128]{1,0:T(8,128)S(1)}) custom-call(s32[4]{0:T(128)S(1)} %copy-done.5, s32[4]{0:T(128)S(1)} %copy-done.6, s32[4,4]{1,0:T(4,128)S(1)} %copy-done.4, f32[8,128]{1,0:T(8,128)S(1)} %get-tuple-element.14.refs_0_, f32[8,128]{1,0:T(8,128)S(1)} %get-tuple-element.15.refs_1_, ...), custom_call_target="tpu_custom_call" | custom-call | tf_op jit(solution)/shard_map/pallas_call | solution.py:226
  56.3 0.5 slice.27
  (14 shorter events, 0.1 us)
Async XLA Ops:
  0.6 6.6 %collective-permute-start.1 = (f32[4,128,128]{2,1,0:T(8,128)}, f32[4,128,128]{2,1,0:T(8,128)S(1)}, u32[]{:S(2)}, u32[]{:S(2)}) collective-permute-start(f32[4,128,128]{2,1,0:T(8,128)} %refs_0_.3), channel_id=1, source_target_pairs={{4,8},{8,4},{0,0},{12,12},{5,9},{9,5},{1,1},{13,13},{6,10},{10,6},... | collective-permute-start | bytes 786440 | tf_op jit(solution)/shard_map/ppermute | solution.py:179
  2.2 11.6 %collective-permute-start = (f32[4,128,128]{2,1,0:T(8,128)}, f32[4,128,128]{2,1,0:T(8,128)S(1)}, u32[]{:S(2)}, u32[]{:S(2)}) collective-permute-start(f32[4,128,128]{2,1,0:T(8,128)} %refs_0_.3), channel_id=1, source_target_pairs={{0,4},{4,0},{8,12},{12,8},{1,5},{5,1},{9,13},{13,9},{2,6},{6,2},{1... | collective-permute-start | bytes 786440 | tf_op jit(solution)/shard_map/ppermute | solution.py:176
  7.2 12.8 %collective-permute-start.2 = (f32[4,128,128]{2,1,0:T(8,128)S(1)}, f32[4,128,128]{2,1,0:T(8,128)S(1)}, u32[]{:S(2)}, u32[]{:S(2)}) collective-permute-start(f32[4,128,128]{2,1,0:T(8,128)S(1)} %collective-permute-done.1.refs_2_), channel_id=1, source_target_pairs={{0,4},{4,0},{8,12},{12,8},{1,5},{5,1},{9,13},{13,9},{2,6},{6,2},{1... | collective-permute-start | bytes 786440 | tf_op jit(solution)/shard_map/ppermute | solution.py:176
  13.8 8.1 %collective-permute-start.5 = (f32[4,128,128]{2,1,0:T(8,128)S(1)}, f32[4,128,128]{2,1,0:T(8,128)S(1)}, u32[]{:S(2)}, u32[]{:S(2)}) collective-permute-start(f32[4,128,128]{2,1,0:T(8,128)S(1)} %collective-permute-done.refs_1_), channel_id=1, source_target_pairs={{4,8},{8,4},{0,0},{12,12},{5,9},{9,5},{1,1},{13,13},{6,10},{10,6},... | collective-permute-start | bytes 786440 | tf_op jit(solution)/shard_map/ppermute | solution.py:179
  14.5 1.0 %copy-start = (f32[4,128,128]{2,1,0:T(8,128)S(1)}, f32[4,128,128]{2,1,0:T(8,128)}, u32[]{:S(2)}) copy-start(f32[4,128,128]{2,1,0:T(8,128)} %left.5) | copy-start | bytes 786436
  15.4 0.9 %copy-start.3 = (f32[128,512]{1,0:T(8,128)S(1)}, f32[128,512]{1,0:T(8,128)}, u32[]{:S(2)}) copy-start(f32[128,512]{1,0:T(8,128)} %wave.1) | copy-start | bytes 786436
  16.4 0.7 %copy-start.4 = (s32[4,4]{1,0:T(4,128)S(1)}, s32[4,4]{1,0:T(4,128)}, u32[]{:S(2)}) copy-start(s32[4,4]{1,0:T(4,128)} %pairs.7) | copy-start | bytes 196
  17.1 0.7 %copy-start.5 = (s32[4]{0:T(128)S(1)}, s32[4]{0:T(128)}, u32[]{:S(2)}) copy-start(s32[4]{0:T(128)} %left_sizes.7) | copy-start | bytes 52
  17.7 0.7 %copy-start.6 = (s32[4]{0:T(128)S(1)}, s32[4]{0:T(128)}, u32[]{:S(2)}) copy-start(s32[4]{0:T(128)} %right_sizes.7) | copy-start | bytes 52
  18.4 1.6 %copy-start.2 = (f32[4,128,128]{2,1,0:T(8,128)S(1)}, f32[4,128,128]{2,1,0:T(8,128)}, u32[]{:S(2)}) copy-start(f32[4,128,128]{2,1,0:T(8,128)} %refs_0_.3) | copy-start | bytes 786436
  21.8 3.2 %collective-permute-start.3 = (f32[3,128,128]{2,1,0:T(8,128)S(1)}, f32[3,128,128]{2,1,0:T(8,128)S(1)}, u32[]{:S(2)}, u32[]{:S(2)}) collective-permute-start(f32[3,128,128]{2,1,0:T(8,128)S(1)} %shard_map.78), channel_id=1, source_target_pairs={{0,1},{1,0},{2,3},{3,2},{4,5},{5,4},{6,7},{7,6},{8,9},{9,8},{10,11... | collective-permute-start | bytes 589832 | tf_op jit(solution)/shard_map/ppermute | solution.py:182
  21.9 10.0 %collective-permute-start.6 = (f32[4,128,128]{2,1,0:T(8,128)S(1)}, f32[4,128,128]{2,1,0:T(8,128)S(1)}, u32[]{:S(2)}, u32[]{:S(2)}) collective-permute-start(f32[4,128,128]{2,1,0:T(8,128)S(1)} %collective-permute-done.5.refs_0_), channel_id=1, source_target_pairs={{0,4},{4,0},{8,12},{12,8},{1,5},{5,1},{9,13},{13,9},{2,6},{6,2},{1... | collective-permute-start | bytes 786440 | tf_op jit(solution)/shard_map/ppermute | solution.py:176
  25.0 10.4 %collective-permute-start.4 = (f32[3,128,128]{2,1,0:T(8,128)S(1)}, f32[3,128,128]{2,1,0:T(8,128)S(1)}, u32[]{:S(2)}, u32[]{:S(2)}) collective-permute-start(f32[3,128,128]{2,1,0:T(8,128)S(1)} %add.12.own), channel_id=1, source_target_pairs={{0,2},{1,3},{2,0},{3,1},{4,6},{5,7},{6,4},{7,5},{8,10},{9,11},{10,... | collective-permute-start | bytes 589832 | tf_op jit(solution)/shard_map/ppermute | solution.py:185
  31.9 3.6 %copy-start.1 = (f32[4,128,128]{2,1,0:T(8,128)S(1)}, f32[4,128,128]{2,1,0:T(8,128)}, u32[]{:S(2)}) copy-start(f32[4,128,128]{2,1,0:T(8,128)} %left.5) | copy-start | bytes 786436
  32.6 1.3 %collective-permute-start.7 = (f32[1,128,128]{2,1,0:T(8,128)S(1)}, f32[1,128,128]{2,1,0:T(8,128)S(1)}, u32[]{:S(2)}, u32[]{:S(2)}) collective-permute-start(f32[1,128,128]{2,1,0:T(8,128)S(1)} %shard_map.80), channel_id=1, source_target_pairs={{0,1},{1,0},{2,3},{3,2},{4,5},{5,4},{6,7},{7,6},{8,9},{9,8},{10,11... | collective-permute-start | bytes 196616 | tf_op jit(solution)/shard_map/ppermute | solution.py:182
  33.9 4.9 %collective-permute-start.8 = (f32[1,128,128]{2,1,0:T(8,128)S(1)}, f32[1,128,128]{2,1,0:T(8,128)S(1)}, u32[]{:S(2)}, u32[]{:S(2)}) collective-permute-start(f32[1,128,128]{2,1,0:T(8,128)S(1)} %add.13.own), channel_id=1, source_target_pairs={{0,2},{1,3},{2,0},{3,1},{4,6},{5,7},{6,4},{7,5},{8,10},{9,11},{10,... | collective-permute-start | bytes 196616 | tf_op jit(solution)/shard_map/ppermute | solution.py:185
  40.7 5.5 %collective-permute-start.11 = (f32[16,128]{1,0:T(8,128)S(1)}, f32[16,128]{1,0:T(8,128)S(1)}, u32[]{:S(2)}, u32[]{:S(2)}) collective-permute-start(f32[16,128]{1,0:T(8,128)S(1)} %constant_dynamic-update-slice_fusion), channel_id=1, source_target_pairs={{0,12},{12,0},{4,8},{8,4},{1,13},{13,1},{5,9},{9,5},{2,14},{14,2},... | collective-permute-start | bytes 24584 | tf_op jit(solution)/shard_map/ppermute | solution.py:224
  43.3 4.5 %collective-permute-start.10 = (f32[16,128]{1,0:T(8,128)S(1)}, f32[16,128]{1,0:T(8,128)S(1)}, u32[]{:S(2)}, u32[]{:S(2)}) collective-permute-start(f32[16,128]{1,0:T(8,128)S(1)} %constant_dynamic-update-slice_fusion), channel_id=1, source_target_pairs={{0,8},{8,0},{4,12},{12,4},{1,9},{9,1},{5,13},{13,5},{2,10},{10,2},... | collective-permute-start | bytes 24584 | tf_op jit(solution)/shard_map/ppermute | solution.py:223
  44.0 6.0 %collective-permute-start.9 = (f32[16,128]{1,0:T(8,128)S(1)}, f32[16,128]{1,0:T(8,128)S(1)}, u32[]{:S(2)}, u32[]{:S(2)}) collective-permute-start(f32[16,128]{1,0:T(8,128)S(1)} %constant_dynamic-update-slice_fusion), channel_id=1, source_target_pairs={{0,4},{4,0},{8,12},{12,8},{1,5},{5,1},{9,13},{13,9},{2,6},{6,2},{1... | collective-permute-start | bytes 24584 | tf_op jit(solution)/shard_map/ppermute | solution.py:222
  45.2 2.6 %collective-permute-start.14 = (f32[1,128,128]{2,1,0:T(8,128)S(1)}, f32[1,128,128]{2,1,0:T(8,128)S(1)}, u32[]{:S(2)}, u32[]{:S(2)}) collective-permute-start(f32[1,128,128]{2,1,0:T(8,128)S(1)} %get-tuple-element.18), channel_id=1, source_target_pairs={{0,1},{1,0},{2,3},{3,2},{4,5},{5,4},{6,7},{7,6},{8,9},{9,8},{10,11... | collective-permute-start | bytes 196616 | tf_op jit(solution)/shard_map/ppermute | solution.py:182
  45.2 3.6 %collective-permute-start.12 = (f32[3,128,128]{2,1,0:T(8,128)S(1)}, f32[3,128,128]{2,1,0:T(8,128)S(1)}, u32[]{:S(2)}, u32[]{:S(2)}) collective-permute-start(f32[3,128,128]{2,1,0:T(8,128)S(1)} %get-tuple-element.16), channel_id=1, source_target_pairs={{0,1},{1,0},{2,3},{3,2},{4,5},{5,4},{6,7},{7,6},{8,9},{9,8},{10,11... | collective-permute-start | bytes 589832 | tf_op jit(solution)/shard_map/ppermute | solution.py:182
  47.8 5.0 %collective-permute-start.15 = (f32[1,128,128]{2,1,0:T(8,128)S(1)}, f32[1,128,128]{2,1,0:T(8,128)S(1)}, u32[]{:S(2)}, u32[]{:S(2)}) collective-permute-start(f32[1,128,128]{2,1,0:T(8,128)S(1)} %add.15.refs_11_), channel_id=1, source_target_pairs={{0,2},{1,3},{2,0},{3,1},{4,6},{5,7},{6,4},{7,5},{8,10},{9,11},{10,... | collective-permute-start | bytes 196616 | tf_op jit(solution)/shard_map/ppermute | solution.py:185
  48.8 6.1 %collective-permute-start.13 = (f32[3,128,128]{2,1,0:T(8,128)S(1)}, f32[3,128,128]{2,1,0:T(8,128)S(1)}, u32[]{:S(2)}, u32[]{:S(2)}) collective-permute-start(f32[3,128,128]{2,1,0:T(8,128)S(1)} %add.14.refs_8_), channel_id=1, source_target_pairs={{0,2},{1,3},{2,0},{3,1},{4,6},{5,7},{6,4},{7,5},{8,10},{9,11},{10,... | collective-permute-start | bytes 589832 | tf_op jit(solution)/shard_map/ppermute | solution.py:185

commit v2 on v1

v2 whole, which is shorter than its diff:
```python
import functools

import jax
import jax.numpy as jnp
from jax import lax
from jax.experimental import pallas as pl
from jax.experimental.pallas import tpu as pltpu
from jax.sharding import PartitionSpec as P

EXACT = lax.Precision.HIGHEST
TINY = 1e-06
VMEM = pl.BlockSpec(memory_space=pltpu.VMEM)
SMEM = pl.BlockSpec(memory_space=pltpu.SMEM)
F32 = jnp.float32
BF16 = jnp.bfloat16


def split(x):
    high = x.astype(BF16)
    return high, (x - high.astype(F32)).astype(BF16)


def left_terms(x, axis):
    high, low = split(x)
    return jnp.concatenate([high, high, low], axis=axis)


def right_terms(x, axis):
    high, low = split(x)
    return jnp.concatenate([high, low, high], axis=axis)


def dot_nn(a, b):
    return lax.dot_general(a, b, (((1,), (0,)), ((), ())), preferred_element_type=F32)


def dot_nt(a, b):
    return lax.dot_general(a, b, (((1,), (1,)), ((), ())), preferred_element_type=F32)


def block_valid(left_sizes, right_sizes, pairs, a, b, rows, cols):
    row = lax.broadcasted_iota(jnp.int32, (rows, cols), 0) < left_sizes[a]
    col = lax.broadcasted_iota(jnp.int32, (rows, cols), 1) < right_sizes[b]
    return (row & col).astype(F32) * pairs[a, b].astype(F32)


def call(body, outs, n_small, n_big, **kw):
    return pl.pallas_call(
        body,
        out_shape=outs,
        in_specs=[SMEM] * n_small + [VMEM] * n_big,
        out_specs=[VMEM] * len(outs),
        compiler_params=pltpu.CompilerParams(vmem_limit_bytes=32 * 1024 * 1024),
        **kw,
    )


def slot_column(slot, sector):
    return sector ^ (0, 1, 3, 2)[slot]


def columns(b, width):
    return pl.ds(pl.multiple_of(b * width, width), width)


def channel_row(blocks):
    return jnp.concatenate([blocks[w] for w in range(blocks.shape[0])], axis=1)


def half_body(left_sizes, right_sizes, pairs, wave, left, vector, halfway, factors):
    sector = lax.axis_index("sector")
    channels, rows, _ = left.shape
    sectors, _, inner = halfway.shape
    cols = inner // channels
    factors[...] = left_terms(left[...].reshape(channels * rows, rows), 1)
    for b in range(sectors):
        at = slice(b * cols, (b + 1) * cols)
        here = wave[:, at] * block_valid(left_sizes, right_sizes, pairs, sector, b, rows, cols)
        vector[:, at] = here
        part = dot_nn(factors[...], right_terms(here, 0))
        for w in range(channels):
            halfway[b, :, w * cols : (w + 1) * cols] = part[w * rows : (w + 1) * rows]


def first_body(slots, halfway, *refs):
    out = refs[-1]
    sector = lax.axis_index("sector")
    for k, slot in enumerate(slots):
        out[k] = dot_nt(
            left_terms(halfway[slot_column(slot, sector)], 1),
            right_terms(channel_row(refs[k]), 1),
        )


def second_body(slots, left_sizes, right_sizes, pairs, own, other, vector, factors, *refs):
    n = len(slots)
    image, partial, sums = refs[-3:]
    sector = lax.axis_index("sector")
    _, rows, cols = own.shape
    channels = factors.shape[0] // rows
    cross = jnp.zeros((1, cols), F32)
    square = jnp.zeros((1, cols), F32)
    vectors = []
    for k, slot in enumerate(slots):
        b = slot_column(slot, sector)
        valid = block_valid(left_sizes, right_sizes, pairs, sector, b, rows, cols)
        here = (own[k] + other[k]) * valid
        image[k] = here
        half = dot_nn(factors[...], right_terms(here, 0))
        half = channel_row(half.reshape(channels, rows, cols))
        partial[k] = dot_nt(left_terms(half, 1), right_terms(channel_row(refs[k]), 1))
        v = vector[:, columns(b, cols)]
        vectors.append(v)
        cross += jnp.sum(v * here, axis=0, keepdims=True)
        square += jnp.sum(v * v, axis=0, keepdims=True)
    ratio = jnp.where(square > 0, cross / jnp.where(square > 0, square, 1.0), 0.0)
    rest = jnp.zeros((1, cols), F32)
    for k in range(n):
        away = image[k] - ratio * vectors[k]
        rest += jnp.sum(away * away, axis=0, keepdims=True)
    if len(refs) > n + 3:
        sums[...] = refs[n][...]
        at = 3
    else:
        sums[...] = jnp.zeros_like(sums)
        at = 0
    sums[at : at + 1, :] = cross
    sums[at + 1 : at + 2, :] = square
    sums[at + 2 : at + 3, :] = rest


def last_body(groups, cells, left_sizes, right_sizes, pairs, *refs):
    mine, near, far, cross = refs[:4]
    product, ritz = refs[-2:]
    sector = lax.axis_index("sector")

    def everyone(read):
        lanes = (read(mine) + read(near)) + (read(far) + read(cross))
        return jnp.sum(lanes)

    def both(row):
        return lambda s: s[row : row + 1, :] + s[row + 3 : row + 4, :]

    value = everyone(both(0)) / (everyone(both(1)) + TINY)

    def rest_of(s):
        total = s[2:3, :] + s[5:6, :]
        for row in (0, 3):
            c = s[row + 1 : row + 2, :]
            ratio = jnp.where(c > 0, s[row : row + 1, :] / jnp.where(c > 0, c, 1.0), 0.0)
            total += (ratio - value) * (ratio - value) * c
        return total

    scale = 1.0 / jnp.sqrt(everyone(rest_of) / cells + TINY)
    ritz[0] = value
    at = 4
    for slots in groups:
        own, other, image = refs[at : at + 3]
        at += 3
        for k, slot in enumerate(slots):
            b = slot_column(slot, sector)
            _, rows, cols = own.shape
            valid = block_valid(left_sizes, right_sizes, pairs, sector, b, rows, cols)
            product[:, columns(b, cols)] = (
                (own[k] + other[k]) * valid - value * image[k]
            ) * scale


def line_device(wave, left, right, left_sizes, right_sizes, pairs):
    channels, rows, _ = left.shape
    cols = right.shape[2]
    sectors = 4
    cells = float(sectors * rows * sectors * cols)
    small = (left_sizes, right_sizes, pairs)

    def near(x):
        return lax.ppermute(x, "sector", [(0, 1), (1, 0), (2, 3), (3, 2)])

    def far(x):
        return lax.ppermute(x, "sector", [(0, 2), (2, 0), (1, 3), (3, 1)])

    def mirror(x):
        return lax.ppermute(x, "sector", [(0, 3), (3, 0), (1, 2), (2, 1)])

    def core(x):
        return lax.ppermute(x, "mpo", [(0, 1), (1, 0), (2, 3), (3, 2)])

    def across(x):
        return lax.ppermute(x, "mpo", [(0, 2), (1, 3), (2, 0), (3, 1)])

    def shape(*dims, of=F32):
        return jax.ShapeDtypeStruct(dims, of)

    right_near = near(right)
    right_mirror = mirror(right)
    right_far = near(right_mirror)
    vector, halfway, factors = call(
        half_body,
        [
            shape(rows, sectors * cols),
            shape(sectors, rows, channels * cols),
            shape(channels * rows, 3 * rows, of=BF16),
        ],
        3,
        2,
    )(*small, wave, left)

    groups = ((0, 1), (2, 3))
    rights = ((right, right_near), (right_mirror, right_far))
    parts = []
    sums = ()
    for slots, envs in zip(groups, rights):
        n = len(slots)
        (partial,) = call(
            functools.partial(first_body, slots), [shape(n, rows, cols)], 0, 1 + n
        )(halfway, *envs)
        both = partial + core(partial)
        image, partial, total = call(
            functools.partial(second_body, slots),
            [shape(n, rows, cols), shape(n, rows, cols), shape(8, cols)],
            3,
            4 + n + len(sums),
        )(*small, both, across(both), vector, factors, *envs, *sums)
        sums = (total,)
        both = partial + core(partial)
        parts += [both, across(both), image]

    (mine,) = sums
    product, ritz = pl.pallas_call(
        functools.partial(last_body, groups, cells),
        out_shape=[shape(rows, sectors * cols), shape(1)],
        in_specs=[SMEM] * 3 + [VMEM] * 10,
        out_specs=[VMEM, SMEM],
    )(*small, mine, near(mine), far(mine), mirror(mine), *parts)
    return product, ritz


def wide_device(wave, left, right, left_sizes, right_sizes, pairs):
    sector = lax.axis_index("sector")
    sectors = lax.axis_size("sector")
    channels, rows, _ = left.shape
    cols = right.shape[2]
    cells = float(sectors * rows * sectors * cols)
    own = lax.dynamic_index_in_dim(pairs, sector, 0, keepdims=False).astype(F32)
    size = lax.dynamic_index_in_dim(left_sizes, sector, 0, keepdims=False)
    row = (jnp.arange(rows) < size).astype(F32)
    col = (jnp.arange(cols)[None, :] < right_sizes[:, None]).astype(F32) * own[:, None]
    valid = row[:, None] * col.reshape(1, -1)
    vector = wave * valid
    rights = lax.all_gather(right, "sector", axis=1)

    def image_of(v):
        half = jnp.einsum("wik,kbc->wibc", left, v.reshape(rows, sectors, cols), precision=EXACT)
        out = jnp.einsum("wibc,wbjc->ibj", half, rights, precision=EXACT)
        return lax.psum(out.reshape(rows, sectors * cols), "mpo") * valid

    first = image_of(vector)
    cross, square = lax.psum((jnp.sum(vector * first), jnp.sum(vector * vector)), "sector")
    value = cross / (square + TINY)
    residual = first - value * vector
    rest = lax.psum(jnp.sum(residual * residual), "sector")
    product = image_of(residual / jnp.sqrt(rest / cells + TINY))
    return product, jnp.reshape(value, (1,))


def solution(mesh):
    line = mesh.shape["sector"] == 4 and mesh.shape["mpo"] == 4
    return jax.shard_map(
        line_device if line else wide_device,
        mesh=mesh,
        in_specs=(
            P(("groups", "sector"), None),
            P("mpo", ("groups", "sector"), None),
            P("mpo", ("groups", "sector"), None),
            P("groups"),
            P("groups"),
            P("groups", None),
        ),
        out_specs=(P(("groups", "sector"), None), P("groups")),
        check_vma=False,
    )
```

time: 57.1 us -> 50.3 us (0.88)
  starting transfers between devices: 27.3 us -> 19.6 us
  Pallas kernels: 10.7 us -> 7.39 us
  waiting for transfers between devices: 13.6 us -> 16.2 us
  local copies, waits for them, and re-layouts: 4.41 us -> 5.87 us
    ppermute x8 -> x6, starting transfers between devices: 21.4 us -> 13.9 us  [the longest x2 6.46 us: mirror(): return lax.ppermute(x, 'sector', [(0, 3), (3, 0), (1, 2), (2, 1)])]
    ppermute x8 -> x6, waiting for transfers between devices: 7.43 us -> 11.9 us  [the longest x2 10.1 us: mirror(): return lax.ppermute(x, 'sector', [(0, 3), (3, 0), (1, 2), (2, 1)])]
    pallas_call x5, Pallas kernels: 9.05 us -> 6.22 us  [the longest x2 3.13 us: line_device(): call(functools.partial(second_body, slots), [shape(n, rows, cols), shape(...]
    unnamed x15 -> x38, local copies, waits for them, and re-layouts: 3.9 us -> 5.87 us
    ppermute x4, waiting for transfers between devices: 4.88 us -> 3.93 us  [across(): return lax.ppermute(x, 'mpo', [(0, 2), (1, 3), (2, 0), (3, 1)])]
    ppermute x4, waiting for transfers between devices: 1.25 us -> 0.39 us  [core(): return lax.ppermute(x, 'mpo', [(0, 1), (1, 0), (2, 3), (3, 2)])]
  transfers between devices with their start and end apart: 16 -> 14, of which waited for: 6 -> 6; matrix products, arithmetic and copies ran while one was open for 0% -> 0% of each run, Pallas kernels for 13% -> 10%
where the time goes in v2:
time: 50.3 us; the launch traced here: 50 us
  starting transfers between devices  19.6 us (39%)
  waiting for transfers between devices  16.2 us (32%)
  Pallas kernels  7.39 us (15%)
  local copies, waits for them, and re-layouts  5.87 us (12%)
  between operations  0.81 us (2%)
    ppermute x2, waiting for transfers between devices, mirror(): return lax.ppermute(x, 'sector', [(0, 3), (3, 0), (1, 2), (2, 1)])  10.1 us
    ppermute x2, starting transfers between devices, mirror(): return lax.ppermute(x, 'sector', [(0, 3), (3, 0), (1, 2), (2, 1)])  6.46 us
    unnamed x38, local copies, waits for them, and re-layouts  5.87 us
    ppermute x3, starting transfers between devices, near(): return lax.ppermute(x, 'sector', [(0, 1), (1, 0), (2, 3), (3, 2)])  5.66 us
    ppermute x4, starting transfers between devices, across(): return lax.ppermute(x, 'mpo', [(0, 2), (1, 3), (2, 0), (3, 1)])  4.95 us
    ppermute x4, waiting for transfers between devices, across(): return lax.ppermute(x, 'mpo', [(0, 2), (1, 3), (2, 0), (3, 1)])  3.93 us
    pallas_call x2, Pallas kernels, line_device(): call(functools.partial(second_body, slots), [shape(n, rows, cols), shape(...  3.13 us
    pallas_call x1, Pallas kernels, line_device(): pl.pallas_call(functools.partial(last_body, groups, cells), out_shape=[sh...  2.34 us
  transfers between devices with their start and end apart: 14, of which 6 were waited for; matrix products, arithmetic and copies ran while one was open for 0% of the time, Pallas kernels for 10%

profile of v2, /device:TPU:0, one launch (start us, length us, event | category | flops | bytes accessed | tf_op | source)
XLA Modules:
  0.0 50.0 jit_solution(17530862288921947245)
XLA Ops:
  0.6 0.0 copy-start
  0.6 5.1 %collective-permute-start = (f32[4,128,128]{2,1,0:T(8,128)}, f32[4,128,128]{2,1,0:T(8,128)S(1)}, u32[]{:S(2)}, u32[]{:S(2)}) collective-permute-start(f32[4,128,128]{2,1,0:T(8,128)} %refs_0_.3), channel_id=1, source_target_pairs={{0,12},{12,0},{4,8},{8,4},{1,13},{13,1},{5,9},{9,5},{2,14},{14,2},... | collective-permute-start | bytes 786440 | tf_op jit(solution)/shard_map/ppermute | solution.py:183
  5.8 0.0 collective-permute-start.4
  5.8 7.4 %collective-permute-done.refs_0_ = f32[4,128,128]{2,1,0:T(8,128)S(1)} collective-permute-done((f32[4,128,128]{2,1,0:T(8,128)}, f32[4,128,128]{2,1,0:T(8,128)S(1)}, u32[]{:S(2)}, u32[]{:S(2)}) %collective-permute-start) | collective-permute-done | bytes 262176 | tf_op jit(solution)/shard_map/ppermute | solution.py:183
  13.2 4.4 %collective-permute-start.1 = (f32[4,128,128]{2,1,0:T(8,128)S(1)}, f32[4,128,128]{2,1,0:T(8,128)S(1)}, u32[]{:S(2)}, u32[]{:S(2)}) collective-permute-start(f32[4,128,128]{2,1,0:T(8,128)S(1)} %collective-permute-done.refs_0_), channel_id=1, source_target_pairs={{0,4},{4,0},{8,12},{12,8},{1,5},{5,1},{9,13},{13,9},{2,6},{6,2},{1... | collective-permute-start | bytes 786440 | tf_op jit(solution)/shard_map/ppermute | solution.py:177
  17.6 0.9 %copy-done.1 = f32[128,512]{1,0:T(8,128)S(1)} copy-done((f32[128,512]{1,0:T(8,128)S(1)}, f32[128,512]{1,0:T(8,128)}, u32[]{:S(2)}) %copy-start.1) | copy-done | bytes 262168
  18.6 0.9 %copy-done.2 = f32[4,128,128]{2,1,0:T(8,128)S(1)} copy-done((f32[4,128,128]{2,1,0:T(8,128)S(1)}, f32[4,128,128]{2,1,0:T(8,128)}, u32[]{:S(2)}) %copy-start.2) | copy-done | bytes 262168
  19.5 0.7 %copy-done.5 = s32[4,4]{1,0:T(4,128)S(1)} copy-done((s32[4,4]{1,0:T(4,128)S(1)}, s32[4,4]{1,0:T(4,128)}, u32[]{:S(2)}) %copy-start.5) | copy-done | bytes 88
  20.2 0.7 %copy-done.7 = s32[4]{0:T(128)S(1)} copy-done((s32[4]{0:T(128)S(1)}, s32[4]{0:T(128)}, u32[]{:S(2)}) %copy-start.7) | copy-done | bytes 40
  20.8 0.7 %copy-done.9 = s32[4]{0:T(128)S(1)} copy-done((s32[4]{0:T(128)S(1)}, s32[4]{0:T(128)}, u32[]{:S(2)}) %copy-start.9) | copy-done | bytes 40
  21.5 1.2 %shard_map.77 = (f32[128,512]{1,0:T(8,128)S(1)}, f32[4,128,512]{2,1,0:T(8,128)S(1)}, bf16[512,384]{1,0:T(8,128)(2,1)S(1)}) custom-call(s32[4]{0:T(128)S(1)} %copy-done.7, s32[4]{0:T(128)S(1)} %copy-done.9, s32[4,4]{1,0:T(4,128)S(1)} %copy-done.5, f32[128,512]{1,0:T(8,128)S(1)} %copy-done.1, f32[4,128,128]{2,1,0:T(8,128)S(1)} %copy-done.2), custom_call_target="tpu_custom_call" | custom-call | tf_op jit(solution)/shard_map/pallas_call | solution.py:197
  22.7 0.0 collective-permute-done.4.refs_1_
  22.7 0.4 shard_map.79
  23.1 0.1 collective-permute-start.5
  23.1 0.5 collective-permute-done.1.refs_1_
  23.6 0.4 shard_map.78
  24.0 0.1 collective-permute-start.2
  24.1 0.4 collective-permute-done.5
  24.5 1.6 %collective-permute-start.6 = (f32[2,128,128]{2,1,0:T(8,128)S(1)}, f32[2,128,128]{2,1,0:T(8,128)S(1)}, u32[]{:S(2)}, u32[]{:S(2)}) collective-permute-start(f32[2,128,128]{2,1,0:T(8,128)S(1)} %add.13.own), channel_id=1, source_target_pairs={{0,2},{1,3},{2,0},{3,1},{4,6},{5,7},{6,4},{7,5},{8,10},{9,11},{10,... | collective-permute-start | bytes 393224 | tf_op jit(solution)/shard_map/ppermute | solution.py:189
  26.1 0.0 collective-permute-done.2
  26.1 0.0 copy-start.6
  26.1 0.9 %collective-permute-start.3 = (f32[2,128,128]{2,1,0:T(8,128)S(1)}, f32[2,128,128]{2,1,0:T(8,128)S(1)}, u32[]{:S(2)}, u32[]{:S(2)}) collective-permute-start(f32[2,128,128]{2,1,0:T(8,128)S(1)} %add.12.own), channel_id=1, source_target_pairs={{0,2},{1,3},{2,0},{3,1},{4,6},{5,7},{6,4},{7,5},{8,10},{9,11},{10,... | collective-permute-start | bytes 393224 | tf_op jit(solution)/shard_map/ppermute | solution.py:189
  27.0 3.9 %collective-permute-done.6.other = f32[2,128,128]{2,1,0:T(8,128)S(1)} collective-permute-done((f32[2,128,128]{2,1,0:T(8,128)S(1)}, f32[2,128,128]{2,1,0:T(8,128)S(1)}, u32[]{:S(2)}, u32[]{:S(2)}) %collective-permute-start.6) | collective-permute-done | bytes 131104 | tf_op jit(solution)/shard_map/ppermute | solution.py:189
  30.9 0.6 %copy-done.8 = s32[4]{0:T(128)S(1)} copy-done((s32[4]{0:T(128)S(1)}, s32[4]{0:T(128)}, u32[]{:S(2)}) %copy-start.8) | copy-done | bytes 40
  31.6 0.0 copy-done.10
  31.6 1.6 %shard_map.80 = (f32[2,128,128]{2,1,0:T(8,128)S(1)}, f32[2,128,128]{2,1,0:T(8,128)S(1)}, f32[8,128]{1,0:T(8,128)S(1)}) custom-call(s32[4]{0:T(128)S(1)} %copy-done.8, s32[4]{0:T(128)S(1)} %copy-done.10, s32[4,4]{1,0:T(4,128)S(1)} %copy-done.6, f32[2,128,128]{2,1,0:T(8,128)S(1)} %add.13.own, f32[2,128,128]{2,1,0:T(8,128)S(1)} %collective-permute-done.6.other, ...), custom_call_target="tpu_custom_call" | custom-call | tf_op jit(solution)/shard_map/pallas_call | solution.py:218
  33.2 0.6 %copy-done.3 = f32[2,128,128]{2,1,0:T(8,128)} copy-done((f32[2,128,128]{2,1,0:T(8,128)}, f32[2,128,128]{2,1,0:T(8,128)S(1)}, u32[]{:S(2)}) %copy-start.3) | copy-done | bytes 131096
  33.8 0.0 collective-permute-start.10
  33.8 0.0 collective-permute-done.3.other
  33.8 1.6 %shard_map.81 = (f32[2,128,128]{2,1,0:T(8,128)S(1)}, f32[2,128,128]{2,1,0:T(8,128)S(1)}, f32[8,128]{1,0:T(8,128)S(1)}) custom-call(s32[4]{0:T(128)S(1)} %copy-done.8, s32[4]{0:T(128)S(1)} %copy-done.10, s32[4,4]{1,0:T(4,128)S(1)} %copy-done.6, f32[2,128,128]{2,1,0:T(8,128)S(1)} %add.12.own, f32[2,128,128]{2,1,0:T(8,128)S(1)} %collective-permute-done.3.other, ...), custom_call_target="tpu_custom_call" | custom-call | tf_op jit(solution)/shard_map/pallas_call | solution.py:218
  35.4 0.0 copy-start.4
  35.4 0.6 %collective-permute-start.12 = (f32[2,128,128]{2,1,0:T(8,128)S(1)}, f32[2,128,128]{2,1,0:T(8,128)S(1)}, u32[]{:S(2)}, u32[]{:S(2)}) collective-permute-start(f32[2,128,128]{2,1,0:T(8,128)S(1)} %get-tuple-element.18), channel_id=1, source_target_pairs={{0,1},{1,0},{2,3},{3,2},{4,5},{5,4},{6,7},{7,6},{8,9},{9,8},{10,11... | collective-permute-start | bytes 393224 | tf_op jit(solution)/shard_map/ppermute | solution.py:186
  36.0 0.0 collective-permute-done.10
  36.0 0.0 copy-done.4
  36.0 1.5 %collective-permute-start.11 = (f32[2,128,128]{2,1,0:T(8,128)S(1)}, f32[2,128,128]{2,1,0:T(8,128)S(1)}, u32[]{:S(2)}, u32[]{:S(2)}) collective-permute-start(f32[2,128,128]{2,1,0:T(8,128)S(1)} %add.14.refs_4_), channel_id=1, source_target_pairs={{0,2},{1,3},{2,0},{3,1},{4,6},{5,7},{6,4},{7,5},{8,10},{9,11},{10,... | collective-permute-start | bytes 393224 | tf_op jit(solution)/shard_map/ppermute | solution.py:189
  37.6 0.0 collective-permute-done.12
  37.6 1.0 %collective-permute-start.13 = (f32[2,128,128]{2,1,0:T(8,128)S(1)}, f32[2,128,128]{2,1,0:T(8,128)S(1)}, u32[]{:S(2)}, u32[]{:S(2)}) collective-permute-start(f32[2,128,128]{2,1,0:T(8,128)S(1)} %add.15.refs_7_), channel_id=1, source_target_pairs={{0,2},{1,3},{2,0},{3,1},{4,6},{5,7},{6,4},{7,5},{8,10},{9,11},{10,... | collective-permute-start | bytes 393224 | tf_op jit(solution)/shard_map/ppermute | solution.py:189
  38.6 1.2 %collective-permute-start.7 = (f32[8,128]{1,0:T(8,128)S(1)}, f32[8,128]{1,0:T(8,128)S(1)}, u32[]{:S(2)}, u32[]{:S(2)}) collective-permute-start(f32[8,128]{1,0:T(8,128)S(1)} %get-tuple-element.15.refs_0_), channel_id=1, source_target_pairs={{0,4},{4,0},{8,12},{12,8},{1,5},{5,1},{9,13},{13,9},{2,6},{6,2},{1... | collective-permute-start | bytes 12296 | tf_op jit(solution)/shard_map/ppermute | solution.py:177
  39.8 1.8 %collective-permute-start.8 = (f32[8,128]{1,0:T(8,128)S(1)}, f32[8,128]{1,0:T(8,128)S(1)}, u32[]{:S(2)}, u32[]{:S(2)}) collective-permute-start(f32[8,128]{1,0:T(8,128)S(1)} %get-tuple-element.15.refs_0_), channel_id=1, source_target_pairs={{0,8},{8,0},{4,12},{12,4},{1,9},{9,1},{5,13},{13,5},{2,10},{10,2},... | collective-permute-start | bytes 12296 | tf_op jit(solution)/shard_map/ppermute | solution.py:180
  41.6 1.4 %collective-permute-start.9 = (f32[8,128]{1,0:T(8,128)S(1)}, f32[8,128]{1,0:T(8,128)S(1)}, u32[]{:S(2)}, u32[]{:S(2)}) collective-permute-start(f32[8,128]{1,0:T(8,128)S(1)} %get-tuple-element.15.refs_0_), channel_id=1, source_target_pairs={{0,12},{12,0},{4,8},{8,4},{1,13},{13,1},{5,9},{9,5},{2,14},{14,2},... | collective-permute-start | bytes 12296 | tf_op jit(solution)/shard_map/ppermute | solution.py:183
  43.0 0.0 collective-permute-done.11.refs_5_
  43.0 0.0 collective-permute-done.7.refs_1_
  43.0 1.3 %collective-permute-done.8.refs_2_ = f32[8,128]{1,0:T(8,128)S(1)} collective-permute-done((f32[8,128]{1,0:T(8,128)S(1)}, f32[8,128]{1,0:T(8,128)S(1)}, u32[]{:S(2)}, u32[]{:S(2)}) %collective-permute-start.8) | collective-permute-done | bytes 4128 | tf_op jit(solution)/shard_map/ppermute | solution.py:180
  44.3 2.7 %collective-permute-done.9.refs_3_ = f32[8,128]{1,0:T(8,128)S(1)} collective-permute-done((f32[8,128]{1,0:T(8,128)S(1)}, f32[8,128]{1,0:T(8,128)S(1)}, u32[]{:S(2)}, u32[]{:S(2)}) %collective-permute-start.9) | collective-permute-done | bytes 4128 | tf_op jit(solution)/shard_map/ppermute | solution.py:183
  47.0 0.0 collective-permute-done.13.refs_8_
  47.1 0.5 %copy-done.18 = f32[8,128]{1,0:T(8,128)} copy-done((f32[8,128]{1,0:T(8,128)}, f32[8,128]{1,0:T(8,128)S(1)}, u32[]{:S(2)}) %copy-start.18) | copy-done | bytes 4120
  47.6 0.1 copy-done.15
  47.7 2.3 %shard_map.82 = (f32[128,512]{1,0:T(8,128)}, f32[1]{0:T(128)}) custom-call(s32[4]{0:T(128)} %left_sizes.7, s32[4]{0:T(128)} %right_sizes.7, s32[4,4]{1,0:T(4,128)} %pairs.7, f32[8,128]{1,0:T(8,128)} %copy-done.11, f32[8,128]{1,0:T(8,128)} %copy-done.16, f32[8,128]{1,0:T(8,128)} %copy-done.17, f32[8,128]{1,0:T(8,128)} %copy-done.18, ...), custom_call_target="tpu_custom_call" | custom-call | tf_op jit(solution)/shard_map/pallas_call | solution.py:229
  (28 shorter events, 0.1 us)
Async XLA Ops:
  0.6 22.1 %copy-start = (f32[4,128,128]{2,1,0:T(8,128)S(1)}, f32[4,128,128]{2,1,0:T(8,128)}, u32[]{:S(2)}) copy-start(f32[4,128,128]{2,1,0:T(8,128)} %refs_0_.3) | copy-start | bytes 786436
  0.6 12.5 %collective-permute-start = (f32[4,128,128]{2,1,0:T(8,128)}, f32[4,128,128]{2,1,0:T(8,128)S(1)}, u32[]{:S(2)}, u32[]{:S(2)}) collective-permute-start(f32[4,128,128]{2,1,0:T(8,128)} %refs_0_.3), channel_id=1, source_target_pairs={{0,12},{12,0},{4,8},{8,4},{1,13},{13,1},{5,9},{9,5},{2,14},{14,2},... | collective-permute-start | bytes 786440 | tf_op jit(solution)/shard_map/ppermute | solution.py:183
  5.8 16.9 %collective-permute-start.4 = (f32[4,128,128]{2,1,0:T(8,128)}, f32[4,128,128]{2,1,0:T(8,128)S(1)}, u32[]{:S(2)}, u32[]{:S(2)}) collective-permute-start(f32[4,128,128]{2,1,0:T(8,128)} %refs_0_.3), channel_id=1, source_target_pairs={{0,4},{4,0},{8,12},{12,8},{1,5},{5,1},{9,13},{13,9},{2,6},{6,2},{1... | collective-permute-start | bytes 786440 | tf_op jit(solution)/shard_map/ppermute | solution.py:177
  13.2 10.4 %collective-permute-start.1 = (f32[4,128,128]{2,1,0:T(8,128)S(1)}, f32[4,128,128]{2,1,0:T(8,128)S(1)}, u32[]{:S(2)}, u32[]{:S(2)}) collective-permute-start(f32[4,128,128]{2,1,0:T(8,128)S(1)} %collective-permute-done.refs_0_), channel_id=1, source_target_pairs={{0,4},{4,0},{8,12},{12,8},{1,5},{5,1},{9,13},{13,9},{2,6},{6,2},{1... | collective-permute-start | bytes 786440 | tf_op jit(solution)/shard_map/ppermute | solution.py:177
  17.6 0.9 %copy-start.1 = (f32[128,512]{1,0:T(8,128)S(1)}, f32[128,512]{1,0:T(8,128)}, u32[]{:S(2)}) copy-start(f32[128,512]{1,0:T(8,128)} %wave.1) | copy-start | bytes 786436
  18.6 0.9 %copy-start.2 = (f32[4,128,128]{2,1,0:T(8,128)S(1)}, f32[4,128,128]{2,1,0:T(8,128)}, u32[]{:S(2)}) copy-start(f32[4,128,128]{2,1,0:T(8,128)} %left.1) | copy-start | bytes 786436
  19.5 0.7 %copy-start.5 = (s32[4,4]{1,0:T(4,128)S(1)}, s32[4,4]{1,0:T(4,128)}, u32[]{:S(2)}) copy-start(s32[4,4]{1,0:T(4,128)} %pairs.7) | copy-start | bytes 196
  20.2 0.7 %copy-start.7 = (s32[4]{0:T(128)S(1)}, s32[4]{0:T(128)}, u32[]{:S(2)}) copy-start(s32[4]{0:T(128)} %left_sizes.7) | copy-start | bytes 52
  20.8 0.7 %copy-start.9 = (s32[4]{0:T(128)S(1)}, s32[4]{0:T(128)}, u32[]{:S(2)}) copy-start(s32[4]{0:T(128)} %right_sizes.7) | copy-start | bytes 52
  23.1 1.4 %collective-permute-start.5 = (f32[2,128,128]{2,1,0:T(8,128)S(1)}, f32[2,128,128]{2,1,0:T(8,128)S(1)}, u32[]{:S(2)}, u32[]{:S(2)}) collective-permute-start(f32[2,128,128]{2,1,0:T(8,128)S(1)} %shard_map.79), channel_id=1, source_target_pairs={{0,1},{1,0},{2,3},{3,2},{4,5},{5,4},{6,7},{7,6},{8,9},{9,8},{10,11... | collective-permute-start | bytes 393224 | tf_op jit(solution)/shard_map/ppermute | solution.py:186
  24.0 2.1 %collective-permute-start.2 = (f32[2,128,128]{2,1,0:T(8,128)S(1)}, f32[2,128,128]{2,1,0:T(8,128)S(1)}, u32[]{:S(2)}, u32[]{:S(2)}) collective-permute-start(f32[2,128,128]{2,1,0:T(8,128)S(1)} %shard_map.78), channel_id=1, source_target_pairs={{0,1},{1,0},{2,3},{3,2},{4,5},{5,4},{6,7},{7,6},{8,9},{9,8},{10,11... | collective-permute-start | bytes 393224 | tf_op jit(solution)/shard_map/ppermute | solution.py:186
  24.5 6.4 %collective-permute-start.6 = (f32[2,128,128]{2,1,0:T(8,128)S(1)}, f32[2,128,128]{2,1,0:T(8,128)S(1)}, u32[]{:S(2)}, u32[]{:S(2)}) collective-permute-start(f32[2,128,128]{2,1,0:T(8,128)S(1)} %add.13.own), channel_id=1, source_target_pairs={{0,2},{1,3},{2,0},{3,1},{4,6},{5,7},{6,4},{7,5},{8,10},{9,11},{10,... | collective-permute-start | bytes 393224 | tf_op jit(solution)/shard_map/ppermute | solution.py:189
  26.1 4.8 %copy-start.6 = (s32[4,4]{1,0:T(4,128)S(1)}, s32[4,4]{1,0:T(4,128)}, u32[]{:S(2)}) copy-start(s32[4,4]{1,0:T(4,128)} %pairs.7) | copy-start | bytes 196
  26.1 7.7 %collective-permute-start.3 = (f32[2,128,128]{2,1,0:T(8,128)S(1)}, f32[2,128,128]{2,1,0:T(8,128)S(1)}, u32[]{:S(2)}, u32[]{:S(2)}) collective-permute-start(f32[2,128,128]{2,1,0:T(8,128)S(1)} %add.12.own), channel_id=1, source_target_pairs={{0,2},{1,3},{2,0},{3,1},{4,6},{5,7},{6,4},{7,5},{8,10},{9,11},{10,... | collective-permute-start | bytes 393224 | tf_op jit(solution)/shard_map/ppermute | solution.py:189
  30.9 0.7 %copy-start.8 = (s32[4]{0:T(128)S(1)}, s32[4]{0:T(128)}, u32[]{:S(2)}) copy-start(s32[4]{0:T(128)} %left_sizes.7) | copy-start | bytes 52
  30.9 0.7 %copy-start.10 = (s32[4]{0:T(128)S(1)}, s32[4]{0:T(128)}, u32[]{:S(2)}) copy-start(s32[4]{0:T(128)} %right_sizes.7) | copy-start | bytes 52
  33.2 0.7 %copy-start.3 = (f32[2,128,128]{2,1,0:T(8,128)}, f32[2,128,128]{2,1,0:T(8,128)S(1)}, u32[]{:S(2)}) copy-start(f32[2,128,128]{2,1,0:T(8,128)S(1)} %get-tuple-element.17.refs_6_) | copy-start | bytes 393220
  33.8 2.2 %collective-permute-start.10 = (f32[2,128,128]{2,1,0:T(8,128)S(1)}, f32[2,128,128]{2,1,0:T(8,128)S(1)}, u32[]{:S(2)}, u32[]{:S(2)}) collective-permute-start(f32[2,128,128]{2,1,0:T(8,128)S(1)} %get-tuple-element.16), channel_id=1, source_target_pairs={{0,1},{1,0},{2,3},{3,2},{4,5},{5,4},{6,7},{7,6},{8,9},{9,8},{10,11... | collective-permute-start | bytes 393224 | tf_op jit(solution)/shard_map/ppermute | solution.py:186
  35.4 0.6 %copy-start.4 = (f32[2,128,128]{2,1,0:T(8,128)}, f32[2,128,128]{2,1,0:T(8,128)S(1)}, u32[]{:S(2)}) copy-start(f32[2,128,128]{2,1,0:T(8,128)S(1)} %get-tuple-element.19.refs_9_) | copy-start | bytes 393220
  35.4 6.2 %copy-start.11 = (f32[8,128]{1,0:T(8,128)}, f32[8,128]{1,0:T(8,128)S(1)}, u32[]{:S(2)}) copy-start(f32[8,128]{1,0:T(8,128)S(1)} %get-tuple-element.15.refs_0_) | copy-start | bytes 12292
  35.4 2.2 %collective-permute-start.12 = (f32[2,128,128]{2,1,0:T(8,128)S(1)}, f32[2,128,128]{2,1,0:T(8,128)S(1)}, u32[]{:S(2)}, u32[]{:S(2)}) collective-permute-start(f32[2,128,128]{2,1,0:T(8,128)S(1)} %get-tuple-element.18), channel_id=1, source_target_pairs={{0,1},{1,0},{2,3},{3,2},{4,5},{5,4},{6,7},{7,6},{8,9},{9,8},{10,11... | collective-permute-start | bytes 393224 | tf_op jit(solution)/shard_map/ppermute | solution.py:186
  36.0 1.6 %copy-start.12 = (f32[2,128,128]{2,1,0:T(8,128)}, f32[2,128,128]{2,1,0:T(8,128)S(1)}, u32[]{:S(2)}) copy-start(f32[2,128,128]{2,1,0:T(8,128)S(1)} %add.14.refs_4_) | copy-start | bytes 393220
  36.0 6.9 %collective-permute-start.11 = (f32[2,128,128]{2,1,0:T(8,128)S(1)}, f32[2,128,128]{2,1,0:T(8,128)S(1)}, u32[]{:S(2)}, u32[]{:S(2)}) collective-permute-start(f32[2,128,128]{2,1,0:T(8,128)S(1)} %add.14.refs_4_), channel_id=1, source_target_pairs={{0,2},{1,3},{2,0},{3,1},{4,6},{5,7},{6,4},{7,5},{8,10},{9,11},{10,... | collective-permute-start | bytes 393224 | tf_op jit(solution)/shard_map/ppermute | solution.py:189
  37.6 9.4 %copy-start.13 = (f32[2,128,128]{2,1,0:T(8,128)}, f32[2,128,128]{2,1,0:T(8,128)S(1)}, u32[]{:S(2)}) copy-start(f32[2,128,128]{2,1,0:T(8,128)S(1)} %add.15.refs_7_) | copy-start | bytes 393220
  37.6 9.4 %collective-permute-start.13 = (f32[2,128,128]{2,1,0:T(8,128)S(1)}, f32[2,128,128]{2,1,0:T(8,128)S(1)}, u32[]{:S(2)}, u32[]{:S(2)}) collective-permute-start(f32[2,128,128]{2,1,0:T(8,128)S(1)} %add.15.refs_7_), channel_id=1, source_target_pairs={{0,2},{1,3},{2,0},{3,1},{4,6},{5,7},{6,4},{7,5},{8,10},{9,11},{10,... | collective-permute-start | bytes 393224 | tf_op jit(solution)/shard_map/ppermute | solution.py:189
  38.6 4.4 %collective-permute-start.7 = (f32[8,128]{1,0:T(8,128)S(1)}, f32[8,128]{1,0:T(8,128)S(1)}, u32[]{:S(2)}, u32[]{:S(2)}) collective-permute-start(f32[8,128]{1,0:T(8,128)S(1)} %get-tuple-element.15.refs_0_), channel_id=1, source_target_pairs={{0,4},{4,0},{8,12},{12,8},{1,5},{5,1},{9,13},{13,9},{2,6},{6,2},{1... | collective-permute-start | bytes 12296 | tf_op jit(solution)/shard_map/ppermute | solution.py:177
  39.8 4.5 %collective-permute-start.8 = (f32[8,128]{1,0:T(8,128)S(1)}, f32[8,128]{1,0:T(8,128)S(1)}, u32[]{:S(2)}, u32[]{:S(2)}) collective-permute-start(f32[8,128]{1,0:T(8,128)S(1)} %get-tuple-element.15.refs_0_), channel_id=1, source_target_pairs={{0,8},{8,0},{4,12},{12,4},{1,9},{9,1},{5,13},{13,5},{2,10},{10,2},... | collective-permute-start | bytes 12296 | tf_op jit(solution)/shard_map/ppermute | solution.py:180
  41.6 5.4 %collective-permute-start.9 = (f32[8,128]{1,0:T(8,128)S(1)}, f32[8,128]{1,0:T(8,128)S(1)}, u32[]{:S(2)}, u32[]{:S(2)}) collective-permute-start(f32[8,128]{1,0:T(8,128)S(1)} %get-tuple-element.15.refs_0_), channel_id=1, source_target_pairs={{0,12},{12,0},{4,8},{8,4},{1,13},{13,1},{5,9},{9,5},{2,14},{14,2},... | collective-permute-start | bytes 12296 | tf_op jit(solution)/shard_map/ppermute | solution.py:183
  43.0 4.1 %copy-start.14 = (f32[2,128,128]{2,1,0:T(8,128)}, f32[2,128,128]{2,1,0:T(8,128)S(1)}, u32[]{:S(2)}) copy-start(f32[2,128,128]{2,1,0:T(8,128)S(1)} %collective-permute-done.11.refs_5_) | copy-start | bytes 393220
  43.0 4.1 %copy-start.16 = (f32[8,128]{1,0:T(8,128)}, f32[8,128]{1,0:T(8,128)S(1)}, u32[]{:S(2)}) copy-start(f32[8,128]{1,0:T(8,128)S(1)} %collective-permute-done.7.refs_1_) | copy-start | bytes 12292
  44.3 2.7 %copy-start.17 = (f32[8,128]{1,0:T(8,128)}, f32[8,128]{1,0:T(8,128)S(1)}, u32[]{:S(2)}) copy-start(f32[8,128]{1,0:T(8,128)S(1)} %collective-permute-done.8.refs_2_) | copy-start | bytes 12292
  47.0 0.6 %copy-start.18 = (f32[8,128]{1,0:T(8,128)}, f32[8,128]{1,0:T(8,128)S(1)}, u32[]{:S(2)}) copy-start(f32[8,128]{1,0:T(8,128)S(1)} %collective-permute-done.9.refs_3_) | copy-start | bytes 12292
  47.0 0.6 %copy-start.15 = (f32[2,128,128]{2,1,0:T(8,128)}, f32[2,128,128]{2,1,0:T(8,128)S(1)}, u32[]{:S(2)}) copy-start(f32[2,128,128]{2,1,0:T(8,128)S(1)} %collective-permute-done.13.refs_8_) | copy-start | bytes 393220

commit v3 on v2

v3 whole, which is shorter than its diff:
```python
import functools

import jax
import jax.numpy as jnp
from jax import lax
from jax.experimental import pallas as pl
from jax.experimental.pallas import tpu as pltpu
from jax.sharding import PartitionSpec as P

EXACT = lax.Precision.HIGHEST
TINY = 1e-06
PARAMS = pltpu.CompilerParams(vmem_limit_bytes=32 * 1024 * 1024)
VMEM = pl.BlockSpec(memory_space=pltpu.VMEM)
SMEM = pl.BlockSpec(memory_space=pltpu.SMEM)
F32 = jnp.float32
BF16 = jnp.bfloat16

EARLY, LATE = (0, 1, 2), (3,)


def split(x):
    high = x.astype(BF16)
    return high, (x - high.astype(F32)).astype(BF16)


def left_terms(x):
    high, low = split(x)
    return jnp.concatenate([high, high, low], axis=1)


def right_terms(x):
    high, low = split(x)
    return jnp.concatenate([high, low, high], axis=0)


def times(a, b):
    return lax.dot_general(a, b, (((1,), (0,)), ((), ())), preferred_element_type=F32)


def times_turned(a, b):
    m, n = a.shape[0], b.shape[0]
    both = lax.dot_general(
        jnp.concatenate(split(a), axis=0),
        jnp.concatenate(split(b), axis=0),
        (((1,), (1,)), ((), ())),
        preferred_element_type=F32,
    )
    return (both[m:, n:] + (both[m:, :n] + both[:m, n:])) + both[:m, :n]


def block_valid(left_sizes, right_sizes, pairs, a, b, rows, cols):
    row = lax.broadcasted_iota(jnp.int32, (rows, cols), 0) < left_sizes[a]
    col = lax.broadcasted_iota(jnp.int32, (rows, cols), 1) < right_sizes[b]
    return (row & col).astype(F32) * pairs[a, b].astype(F32)


def call(body, outs, n_small, n_big):
    return pl.pallas_call(
        body,
        out_shape=outs,
        in_specs=[SMEM] * n_small + [VMEM] * n_big,
        out_specs=[VMEM] * len(outs),
        compiler_params=PARAMS,
    )


def slot_column(slot, sector):
    return sector ^ (0, 1, 3, 2)[slot]


def columns(b, width):
    return pl.ds(pl.multiple_of(b * width, width), width)


def channel_row(blocks):
    return jnp.concatenate([blocks[w] for w in range(blocks.shape[0])], axis=1)


def half_body(left_sizes, right_sizes, pairs, wave, left, vector, halfway, factors, valid):
    sector = lax.axis_index("sector")
    channels, rows, _ = left.shape
    slots, _, inner = halfway.shape
    cols = inner // channels
    factors[...] = left_terms(left[...].reshape(channels * rows, rows))
    for k in range(slots):
        b = slot_column(k, sector)
        valid[k] = block_valid(left_sizes, right_sizes, pairs, sector, b, rows, cols)
        vector[k] = wave[:, columns(b, cols)] * valid[k]
    part = times(factors[...], right_terms(channel_row(vector)))
    for k in range(slots):
        for w in range(channels):
            halfway[k, :, w * cols : (w + 1) * cols] = part[
                w * rows : (w + 1) * rows, k * cols : (k + 1) * cols
            ]


def first_body(slots, halfway, *refs):
    out = refs[-1]
    for k, slot in enumerate(slots):
        out[k] = times_turned(halfway[slot], channel_row(refs[k]))


def second_images(slots, own, other, valid, factors, rights, image):
    _, rows, cols = own.shape
    channels = factors.shape[0] // rows
    for k, slot in enumerate(slots):
        image[k] = (own[k] + other[k]) * valid[slot]
    half = times(factors[...], right_terms(channel_row(image)))
    partials = []
    for k in range(len(slots)):
        here = half[:, k * cols : (k + 1) * cols].reshape(channels, rows, cols)
        partials.append(times_turned(channel_row(here), channel_row(rights[k])))
    return partials


def write_sums(slots, vector, image, sums, at):
    cols = vector.shape[2]
    cross = jnp.zeros((1, cols), F32)
    square = jnp.zeros((1, cols), F32)
    for k, slot in enumerate(slots):
        v = vector[slot]
        cross += jnp.sum(v * image[k], axis=0, keepdims=True)
        square += jnp.sum(v * v, axis=0, keepdims=True)
    ratio = jnp.where(square > 0, cross / jnp.where(square > 0, square, 1.0), 0.0)
    rest = jnp.zeros((1, cols), F32)
    for k, slot in enumerate(slots):
        away = image[k] - ratio * vector[slot]
        rest += jnp.sum(away * away, axis=0, keepdims=True)
    sums[at : at + 1, :] = cross
    sums[at + 1 : at + 2, :] = square
    sums[at + 2 : at + 3, :] = rest


def early_body(slots, own, other, valid, factors, vector, *refs):
    image, partial, sums = refs[-3:]
    parts = second_images(slots, own, other, valid, factors, refs[:-3], image)
    for k, part in enumerate(parts):
        partial[k] = part
    sums[...] = jnp.zeros_like(sums)
    write_sums(slots, vector, image, sums, 0)


def late_body(early, slots, own, other, valid, factors, vector, sums_before, before, *refs):
    image, keep, send, sums = refs[-4:]
    me = lax.axis_index("mpo") % 2
    parts = second_images(slots, own, other, valid, factors, refs[:-4], image)
    everything = {slot: before[k] for k, slot in enumerate(early)}
    everything.update(zip(slots, parts))
    for half in (0, 1):

        @pl.when(me == half)
        def _():
            for k in (0, 1):
                keep[k] = everything[2 * half + k]
                send[k] = everything[2 * (1 - half) + k]

    sums[...] = sums_before[...]
    write_sums(slots, vector, image, sums, 3)


def last_body(groups, cells, valid, near, far, *refs):
    product, ritz = refs[-2:]
    sector = lax.axis_index("sector")

    def everyone(read):
        lanes = (read(near, 0) + read(near, 16)) + (read(far, 0) + read(far, 16))
        return jnp.sum(lanes)

    def every_group(row):
        return lambda s, at: sum(
            s[at + row + 3 * g : at + row + 3 * g + 1, :] for g in range(len(groups))
        )

    value = everyone(every_group(0)) / (everyone(every_group(1)) + TINY)

    def rest_of(s, at):
        total = every_group(2)(s, at)
        for row in range(at, at + 3 * len(groups), 3):
            c = s[row + 1 : row + 2, :]
            ratio = jnp.where(c > 0, s[row : row + 1, :] / jnp.where(c > 0, c, 1.0), 0.0)
            total += (ratio - value) * (ratio - value) * c
        return total

    scale = 1.0 / jnp.sqrt(everyone(rest_of) / cells + TINY)
    ritz[0] = value
    total, others = refs[:2]
    me = lax.axis_index("mpo") % 2
    cols = total.shape[2]
    for slots, image in zip(groups, refs[2:-2]):
        for k, slot in enumerate(slots):
            b = slot_column(slot, sector)
            second = jnp.where(me == slot // 2, total[slot % 2], others[slot % 2])
            product[:, columns(b, cols)] = (second * valid[slot] - value * image[k]) * scale


def line_device(wave, left, right, left_sizes, right_sizes, pairs):
    channels, rows, _ = left.shape
    cols = right.shape[2]
    sectors = 4
    cells = float(sectors * rows * sectors * cols)

    def near(x):
        return lax.ppermute(x, "sector", [(0, 1), (1, 0), (2, 3), (3, 2)])

    def far(x):
        return lax.ppermute(x, "sector", [(0, 2), (2, 0), (1, 3), (3, 1)])

    def mirror(x):
        return lax.ppermute(x, "sector", [(0, 3), (3, 0), (1, 2), (2, 1)])

    def core(x):
        return lax.ppermute(x, "mpo", [(0, 1), (1, 0), (2, 3), (3, 2)])

    def across(x):
        return lax.ppermute(x, "mpo", [(0, 2), (1, 3), (2, 0), (3, 1)])

    def shape(*dims, of=F32):
        return jax.ShapeDtypeStruct(dims, of)

    def after(x, *others):
        return lax.optimization_barrier((x, *others))[0]

    right_near = near(right)
    right_mirror = mirror(right)
    vector, halfway, factors, valid = call(
        half_body,
        [
            shape(sectors, rows, cols),
            shape(sectors, rows, channels * cols),
            shape(channels * rows, 3 * rows, of=BF16),
            shape(sectors, rows, cols),
        ],
        3,
        2,
    )(left_sizes, right_sizes, pairs, wave, left)
    right_far = near(after(right_mirror, halfway))

    def partials(slots, halfway, *rights):
        return call(
            functools.partial(first_body, slots), [shape(len(slots), rows, cols)], 0, 1 + len(slots)
        )(halfway, *rights)[0]

    def chip_sum(x):
        return x + core(x)

    one = chip_sum(after(partials((0,), halfway, right), right_mirror))
    two = chip_sum(partials((1, 2), after(halfway, one), right_near, right_mirror))
    three = chip_sum(partials((3,), after(halfway, two), right_far))
    image_early, second_early, sums = call(
        functools.partial(early_body, EARLY),
        [shape(3, rows, cols), shape(3, rows, cols), shape(16, cols)],
        0,
        8,
    )(
        jnp.concatenate([one, two]),
        jnp.concatenate([across(one), across(two)]),
        valid,
        factors,
        vector,
        right,
        right_near,
        right_mirror,
    )
    image_late, keep, send, sums = call(
        functools.partial(late_body, EARLY, LATE),
        [shape(1, rows, cols), shape(2, rows, cols), shape(2, rows, cols), shape(16, cols)],
        0,
        8,
    )(three, across(three), valid, factors, vector, sums, second_early, right_far)

    mine = keep + core(send)
    sums_near = jnp.concatenate([sums, near(sums)])
    sums_far = far(sums_near)
    total = after(mine + across(mine), sums_far)
    others = core(total)
    product, ritz = pl.pallas_call(
        functools.partial(last_body, (EARLY, LATE), cells),
        out_shape=[shape(rows, sectors * cols), shape(1)],
        in_specs=[VMEM] * 7,
        out_specs=[VMEM, SMEM],
        compiler_params=PARAMS,
    )(valid, sums_near, sums_far, total, others, image_early, image_late)
    return product, ritz


def wide_device(wave, left, right, left_sizes, right_sizes, pairs):
    sector = lax.axis_index("sector")
    sectors = lax.axis_size("sector")
    channels, rows, _ = left.shape
    cols = right.shape[2]
    cells = float(sectors * rows * sectors * cols)
    own = lax.dynamic_index_in_dim(pairs, sector, 0, keepdims=False).astype(F32)
    size = lax.dynamic_index_in_dim(left_sizes, sector, 0, keepdims=False)
    row = (jnp.arange(rows) < size).astype(F32)
    col = (jnp.arange(cols)[None, :] < right_sizes[:, None]).astype(F32) * own[:, None]
    valid = row[:, None] * col.reshape(1, -1)
    vector = wave * valid
    rights = lax.all_gather(right, "sector", axis=1)

    def image_of(v):
        half = jnp.einsum("wik,kbc->wibc", left, v.reshape(rows, sectors, cols), precision=EXACT)
        out = jnp.einsum("wibc,wbjc->ibj", half, rights, precision=EXACT)
        return lax.psum(out.reshape(rows, sectors * cols), "mpo") * valid

    first = image_of(vector)
    cross, square = lax.psum((jnp.sum(vector * first), jnp.sum(vector * vector)), "sector")
    value = cross / (square + TINY)
    residual = first - value * vector
    rest = lax.psum(jnp.sum(residual * residual), "sector")
    product = image_of(residual / jnp.sqrt(rest / cells + TINY))
    return product, jnp.reshape(value, (1,))


def solution(mesh):
    line = mesh.shape["sector"] == 4 and mesh.shape["mpo"] == 4
    return jax.shard_map(
        line_device if line else wide_device,
        mesh=mesh,
        in_specs=(
            P(("groups", "sector"), None),
            P("mpo", ("groups", "sector"), None),
            P("mpo", ("groups", "sector"), None),
            P("groups"),
            P("groups"),
            P("groups", None),
        ),
        out_specs=(P(("groups", "sector"), None), P("groups")),
        check_vma=False,
    )
```

time: 50.3 us -> 41.2 us (0.82)
  waiting for transfers between devices: 16.2 us -> 12.7 us
  Pallas kernels: 7.39 us -> 4.41 us
  local copies, waits for them, and re-layouts: 5.87 us -> 3.9 us
    ppermute x2 -> x1, waiting for transfers between devices: 10.1 us -> 2.43 us  [mirror(): return lax.ppermute(x, 'sector', [(0, 3), (3, 0), (1, 2), (2, 1)])]
    ppermute x4 -> x5, waiting for transfers between devices: 0.39 us -> 5 us  [core(): return lax.ppermute(x, 'mpo', [(0, 1), (1, 0), (2, 3), (3, 2)])]
    pallas_call x6 -> x7, Pallas kernels: 7.39 us -> 4.41 us  [the longest x1 1.12 us: line_device(): pl.pallas_call(functools.partial(last_body, (EARLY, LATE), cells), out_sh...]
    unnamed x38 -> x13, local copies, waits for them, and re-layouts: 5.87 us -> 3.9 us
    ppermute x2 -> x1, starting transfers between devices: 6.46 us -> 5.11 us  [mirror(): return lax.ppermute(x, 'sector', [(0, 3), (3, 0), (1, 2), (2, 1)])]
    ppermute x3, starting transfers between devices: 5.66 us -> 6.16 us  [near(): return lax.ppermute(x, 'sector', [(0, 1), (1, 0), (2, 3), (3, 2)])]
  transfers between devices with their start and end apart: 14 -> 14, of which waited for: 6 -> 11; matrix products, arithmetic and copies ran while one was open for 0% -> 0% of each run, Pallas kernels for 10% -> 7%
where the time goes in v3:
time: 41.2 us; the launch traced here: 41 us
  starting transfers between devices  19.1 us (46%)
  waiting for transfers between devices  12.7 us (31%)
  Pallas kernels  4.41 us (11%)
  local copies, waits for them, and re-layouts  3.9 us (9%)
  between operations  0.75 us (2%)
    ppermute x3, starting transfers between devices, near(): return lax.ppermute(x, 'sector', [(0, 1), (1, 0), (2, 3), (3, 2)])  6.16 us
    ppermute x4, starting transfers between devices, across(): return lax.ppermute(x, 'mpo', [(0, 2), (1, 3), (2, 0), (3, 1)])  5.21 us
    ppermute x1, starting transfers between devices, mirror(): return lax.ppermute(x, 'sector', [(0, 3), (3, 0), (1, 2), (2, 1)])  5.11 us
    ppermute x5, waiting for transfers between devices, core(): return lax.ppermute(x, 'mpo', [(0, 1), (1, 0), (2, 3), (3, 2)])  5 us
    unnamed x13, local copies, waits for them, and re-layouts  3.9 us
    ppermute x4, waiting for transfers between devices, across(): return lax.ppermute(x, 'mpo', [(0, 2), (1, 3), (2, 0), (3, 1)])  3.46 us
    ppermute x1, waiting for transfers between devices, mirror(): return lax.ppermute(x, 'sector', [(0, 3), (3, 0), (1, 2), (2, 1)])  2.43 us
    ppermute x1, starting transfers between devices, far(): return lax.ppermute(x, 'sector', [(0, 2), (2, 0), (1, 3), (3, 1)])  2.18 us
  transfers between devices with their start and end apart: 14, of which 11 were waited for; matrix products, arithmetic and copies ran while one was open for 0% of the time, Pallas kernels for 7%

profile of v3, /device:TPU:0, one launch (start us, length us, event | category | flops | bytes accessed | tf_op | source)
XLA Modules:
  0.0 41.0 jit_solution(11786346272475589029)
XLA Ops:
  0.6 0.0 copy-start
  0.6 5.1 %collective-permute-start = (f32[4,128,128]{2,1,0:T(8,128)}, f32[4,128,128]{2,1,0:T(8,128)S(1)}, u32[]{:S(2)}, u32[]{:S(2)}) collective-permute-start(f32[4,128,128]{2,1,0:T(8,128)} %refs_0_.3), channel_id=1, source_target_pairs={{0,12},{12,0},{4,8},{8,4},{1,13},{13,1},{5,9},{9,5},{2,14},{14,2},... | collective-permute-start | bytes 786440 | tf_op jit(solution)/shard_map/ppermute | solution.py:209
  5.8 0.0 collective-permute-start.2
  5.8 0.0 copy-start.1
  5.8 0.9 %copy-done.1 = f32[128,512]{1,0:T(8,128)S(1)} copy-done((f32[128,512]{1,0:T(8,128)S(1)}, f32[128,512]{1,0:T(8,128)}, u32[]{:S(2)}) %copy-start.1) | copy-done | bytes 262168
  6.7 0.0 copy-start.2
  6.7 0.9 %copy-done.2 = f32[4,128,128]{2,1,0:T(8,128)S(1)} copy-done((f32[4,128,128]{2,1,0:T(8,128)S(1)}, f32[4,128,128]{2,1,0:T(8,128)}, u32[]{:S(2)}) %copy-start.2) | copy-done | bytes 262168
  7.7 0.0 copy-start.3
  7.7 0.7 %copy-done.3 = s32[4,4]{1,0:T(4,128)S(1)} copy-done((s32[4,4]{1,0:T(4,128)S(1)}, s32[4,4]{1,0:T(4,128)}, u32[]{:S(2)}) %copy-start.3) | copy-done | bytes 88
  8.3 0.0 copy-start.4
  8.3 0.7 %copy-done.4 = s32[4]{0:T(128)S(1)} copy-done((s32[4]{0:T(128)S(1)}, s32[4]{0:T(128)}, u32[]{:S(2)}) %copy-start.4) | copy-done | bytes 40
  9.0 0.0 copy-start.5
  9.0 0.7 %copy-done.5 = s32[4]{0:T(128)S(1)} copy-done((s32[4]{0:T(128)S(1)}, s32[4]{0:T(128)}, u32[]{:S(2)}) %copy-start.5) | copy-done | bytes 40
  9.7 1.1 %shard_map.77 = (f32[4,128,128]{2,1,0:T(8,128)S(1)}, f32[4,128,512]{2,1,0:T(8,128)S(1)}, bf16[512,384]{1,0:T(8,128)(2,1)S(1)}, f32[4,128,128]{2,1,0:T(8,128)S(1)}) custom-call(s32[4]{0:T(128)S(1)} %copy-done.4, s32[4]{0:T(128)S(1)} %copy-done.5, s32[4,4]{1,0:T(4,128)S(1)} %copy-done.3, f32[128,512]{1,0:T(8,128)S(1)} %copy-done.1, f32[4,128,128]{2,1,0:T(8,128)S(1)} %copy-done.2), custom_call_target="tpu_custom_call" | custom-call | tf_op jit(solution)/shard_map/pallas_call | solution.py:225
  10.8 2.4 %collective-permute-done.refs_1_.refs_2_ = f32[4,128,128]{2,1,0:T(8,128)S(1)} collective-permute-done((f32[4,128,128]{2,1,0:T(8,128)}, f32[4,128,128]{2,1,0:T(8,128)S(1)}, u32[]{:S(2)}, u32[]{:S(2)}) %collective-permute-start) | collective-permute-done | bytes 262176 | tf_op jit(solution)/shard_map/ppermute | solution.py:209
  13.2 4.4 %collective-permute-start.4 = (f32[4,128,128]{2,1,0:T(8,128)S(1)}, f32[4,128,128]{2,1,0:T(8,128)S(1)}, u32[]{:S(2)}, u32[]{:S(2)}) collective-permute-start(f32[4,128,128]{2,1,0:T(8,128)S(1)} %collective-permute-done.refs_1_.refs_2_), channel_id=1, source_target_pairs={{0,4},{4,0},{8,12},{12,8},{1,5},{5,1},{9,13},{13,9},{2,6},{6,2},{1... | collective-permute-start | bytes 786440 | tf_op jit(solution)/shard_map/ppermute | solution.py:203
  17.6 0.0 copy-done
  17.6 0.3 shard_map.78
  17.9 0.1 collective-permute-start.1
  18.0 1.2 %collective-permute-done.1 = f32[1,128,128]{2,1,0:T(8,128)S(1)} collective-permute-done((f32[1,128,128]{2,1,0:T(8,128)S(1)}, f32[1,128,128]{2,1,0:T(8,128)S(1)}, u32[]{:S(2)}, u32[]{:S(2)}) %collective-permute-start.1) | collective-permute-done | bytes 65568 | tf_op jit(solution)/shard_map/ppermute | solution.py:212
  19.2 0.0 collective-permute-done.2.refs_0_.refs_1_
  19.2 0.4 shard_map.79
  19.6 0.2 collective-permute-start.3
  19.8 1.2 %collective-permute-done.3 = f32[2,128,128]{2,1,0:T(8,128)S(1)} collective-permute-done((f32[2,128,128]{2,1,0:T(8,128)S(1)}, f32[2,128,128]{2,1,0:T(8,128)S(1)}, u32[]{:S(2)}, u32[]{:S(2)}) %collective-permute-start.3) | collective-permute-done | bytes 131104 | tf_op jit(solution)/shard_map/ppermute | solution.py:212
  21.0 1.6 %collective-permute-start.8 = (f32[2,128,128]{2,1,0:T(8,128)S(1)}, f32[2,128,128]{2,1,0:T(8,128)S(1)}, u32[]{:S(2)}, u32[]{:S(2)}) collective-permute-start(f32[2,128,128]{2,1,0:T(8,128)S(1)} %add.16), channel_id=1, source_target_pairs={{0,2},{1,3},{2,0},{3,1},{4,6},{5,7},{6,4},{7,5},{8,10},{9,11},{10,... | collective-permute-start | bytes 393224 | tf_op jit(solution)/shard_map/ppermute | solution.py:215
  22.6 0.5 %collective-permute-start.7 = (f32[1,128,128]{2,1,0:T(8,128)S(1)}, f32[1,128,128]{2,1,0:T(8,128)S(1)}, u32[]{:S(2)}, u32[]{:S(2)}) collective-permute-start(f32[1,128,128]{2,1,0:T(8,128)S(1)} %add.15), channel_id=1, source_target_pairs={{0,2},{1,3},{2,0},{3,1},{4,6},{5,7},{6,4},{7,5},{8,10},{9,11},{10,... | collective-permute-start | bytes 196616 | tf_op jit(solution)/shard_map/ppermute | solution.py:215
  23.1 0.5 %collective-permute-done.4.refs_0_ = f32[4,128,128]{2,1,0:T(8,128)S(1)} collective-permute-done((f32[4,128,128]{2,1,0:T(8,128)S(1)}, f32[4,128,128]{2,1,0:T(8,128)S(1)}, u32[]{:S(2)}, u32[]{:S(2)}) %collective-permute-start.4) | collective-permute-done | bytes 262176 | tf_op jit(solution)/shard_map/ppermute | solution.py:203
  23.6 0.3 shard_map.80
  23.9 0.1 collective-permute-start.5
  24.0 1.2 %collective-permute-done.5 = f32[1,128,128]{2,1,0:T(8,128)S(1)} collective-permute-done((f32[1,128,128]{2,1,0:T(8,128)S(1)}, f32[1,128,128]{2,1,0:T(8,128)S(1)}, u32[]{:S(2)}, u32[]{:S(2)}) %collective-permute-start.5) | collective-permute-done | bytes 65568 | tf_op jit(solution)/shard_map/ppermute | solution.py:212
  25.2 1.6 %collective-permute-start.6 = (f32[1,128,128]{2,1,0:T(8,128)S(1)}, f32[1,128,128]{2,1,0:T(8,128)S(1)}, u32[]{:S(2)}, u32[]{:S(2)}) collective-permute-start(f32[1,128,128]{2,1,0:T(8,128)S(1)} %add.17.own), channel_id=1, source_target_pairs={{0,2},{1,3},{2,0},{3,1},{4,6},{5,7},{6,4},{7,5},{8,10},{9,11},{10,... | collective-permute-start | bytes 196616 | tf_op jit(solution)/shard_map/ppermute | solution.py:215
  26.8 1.3 %collective-permute-done.7 = f32[1,128,128]{2,1,0:T(8,128)S(1)} collective-permute-done((f32[1,128,128]{2,1,0:T(8,128)S(1)}, f32[1,128,128]{2,1,0:T(8,128)S(1)}, u32[]{:S(2)}, u32[]{:S(2)}) %collective-permute-start.7) | collective-permute-done | bytes 65568 | tf_op jit(solution)/shard_map/ppermute | solution.py:215
  28.0 0.0 collective-permute-done.8
  28.1 0.8 %shard_map.81 = (f32[3,128,128]{2,1,0:T(8,128)S(1)}, f32[3,128,128]{2,1,0:T(8,128)S(1)}, f32[16,128]{1,0:T(8,128)S(1)}) custom-call(f32[3,128,128]{2,1,0:T(8,128)S(1)} %pad_maximum_fusion.own, f32[3,128,128]{2,1,0:T(8,128)S(1)} %pad_maximum_fusion.1.other, f32[4,128,128]{2,1,0:T(8,128)S(1)} %get-tuple-element.18.valid, ...), custom_call_target="tpu_custom_call" | custom-call | tf_op jit(solution)/shard_map/pallas_call | solution.py:249
  28.9 0.7 %collective-permute-done.6.other = f32[1,128,128]{2,1,0:T(8,128)S(1)} collective-permute-done((f32[1,128,128]{2,1,0:T(8,128)S(1)}, f32[1,128,128]{2,1,0:T(8,128)S(1)}, u32[]{:S(2)}, u32[]{:S(2)}) %collective-permute-start.6) | collective-permute-done | bytes 65568 | tf_op jit(solution)/shard_map/ppermute | solution.py:215
  29.5 0.5 %shard_map.82 = (f32[1,128,128]{2,1,0:T(8,128)S(1)}, f32[2,128,128]{2,1,0:T(8,128)S(1)}, f32[2,128,128]{2,1,0:T(8,128)S(1)}, f32[16,128]{1,0:T(8,128)S(1)}) custom-call(f32[1,128,128]{2,1,0:T(8,128)S(1)} %add.17.own, f32[1,128,128]{2,1,0:T(8,128)S(1)} %collective-permute-done.6.other, f32[4,128,128]{2,1,0:T(8,128)S(1)} %get-tuple-element.18.valid, ...), custom_call_target="tpu_custom_call" | custom-call | tf_op jit(solution)/shard_map/pallas_call | solution.py:264
  30.1 0.1 collective-permute-start.11
  30.1 1.7 %collective-permute-start.9 = (f32[16,128]{1,0:T(8,128)S(1)}, f32[16,128]{1,0:T(8,128)S(1)}, u32[]{:S(2)}, u32[]{:S(2)}) collective-permute-start(f32[16,128]{1,0:T(8,128)S(1)} %get-tuple-element.28), channel_id=1, source_target_pairs={{0,4},{4,0},{8,12},{12,8},{1,5},{5,1},{9,13},{13,9},{2,6},{6,2},{1... | collective-permute-start | bytes 24584 | tf_op jit(solution)/shard_map/ppermute | solution.py:203
  31.9 0.0 collective-permute-done.11
  31.9 1.6 %collective-permute-start.12 = (f32[2,128,128]{2,1,0:T(8,128)S(1)}, f32[2,128,128]{2,1,0:T(8,128)S(1)}, u32[]{:S(2)}, u32[]{:S(2)}) collective-permute-start(f32[2,128,128]{2,1,0:T(8,128)S(1)} %add.18), channel_id=1, source_target_pairs={{0,2},{1,3},{2,0},{3,1},{4,6},{5,7},{6,4},{7,5},{8,10},{9,11},{10,... | collective-permute-start | bytes 393224 | tf_op jit(solution)/shard_map/ppermute | solution.py:215
  33.5 0.4 collective-permute-done.9
  33.9 2.2 %collective-permute-start.10 = (f32[32,128]{1,0:T(8,128)S(1)}, f32[32,128]{1,0:T(8,128)S(1)}, u32[]{:S(2)}, u32[]{:S(2)}) collective-permute-start(f32[32,128]{1,0:T(8,128)S(1)} %constant_dynamic-update-slice_fusion.near), channel_id=1, source_target_pairs={{0,8},{8,0},{4,12},{12,4},{1,9},{9,1},{5,13},{13,5},{2,10},{10,2},... | collective-permute-start | bytes 49160 | tf_op jit(solution)/shard_map/ppermute | solution.py:206
  36.0 1.5 %collective-permute-done.12 = f32[2,128,128]{2,1,0:T(8,128)S(1)} collective-permute-done((f32[2,128,128]{2,1,0:T(8,128)S(1)}, f32[2,128,128]{2,1,0:T(8,128)S(1)}, u32[]{:S(2)}, u32[]{:S(2)}) %collective-permute-start.12) | collective-permute-done | bytes 131104 | tf_op jit(solution)/shard_map/ppermute | solution.py:215
  37.6 0.9 %collective-permute-done.10.far = f32[32,128]{1,0:T(8,128)S(1)} collective-permute-done((f32[32,128]{1,0:T(8,128)S(1)}, f32[32,128]{1,0:T(8,128)S(1)}, u32[]{:S(2)}, u32[]{:S(2)}) %collective-permute-start.10) | collective-permute-done | bytes 16416 | tf_op jit(solution)/shard_map/ppermute | solution.py:206
  38.5 0.0 collective-permute-start.13
  38.5 1.3 %collective-permute-done.13.refs_1_ = f32[2,128,128]{2,1,0:T(8,128)S(1)} collective-permute-done((f32[2,128,128]{2,1,0:T(8,128)S(1)}, f32[2,128,128]{2,1,0:T(8,128)S(1)}, u32[]{:S(2)}, u32[]{:S(2)}) %collective-permute-start.13) | collective-permute-done | bytes 131104 | tf_op jit(solution)/shard_map/ppermute | solution.py:212
  39.8 1.1 %shard_map.83 = (f32[128,512]{1,0:T(8,128)}, f32[1]{0:T(128)}) custom-call(f32[4,128,128]{2,1,0:T(8,128)S(1)} %get-tuple-element.18.valid, f32[32,128]{1,0:T(8,128)S(1)} %constant_dynamic-update-slice_fusion.near, f32[32,128]{1,0:T(8,128)S(1)} %collective-permute-done.10.far, f32[2,128,128]{2,1,0:T(8,128)S(1)} %add.19.refs_0_, ...), custom_call_target="tpu_custom_call" | custom-call | tf_op jit(solution)/shard_map/pallas_call | solution.py:276
  (9 shorter events, 0.1 us)
Async XLA Ops:
  0.6 17.0 %copy-start = (f32[4,128,128]{2,1,0:T(8,128)S(1)}, f32[4,128,128]{2,1,0:T(8,128)}, u32[]{:S(2)}) copy-start(f32[4,128,128]{2,1,0:T(8,128)} %refs_0_.3) | copy-start | bytes 786436
  0.6 12.5 %collective-permute-start = (f32[4,128,128]{2,1,0:T(8,128)}, f32[4,128,128]{2,1,0:T(8,128)S(1)}, u32[]{:S(2)}, u32[]{:S(2)}) collective-permute-start(f32[4,128,128]{2,1,0:T(8,128)} %refs_0_.3), channel_id=1, source_target_pairs={{0,12},{12,0},{4,8},{8,4},{1,13},{13,1},{5,9},{9,5},{2,14},{14,2},... | collective-permute-start | bytes 786440 | tf_op jit(solution)/shard_map/ppermute | solution.py:209
  5.8 13.5 %collective-permute-start.2 = (f32[4,128,128]{2,1,0:T(8,128)}, f32[4,128,128]{2,1,0:T(8,128)S(1)}, u32[]{:S(2)}, u32[]{:S(2)}) collective-permute-start(f32[4,128,128]{2,1,0:T(8,128)} %refs_0_.3), channel_id=1, source_target_pairs={{0,4},{4,0},{8,12},{12,8},{1,5},{5,1},{9,13},{13,9},{2,6},{6,2},{1... | collective-permute-start | bytes 786440 | tf_op jit(solution)/shard_map/ppermute | solution.py:203
  5.8 1.0 %copy-start.1 = (f32[128,512]{1,0:T(8,128)S(1)}, f32[128,512]{1,0:T(8,128)}, u32[]{:S(2)}) copy-start(f32[128,512]{1,0:T(8,128)} %wave.1) | copy-start | bytes 786436
  6.7 0.9 %copy-start.2 = (f32[4,128,128]{2,1,0:T(8,128)S(1)}, f32[4,128,128]{2,1,0:T(8,128)}, u32[]{:S(2)}) copy-start(f32[4,128,128]{2,1,0:T(8,128)} %left.1) | copy-start | bytes 786436
  7.7 0.7 %copy-start.3 = (s32[4,4]{1,0:T(4,128)S(1)}, s32[4,4]{1,0:T(4,128)}, u32[]{:S(2)}) copy-start(s32[4,4]{1,0:T(4,128)} %pairs.1) | copy-start | bytes 196
  8.3 0.7 %copy-start.4 = (s32[4]{0:T(128)S(1)}, s32[4]{0:T(128)}, u32[]{:S(2)}) copy-start(s32[4]{0:T(128)} %left_sizes.1) | copy-start | bytes 52
  9.0 0.7 %copy-start.5 = (s32[4]{0:T(128)S(1)}, s32[4]{0:T(128)}, u32[]{:S(2)}) copy-start(s32[4]{0:T(128)} %right_sizes.1) | copy-start | bytes 52
  13.2 10.4 %collective-permute-start.4 = (f32[4,128,128]{2,1,0:T(8,128)S(1)}, f32[4,128,128]{2,1,0:T(8,128)S(1)}, u32[]{:S(2)}, u32[]{:S(2)}) collective-permute-start(f32[4,128,128]{2,1,0:T(8,128)S(1)} %collective-permute-done.refs_1_.refs_2_), channel_id=1, source_target_pairs={{0,4},{4,0},{8,12},{12,8},{1,5},{5,1},{9,13},{13,9},{2,6},{6,2},{1... | collective-permute-start | bytes 786440 | tf_op jit(solution)/shard_map/ppermute | solution.py:203
  17.9 1.3 %collective-permute-start.1 = (f32[1,128,128]{2,1,0:T(8,128)S(1)}, f32[1,128,128]{2,1,0:T(8,128)S(1)}, u32[]{:S(2)}, u32[]{:S(2)}) collective-permute-start(f32[1,128,128]{2,1,0:T(8,128)S(1)} %shard_map.78), channel_id=1, source_target_pairs={{0,1},{1,0},{2,3},{3,2},{4,5},{5,4},{6,7},{7,6},{8,9},{9,8},{10,11... | collective-permute-start | bytes 196616 | tf_op jit(solution)/shard_map/ppermute | solution.py:212
  19.6 1.4 %collective-permute-start.3 = (f32[2,128,128]{2,1,0:T(8,128)S(1)}, f32[2,128,128]{2,1,0:T(8,128)S(1)}, u32[]{:S(2)}, u32[]{:S(2)}) collective-permute-start(f32[2,128,128]{2,1,0:T(8,128)S(1)} %shard_map.79), channel_id=1, source_target_pairs={{0,1},{1,0},{2,3},{3,2},{4,5},{5,4},{6,7},{7,6},{8,9},{9,8},{10,11... | collective-permute-start | bytes 393224 | tf_op jit(solution)/shard_map/ppermute | solution.py:212
  21.0 7.0 %collective-permute-start.8 = (f32[2,128,128]{2,1,0:T(8,128)S(1)}, f32[2,128,128]{2,1,0:T(8,128)S(1)}, u32[]{:S(2)}, u32[]{:S(2)}) collective-permute-start(f32[2,128,128]{2,1,0:T(8,128)S(1)} %add.16), channel_id=1, source_target_pairs={{0,2},{1,3},{2,0},{3,1},{4,6},{5,7},{6,4},{7,5},{8,10},{9,11},{10,... | collective-permute-start | bytes 393224 | tf_op jit(solution)/shard_map/ppermute | solution.py:215
  22.6 5.5 %collective-permute-start.7 = (f32[1,128,128]{2,1,0:T(8,128)S(1)}, f32[1,128,128]{2,1,0:T(8,128)S(1)}, u32[]{:S(2)}, u32[]{:S(2)}) collective-permute-start(f32[1,128,128]{2,1,0:T(8,128)S(1)} %add.15), channel_id=1, source_target_pairs={{0,2},{1,3},{2,0},{3,1},{4,6},{5,7},{6,4},{7,5},{8,10},{9,11},{10,... | collective-permute-start | bytes 196616 | tf_op jit(solution)/shard_map/ppermute | solution.py:215
  23.9 1.3 %collective-permute-start.5 = (f32[1,128,128]{2,1,0:T(8,128)S(1)}, f32[1,128,128]{2,1,0:T(8,128)S(1)}, u32[]{:S(2)}, u32[]{:S(2)}) collective-permute-start(f32[1,128,128]{2,1,0:T(8,128)S(1)} %shard_map.80), channel_id=1, source_target_pairs={{0,1},{1,0},{2,3},{3,2},{4,5},{5,4},{6,7},{7,6},{8,9},{9,8},{10,11... | collective-permute-start | bytes 196616 | tf_op jit(solution)/shard_map/ppermute | solution.py:212
  25.2 4.3 %collective-permute-start.6 = (f32[1,128,128]{2,1,0:T(8,128)S(1)}, f32[1,128,128]{2,1,0:T(8,128)S(1)}, u32[]{:S(2)}, u32[]{:S(2)}) collective-permute-start(f32[1,128,128]{2,1,0:T(8,128)S(1)} %add.17.own), channel_id=1, source_target_pairs={{0,2},{1,3},{2,0},{3,1},{4,6},{5,7},{6,4},{7,5},{8,10},{9,11},{10,... | collective-permute-start | bytes 196616 | tf_op jit(solution)/shard_map/ppermute | solution.py:215
  30.1 1.8 %collective-permute-start.11 = (f32[2,128,128]{2,1,0:T(8,128)S(1)}, f32[2,128,128]{2,1,0:T(8,128)S(1)}, u32[]{:S(2)}, u32[]{:S(2)}) collective-permute-start(f32[2,128,128]{2,1,0:T(8,128)S(1)} %get-tuple-element.30), channel_id=1, source_target_pairs={{0,1},{1,0},{2,3},{3,2},{4,5},{5,4},{6,7},{7,6},{8,9},{9,8},{10,11... | collective-permute-start | bytes 393224 | tf_op jit(solution)/shard_map/ppermute | solution.py:212
  30.1 3.7 %collective-permute-start.9 = (f32[16,128]{1,0:T(8,128)S(1)}, f32[16,128]{1,0:T(8,128)S(1)}, u32[]{:S(2)}, u32[]{:S(2)}) collective-permute-start(f32[16,128]{1,0:T(8,128)S(1)} %get-tuple-element.28), channel_id=1, source_target_pairs={{0,4},{4,0},{8,12},{12,8},{1,5},{5,1},{9,13},{13,9},{2,6},{6,2},{1... | collective-permute-start | bytes 24584 | tf_op jit(solution)/shard_map/ppermute | solution.py:203
  31.9 5.6 %collective-permute-start.12 = (f32[2,128,128]{2,1,0:T(8,128)S(1)}, f32[2,128,128]{2,1,0:T(8,128)S(1)}, u32[]{:S(2)}, u32[]{:S(2)}) collective-permute-start(f32[2,128,128]{2,1,0:T(8,128)S(1)} %add.18), channel_id=1, source_target_pairs={{0,2},{1,3},{2,0},{3,1},{4,6},{5,7},{6,4},{7,5},{8,10},{9,11},{10,... | collective-permute-start | bytes 393224 | tf_op jit(solution)/shard_map/ppermute | solution.py:215
  33.9 4.6 %collective-permute-start.10 = (f32[32,128]{1,0:T(8,128)S(1)}, f32[32,128]{1,0:T(8,128)S(1)}, u32[]{:S(2)}, u32[]{:S(2)}) collective-permute-start(f32[32,128]{1,0:T(8,128)S(1)} %constant_dynamic-update-slice_fusion.near), channel_id=1, source_target_pairs={{0,8},{8,0},{4,12},{12,4},{1,9},{9,1},{5,13},{13,5},{2,10},{10,2},... | collective-permute-start | bytes 49160 | tf_op jit(solution)/shard_map/ppermute | solution.py:206
  38.5 1.3 %collective-permute-start.13 = (f32[2,128,128]{2,1,0:T(8,128)S(1)}, f32[2,128,128]{2,1,0:T(8,128)S(1)}, u32[]{:S(2)}, u32[]{:S(2)}) collective-permute-start(f32[2,128,128]{2,1,0:T(8,128)S(1)} %add.19.refs_0_), channel_id=1, source_target_pairs={{0,1},{1,0},{2,3},{3,2},{4,5},{5,4},{6,7},{7,6},{8,9},{9,8},{10,11... | collective-permute-start | bytes 393224 | tf_op jit(solution)/shard_map/ppermute | solution.py:212

commit v4 on v3

--- a/solution.py
+++ b/solution.py
@@ -54,13 +54,17 @@
     return (row & col).astype(F32) * pairs[a, b].astype(F32)
 
 
-def call(body, outs, n_small, n_big):
+def call(body, outs, n_small, n_big, flops=None):
+    cost = None
+    if flops is not None:
+        cost = pl.CostEstimate(flops=flops, bytes_accessed=flops // 100, transcendentals=0)
     return pl.pallas_call(
         body,
         out_shape=outs,
         in_specs=[SMEM] * n_small + [VMEM] * n_big,
         out_specs=[VMEM] * len(outs),
         compiler_params=PARAMS,
+        cost_estimate=cost,
     )
 
 
@@ -158,35 +162,38 @@
     write_sums(slots, vector, image, sums, 3)
 
 
-def last_body(groups, cells, valid, near, far, *refs):
-    product, ritz = refs[-2:]
-    sector = lax.axis_index("sector")
-
+def scalar_body(groups, cells, near, far, scalars):
     def everyone(read):
         lanes = (read(near, 0) + read(near, 16)) + (read(far, 0) + read(far, 16))
         return jnp.sum(lanes)
 
     def every_group(row):
         return lambda s, at: sum(
-            s[at + row + 3 * g : at + row + 3 * g + 1, :] for g in range(len(groups))
+            s[at + row + 3 * g : at + row + 3 * g + 1, :] for g in range(groups)
         )
 
     value = everyone(every_group(0)) / (everyone(every_group(1)) + TINY)
 
     def rest_of(s, at):
         total = every_group(2)(s, at)
-        for row in range(at, at + 3 * len(groups), 3):
+        for row in range(at, at + 3 * groups, 3):
             c = s[row + 1 : row + 2, :]
             ratio = jnp.where(c > 0, s[row : row + 1, :] / jnp.where(c > 0, c, 1.0), 0.0)
             total += (ratio - value) * (ratio - value) * c
         return total
 
-    scale = 1.0 / jnp.sqrt(everyone(rest_of) / cells + TINY)
-    ritz[0] = value
-    total, others = refs[:2]
+    row = lax.broadcasted_iota(jnp.int32, scalars.shape, 0)
+    scalars[...] = jnp.where(row == 0, value, 1.0 / jnp.sqrt(everyone(rest_of) / cells + TINY))
+
+
+def last_body(groups, valid, scalars, total, others, *refs):
+    product, ritz = refs[-2:]
+    ritz[0] = scalars[0, 0]
+    sector = lax.axis_index("sector")
     me = lax.axis_index("mpo") % 2
     cols = total.shape[2]
-    for slots, image in zip(groups, refs[2:-2]):
+    value, scale = scalars[0:1, :], scalars[1:2, :]
+    for slots, image in zip(groups, refs[:-2]):
         for k, slot in enumerate(slots):
             b = slot_column(slot, sector)
             second = jnp.where(me == slot // 2, total[slot % 2], others[slot % 2])
@@ -271,15 +278,18 @@
     mine = keep + core(send)
     sums_near = jnp.concatenate([sums, near(sums)])
     sums_far = far(sums_near)
-    total = after(mine + across(mine), sums_far)
+    total = mine + across(mine)
     others = core(total)
+    (scalars,) = call(
+        functools.partial(scalar_body, 2, cells), [shape(8, cols)], 0, 2, flops=3_000_000_000
+    )(sums_near, sums_far)
     product, ritz = pl.pallas_call(
-        functools.partial(last_body, (EARLY, LATE), cells),
+        functools.partial(last_body, (EARLY, LATE)),
         out_shape=[shape(rows, sectors * cols), shape(1)],
-        in_specs=[VMEM] * 7,
+        in_specs=[VMEM] * 6,
         out_specs=[VMEM, SMEM],
         compiler_params=PARAMS,
-    )(valid, sums_near, sums_far, total, others, image_early, image_late)
+    )(valid, scalars, total, others, image_early, image_late)
     return product, ritz
 
 

time: 41.2 us -> 40 us (0.971)
  waiting for transfers between devices: 12.7 us -> 11.4 us
    ppermute x5, waiting for transfers between devices: 5 us -> 3.75 us  [core(): return lax.ppermute(x, 'mpo', [(0, 1), (1, 0), (2, 3), (3, 2)])]
    pallas_call x1 -> x2, Pallas kernels: 1.12 us -> 1.16 us  [the longest x1 0.79 us: line_device(): pl.pallas_call(functools.partial(last_body, (EARLY, LATE)), out_shape=[sh...]
  transfers between devices with their start and end apart: 14 -> 14, of which waited for: 11 -> 11; matrix products, arithmetic and copies ran while one was open for 0% -> 0% of each run, Pallas kernels for 7% -> 8%
where the time goes in v4:
time: 40 us; the launch traced here: 39.8 us
  starting transfers between devices  19.2 us (48%)
  waiting for transfers between devices  11.4 us (28%)
  Pallas kernels  4.46 us (11%)
  local copies, waits for them, and re-layouts  3.9 us (10%)
  between operations  0.77 us (2%)
    ppermute x3, starting transfers between devices, near(): return lax.ppermute(x, 'sector', [(0, 1), (1, 0), (2, 3), (3, 2)])  6.16 us
    ppermute x4, starting transfers between devices, across(): return lax.ppermute(x, 'mpo', [(0, 2), (1, 3), (2, 0), (3, 1)])  5.21 us
    ppermute x1, starting transfers between devices, mirror(): return lax.ppermute(x, 'sector', [(0, 3), (3, 0), (1, 2), (2, 1)])  5.11 us
    unnamed x13, local copies, waits for them, and re-layouts  3.9 us
    ppermute x5, waiting for transfers between devices, core(): return lax.ppermute(x, 'mpo', [(0, 1), (1, 0), (2, 3), (3, 2)])  3.75 us
    ppermute x4, waiting for transfers between devices, across(): return lax.ppermute(x, 'mpo', [(0, 2), (1, 3), (2, 0), (3, 1)])  3.46 us
    ppermute x1, waiting for transfers between devices, mirror(): return lax.ppermute(x, 'sector', [(0, 3), (3, 0), (1, 2), (2, 1)])  2.43 us
    ppermute x1, starting transfers between devices, far(): return lax.ppermute(x, 'sector', [(0, 2), (2, 0), (1, 3), (3, 1)])  2.18 us
  transfers between devices with their start and end apart: 14, of which 11 were waited for; matrix products, arithmetic and copies ran while one was open for 0% of the time, Pallas kernels for 8%

profile of v4, /device:TPU:0, one launch (start us, length us, event | category | flops | bytes accessed | tf_op | source)
XLA Modules:
  0.0 39.8 jit_solution(4159082648961160543)
XLA Ops:
  0.6 0.0 copy-start
  0.6 5.1 %collective-permute-start = (f32[4,128,128]{2,1,0:T(8,128)}, f32[4,128,128]{2,1,0:T(8,128)S(1)}, u32[]{:S(2)}, u32[]{:S(2)}) collective-permute-start(f32[4,128,128]{2,1,0:T(8,128)} %refs_0_.3), channel_id=1, source_target_pairs={{0,12},{12,0},{4,8},{8,4},{1,13},{13,1},{5,9},{9,5},{2,14},{14,2},... | collective-permute-start | bytes 786440 | tf_op jit(solution)/shard_map/ppermute | solution.py:216
  5.8 0.0 collective-permute-start.2
  5.8 0.0 copy-start.1
  5.8 0.9 %copy-done.1 = f32[128,512]{1,0:T(8,128)S(1)} copy-done((f32[128,512]{1,0:T(8,128)S(1)}, f32[128,512]{1,0:T(8,128)}, u32[]{:S(2)}) %copy-start.1) | copy-done | bytes 262168
  6.7 0.0 copy-start.2
  6.7 0.9 %copy-done.2 = f32[4,128,128]{2,1,0:T(8,128)S(1)} copy-done((f32[4,128,128]{2,1,0:T(8,128)S(1)}, f32[4,128,128]{2,1,0:T(8,128)}, u32[]{:S(2)}) %copy-start.2) | copy-done | bytes 262168
  7.7 0.0 copy-start.3
  7.7 0.7 %copy-done.3 = s32[4,4]{1,0:T(4,128)S(1)} copy-done((s32[4,4]{1,0:T(4,128)S(1)}, s32[4,4]{1,0:T(4,128)}, u32[]{:S(2)}) %copy-start.3) | copy-done | bytes 88
  8.3 0.0 copy-start.4
  8.3 0.7 %copy-done.4 = s32[4]{0:T(128)S(1)} copy-done((s32[4]{0:T(128)S(1)}, s32[4]{0:T(128)}, u32[]{:S(2)}) %copy-start.4) | copy-done | bytes 40
  9.0 0.0 copy-start.5
  9.0 0.7 %copy-done.5 = s32[4]{0:T(128)S(1)} copy-done((s32[4]{0:T(128)S(1)}, s32[4]{0:T(128)}, u32[]{:S(2)}) %copy-start.5) | copy-done | bytes 40
  9.7 1.1 %shard_map.77 = (f32[4,128,128]{2,1,0:T(8,128)S(1)}, f32[4,128,512]{2,1,0:T(8,128)S(1)}, bf16[512,384]{1,0:T(8,128)(2,1)S(1)}, f32[4,128,128]{2,1,0:T(8,128)S(1)}) custom-call(s32[4]{0:T(128)S(1)} %copy-done.4, s32[4]{0:T(128)S(1)} %copy-done.5, s32[4,4]{1,0:T(4,128)S(1)} %copy-done.3, f32[128,512]{1,0:T(8,128)S(1)} %copy-done.1, f32[4,128,128]{2,1,0:T(8,128)S(1)} %copy-done.2), custom_call_target="tpu_custom_call" | custom-call | tf_op jit(solution)/shard_map/pallas_call | solution.py:232
  10.8 2.4 %collective-permute-done.refs_1_.refs_2_ = f32[4,128,128]{2,1,0:T(8,128)S(1)} collective-permute-done((f32[4,128,128]{2,1,0:T(8,128)}, f32[4,128,128]{2,1,0:T(8,128)S(1)}, u32[]{:S(2)}, u32[]{:S(2)}) %collective-permute-start) | collective-permute-done | bytes 262176 | tf_op jit(solution)/shard_map/ppermute | solution.py:216
  13.2 4.4 %collective-permute-start.4 = (f32[4,128,128]{2,1,0:T(8,128)S(1)}, f32[4,128,128]{2,1,0:T(8,128)S(1)}, u32[]{:S(2)}, u32[]{:S(2)}) collective-permute-start(f32[4,128,128]{2,1,0:T(8,128)S(1)} %collective-permute-done.refs_1_.refs_2_), channel_id=1, source_target_pairs={{0,4},{4,0},{8,12},{12,8},{1,5},{5,1},{9,13},{13,9},{2,6},{6,2},{1... | collective-permute-start | bytes 786440 | tf_op jit(solution)/shard_map/ppermute | solution.py:210
  17.6 0.0 copy-done
  17.6 0.3 shard_map.78
  17.9 0.1 collective-permute-start.1
  18.0 1.2 %collective-permute-done.1 = f32[1,128,128]{2,1,0:T(8,128)S(1)} collective-permute-done((f32[1,128,128]{2,1,0:T(8,128)S(1)}, f32[1,128,128]{2,1,0:T(8,128)S(1)}, u32[]{:S(2)}, u32[]{:S(2)}) %collective-permute-start.1) | collective-permute-done | bytes 65568 | tf_op jit(solution)/shard_map/ppermute | solution.py:219
  19.2 0.0 collective-permute-done.2.refs_0_.refs_1_
  19.2 0.4 shard_map.79
  19.6 0.2 collective-permute-start.3
  19.8 1.2 %collective-permute-done.3 = f32[2,128,128]{2,1,0:T(8,128)S(1)} collective-permute-done((f32[2,128,128]{2,1,0:T(8,128)S(1)}, f32[2,128,128]{2,1,0:T(8,128)S(1)}, u32[]{:S(2)}, u32[]{:S(2)}) %collective-permute-start.3) | collective-permute-done | bytes 131104 | tf_op jit(solution)/shard_map/ppermute | solution.py:219
  21.0 1.6 %collective-permute-start.8 = (f32[2,128,128]{2,1,0:T(8,128)S(1)}, f32[2,128,128]{2,1,0:T(8,128)S(1)}, u32[]{:S(2)}, u32[]{:S(2)}) collective-permute-start(f32[2,128,128]{2,1,0:T(8,128)S(1)} %add.16), channel_id=1, source_target_pairs={{0,2},{1,3},{2,0},{3,1},{4,6},{5,7},{6,4},{7,5},{8,10},{9,11},{10,... | collective-permute-start | bytes 393224 | tf_op jit(solution)/shard_map/ppermute | solution.py:222
  22.6 0.5 %collective-permute-start.7 = (f32[1,128,128]{2,1,0:T(8,128)S(1)}, f32[1,128,128]{2,1,0:T(8,128)S(1)}, u32[]{:S(2)}, u32[]{:S(2)}) collective-permute-start(f32[1,128,128]{2,1,0:T(8,128)S(1)} %add.15), channel_id=1, source_target_pairs={{0,2},{1,3},{2,0},{3,1},{4,6},{5,7},{6,4},{7,5},{8,10},{9,11},{10,... | collective-permute-start | bytes 196616 | tf_op jit(solution)/shard_map/ppermute | solution.py:222
  23.1 0.5 %collective-permute-done.4.refs_0_ = f32[4,128,128]{2,1,0:T(8,128)S(1)} collective-permute-done((f32[4,128,128]{2,1,0:T(8,128)S(1)}, f32[4,128,128]{2,1,0:T(8,128)S(1)}, u32[]{:S(2)}, u32[]{:S(2)}) %collective-permute-start.4) | collective-permute-done | bytes 262176 | tf_op jit(solution)/shard_map/ppermute | solution.py:210
  23.6 0.3 shard_map.80
  23.9 0.1 collective-permute-start.5
  24.0 1.2 %collective-permute-done.5 = f32[1,128,128]{2,1,0:T(8,128)S(1)} collective-permute-done((f32[1,128,128]{2,1,0:T(8,128)S(1)}, f32[1,128,128]{2,1,0:T(8,128)S(1)}, u32[]{:S(2)}, u32[]{:S(2)}) %collective-permute-start.5) | collective-permute-done | bytes 65568 | tf_op jit(solution)/shard_map/ppermute | solution.py:219
  25.2 1.6 %collective-permute-start.6 = (f32[1,128,128]{2,1,0:T(8,128)S(1)}, f32[1,128,128]{2,1,0:T(8,128)S(1)}, u32[]{:S(2)}, u32[]{:S(2)}) collective-permute-start(f32[1,128,128]{2,1,0:T(8,128)S(1)} %add.17.own), channel_id=1, source_target_pairs={{0,2},{1,3},{2,0},{3,1},{4,6},{5,7},{6,4},{7,5},{8,10},{9,11},{10,... | collective-permute-start | bytes 196616 | tf_op jit(solution)/shard_map/ppermute | solution.py:222
  26.8 1.3 %collective-permute-done.7 = f32[1,128,128]{2,1,0:T(8,128)S(1)} collective-permute-done((f32[1,128,128]{2,1,0:T(8,128)S(1)}, f32[1,128,128]{2,1,0:T(8,128)S(1)}, u32[]{:S(2)}, u32[]{:S(2)}) %collective-permute-start.7) | collective-permute-done | bytes 65568 | tf_op jit(solution)/shard_map/ppermute | solution.py:222
  28.0 0.0 collective-permute-done.8
  28.1 0.8 %shard_map.81 = (f32[3,128,128]{2,1,0:T(8,128)S(1)}, f32[3,128,128]{2,1,0:T(8,128)S(1)}, f32[16,128]{1,0:T(8,128)S(1)}) custom-call(f32[3,128,128]{2,1,0:T(8,128)S(1)} %pad_maximum_fusion.own, f32[3,128,128]{2,1,0:T(8,128)S(1)} %pad_maximum_fusion.1.other, f32[4,128,128]{2,1,0:T(8,128)S(1)} %get-tuple-element.17.valid, ...), custom_call_target="tpu_custom_call" | custom-call | tf_op jit(solution)/shard_map/pallas_call | solution.py:256
  28.9 0.7 %collective-permute-done.6.other = f32[1,128,128]{2,1,0:T(8,128)S(1)} collective-permute-done((f32[1,128,128]{2,1,0:T(8,128)S(1)}, f32[1,128,128]{2,1,0:T(8,128)S(1)}, u32[]{:S(2)}, u32[]{:S(2)}) %collective-permute-start.6) | collective-permute-done | bytes 65568 | tf_op jit(solution)/shard_map/ppermute | solution.py:222
  29.5 0.5 %shard_map.82 = (f32[1,128,128]{2,1,0:T(8,128)S(1)}, f32[2,128,128]{2,1,0:T(8,128)S(1)}, f32[2,128,128]{2,1,0:T(8,128)S(1)}, f32[16,128]{1,0:T(8,128)S(1)}) custom-call(f32[1,128,128]{2,1,0:T(8,128)S(1)} %add.17.own, f32[1,128,128]{2,1,0:T(8,128)S(1)} %collective-permute-done.6.other, f32[4,128,128]{2,1,0:T(8,128)S(1)} %get-tuple-element.17.valid, ...), custom_call_target="tpu_custom_call" | custom-call | tf_op jit(solution)/shard_map/pallas_call | solution.py:271
  30.1 0.1 collective-permute-start.11
  30.1 1.7 %collective-permute-start.9 = (f32[16,128]{1,0:T(8,128)S(1)}, f32[16,128]{1,0:T(8,128)S(1)}, u32[]{:S(2)}, u32[]{:S(2)}) collective-permute-start(f32[16,128]{1,0:T(8,128)S(1)} %get-tuple-element.27), channel_id=1, source_target_pairs={{0,4},{4,0},{8,12},{12,8},{1,5},{5,1},{9,13},{13,9},{2,6},{6,2},{1... | collective-permute-start | bytes 24584 | tf_op jit(solution)/shard_map/ppermute | solution.py:210
  31.9 0.0 collective-permute-done.11
  31.9 1.6 %collective-permute-start.12 = (f32[2,128,128]{2,1,0:T(8,128)S(1)}, f32[2,128,128]{2,1,0:T(8,128)S(1)}, u32[]{:S(2)}, u32[]{:S(2)}) collective-permute-start(f32[2,128,128]{2,1,0:T(8,128)S(1)} %add.18), channel_id=1, source_target_pairs={{0,2},{1,3},{2,0},{3,1},{4,6},{5,7},{6,4},{7,5},{8,10},{9,11},{10,... | collective-permute-start | bytes 393224 | tf_op jit(solution)/shard_map/ppermute | solution.py:222
  33.5 0.4 collective-permute-done.9
  33.9 2.2 %collective-permute-start.10 = (f32[32,128]{1,0:T(8,128)S(1)}, f32[32,128]{1,0:T(8,128)S(1)}, u32[]{:S(2)}, u32[]{:S(2)}) collective-permute-start(f32[32,128]{1,0:T(8,128)S(1)} %constant_dynamic-update-slice_fusion.near), channel_id=1, source_target_pairs={{0,8},{8,0},{4,12},{12,4},{1,9},{9,1},{5,13},{13,5},{2,10},{10,2},... | collective-permute-start | bytes 49160 | tf_op jit(solution)/shard_map/ppermute | solution.py:213
  36.0 1.5 %collective-permute-done.12 = f32[2,128,128]{2,1,0:T(8,128)S(1)} collective-permute-done((f32[2,128,128]{2,1,0:T(8,128)S(1)}, f32[2,128,128]{2,1,0:T(8,128)S(1)}, u32[]{:S(2)}, u32[]{:S(2)}) %collective-permute-start.12) | collective-permute-done | bytes 131104 | tf_op jit(solution)/shard_map/ppermute | solution.py:222
  37.6 0.1 collective-permute-start.13
  37.6 0.9 %collective-permute-done.10.far = f32[32,128]{1,0:T(8,128)S(1)} collective-permute-done((f32[32,128]{1,0:T(8,128)S(1)}, f32[32,128]{1,0:T(8,128)S(1)}, u32[]{:S(2)}, u32[]{:S(2)}) %collective-permute-start.10) | collective-permute-done | bytes 16416 | tf_op jit(solution)/shard_map/ppermute | solution.py:213
  38.5 0.4 shard_map.83.scalars
  38.9 0.1 collective-permute-done.13.others
  39.0 0.8 %shard_map.84 = (f32[128,512]{1,0:T(8,128)}, f32[1]{0:T(128)}) custom-call(f32[4,128,128]{2,1,0:T(8,128)S(1)} %get-tuple-element.17.valid, f32[8,128]{1,0:T(8,128)S(1)} %shard_map.83.scalars, f32[2,128,128]{2,1,0:T(8,128)S(1)} %add.19.total, f32[2,128,128]{2,1,0:T(8,128)S(1)} %collective-permute-done.13.others, ...), custom_call_target="tpu_custom_call" | custom-call | tf_op jit(solution)/shard_map/pallas_call | solution.py:286
  (9 shorter events, 0.1 us)
Async XLA Ops:
  0.6 17.0 %copy-start = (f32[4,128,128]{2,1,0:T(8,128)S(1)}, f32[4,128,128]{2,1,0:T(8,128)}, u32[]{:S(2)}) copy-start(f32[4,128,128]{2,1,0:T(8,128)} %refs_0_.3) | copy-start | bytes 786436
  0.6 12.5 %collective-permute-start = (f32[4,128,128]{2,1,0:T(8,128)}, f32[4,128,128]{2,1,0:T(8,128)S(1)}, u32[]{:S(2)}, u32[]{:S(2)}) collective-permute-start(f32[4,128,128]{2,1,0:T(8,128)} %refs_0_.3), channel_id=1, source_target_pairs={{0,12},{12,0},{4,8},{8,4},{1,13},{13,1},{5,9},{9,5},{2,14},{14,2},... | collective-permute-start | bytes 786440 | tf_op jit(solution)/shard_map/ppermute | solution.py:216
  5.8 13.5 %collective-permute-start.2 = (f32[4,128,128]{2,1,0:T(8,128)}, f32[4,128,128]{2,1,0:T(8,128)S(1)}, u32[]{:S(2)}, u32[]{:S(2)}) collective-permute-start(f32[4,128,128]{2,1,0:T(8,128)} %refs_0_.3), channel_id=1, source_target_pairs={{0,4},{4,0},{8,12},{12,8},{1,5},{5,1},{9,13},{13,9},{2,6},{6,2},{1... | collective-permute-start | bytes 786440 | tf_op jit(solution)/shard_map/ppermute | solution.py:210
  5.8 1.0 %copy-start.1 = (f32[128,512]{1,0:T(8,128)S(1)}, f32[128,512]{1,0:T(8,128)}, u32[]{:S(2)}) copy-start(f32[128,512]{1,0:T(8,128)} %wave.1) | copy-start | bytes 786436
  6.7 0.9 %copy-start.2 = (f32[4,128,128]{2,1,0:T(8,128)S(1)}, f32[4,128,128]{2,1,0:T(8,128)}, u32[]{:S(2)}) copy-start(f32[4,128,128]{2,1,0:T(8,128)} %left.1) | copy-start | bytes 786436
  7.7 0.7 %copy-start.3 = (s32[4,4]{1,0:T(4,128)S(1)}, s32[4,4]{1,0:T(4,128)}, u32[]{:S(2)}) copy-start(s32[4,4]{1,0:T(4,128)} %pairs.1) | copy-start | bytes 196
  8.3 0.7 %copy-start.4 = (s32[4]{0:T(128)S(1)}, s32[4]{0:T(128)}, u32[]{:S(2)}) copy-start(s32[4]{0:T(128)} %left_sizes.1) | copy-start | bytes 52
  9.0 0.7 %copy-start.5 = (s32[4]{0:T(128)S(1)}, s32[4]{0:T(128)}, u32[]{:S(2)}) copy-start(s32[4]{0:T(128)} %right_sizes.1) | copy-start | bytes 52
  13.2 10.4 %collective-permute-start.4 = (f32[4,128,128]{2,1,0:T(8,128)S(1)}, f32[4,128,128]{2,1,0:T(8,128)S(1)}, u32[]{:S(2)}, u32[]{:S(2)}) collective-permute-start(f32[4,128,128]{2,1,0:T(8,128)S(1)} %collective-permute-done.refs_1_.refs_2_), channel_id=1, source_target_pairs={{0,4},{4,0},{8,12},{12,8},{1,5},{5,1},{9,13},{13,9},{2,6},{6,2},{1... | collective-permute-start | bytes 786440 | tf_op jit(solution)/shard_map/ppermute | solution.py:210
  17.9 1.3 %collective-permute-start.1 = (f32[1,128,128]{2,1,0:T(8,128)S(1)}, f32[1,128,128]{2,1,0:T(8,128)S(1)}, u32[]{:S(2)}, u32[]{:S(2)}) collective-permute-start(f32[1,128,128]{2,1,0:T(8,128)S(1)} %shard_map.78), channel_id=1, source_target_pairs={{0,1},{1,0},{2,3},{3,2},{4,5},{5,4},{6,7},{7,6},{8,9},{9,8},{10,11... | collective-permute-start | bytes 196616 | tf_op jit(solution)/shard_map/ppermute | solution.py:219
  19.6 1.4 %collective-permute-start.3 = (f32[2,128,128]{2,1,0:T(8,128)S(1)}, f32[2,128,128]{2,1,0:T(8,128)S(1)}, u32[]{:S(2)}, u32[]{:S(2)}) collective-permute-start(f32[2,128,128]{2,1,0:T(8,128)S(1)} %shard_map.79), channel_id=1, source_target_pairs={{0,1},{1,0},{2,3},{3,2},{4,5},{5,4},{6,7},{7,6},{8,9},{9,8},{10,11... | collective-permute-start | bytes 393224 | tf_op jit(solution)/shard_map/ppermute | solution.py:219
  21.0 7.0 %collective-permute-start.8 = (f32[2,128,128]{2,1,0:T(8,128)S(1)}, f32[2,128,128]{2,1,0:T(8,128)S(1)}, u32[]{:S(2)}, u32[]{:S(2)}) collective-permute-start(f32[2,128,128]{2,1,0:T(8,128)S(1)} %add.16), channel_id=1, source_target_pairs={{0,2},{1,3},{2,0},{3,1},{4,6},{5,7},{6,4},{7,5},{8,10},{9,11},{10,... | collective-permute-start | bytes 393224 | tf_op jit(solution)/shard_map/ppermute | solution.py:222
  22.6 5.5 %collective-permute-start.7 = (f32[1,128,128]{2,1,0:T(8,128)S(1)}, f32[1,128,128]{2,1,0:T(8,128)S(1)}, u32[]{:S(2)}, u32[]{:S(2)}) collective-permute-start(f32[1,128,128]{2,1,0:T(8,128)S(1)} %add.15), channel_id=1, source_target_pairs={{0,2},{1,3},{2,0},{3,1},{4,6},{5,7},{6,4},{7,5},{8,10},{9,11},{10,... | collective-permute-start | bytes 196616 | tf_op jit(solution)/shard_map/ppermute | solution.py:222
  23.9 1.3 %collective-permute-start.5 = (f32[1,128,128]{2,1,0:T(8,128)S(1)}, f32[1,128,128]{2,1,0:T(8,128)S(1)}, u32[]{:S(2)}, u32[]{:S(2)}) collective-permute-start(f32[1,128,128]{2,1,0:T(8,128)S(1)} %shard_map.80), channel_id=1, source_target_pairs={{0,1},{1,0},{2,3},{3,2},{4,5},{5,4},{6,7},{7,6},{8,9},{9,8},{10,11... | collective-permute-start | bytes 196616 | tf_op jit(solution)/shard_map/ppermute | solution.py:219
  25.2 4.3 %collective-permute-start.6 = (f32[1,128,128]{2,1,0:T(8,128)S(1)}, f32[1,128,128]{2,1,0:T(8,128)S(1)}, u32[]{:S(2)}, u32[]{:S(2)}) collective-permute-start(f32[1,128,128]{2,1,0:T(8,128)S(1)} %add.17.own), channel_id=1, source_target_pairs={{0,2},{1,3},{2,0},{3,1},{4,6},{5,7},{6,4},{7,5},{8,10},{9,11},{10,... | collective-permute-start | bytes 196616 | tf_op jit(solution)/shard_map/ppermute | solution.py:222
  30.1 1.8 %collective-permute-start.11 = (f32[2,128,128]{2,1,0:T(8,128)S(1)}, f32[2,128,128]{2,1,0:T(8,128)S(1)}, u32[]{:S(2)}, u32[]{:S(2)}) collective-permute-start(f32[2,128,128]{2,1,0:T(8,128)S(1)} %get-tuple-element.29), channel_id=1, source_target_pairs={{0,1},{1,0},{2,3},{3,2},{4,5},{5,4},{6,7},{7,6},{8,9},{9,8},{10,11... | collective-permute-start | bytes 393224 | tf_op jit(solution)/shard_map/ppermute | solution.py:219
  30.1 3.7 %collective-permute-start.9 = (f32[16,128]{1,0:T(8,128)S(1)}, f32[16,128]{1,0:T(8,128)S(1)}, u32[]{:S(2)}, u32[]{:S(2)}) collective-permute-start(f32[16,128]{1,0:T(8,128)S(1)} %get-tuple-element.27), channel_id=1, source_target_pairs={{0,4},{4,0},{8,12},{12,8},{1,5},{5,1},{9,13},{13,9},{2,6},{6,2},{1... | collective-permute-start | bytes 24584 | tf_op jit(solution)/shard_map/ppermute | solution.py:210
  31.9 5.6 %collective-permute-start.12 = (f32[2,128,128]{2,1,0:T(8,128)S(1)}, f32[2,128,128]{2,1,0:T(8,128)S(1)}, u32[]{:S(2)}, u32[]{:S(2)}) collective-permute-start(f32[2,128,128]{2,1,0:T(8,128)S(1)} %add.18), channel_id=1, source_target_pairs={{0,2},{1,3},{2,0},{3,1},{4,6},{5,7},{6,4},{7,5},{8,10},{9,11},{10,... | collective-permute-start | bytes 393224 | tf_op jit(solution)/shard_map/ppermute | solution.py:222
  33.9 4.6 %collective-permute-start.10 = (f32[32,128]{1,0:T(8,128)S(1)}, f32[32,128]{1,0:T(8,128)S(1)}, u32[]{:S(2)}, u32[]{:S(2)}) collective-permute-start(f32[32,128]{1,0:T(8,128)S(1)} %constant_dynamic-update-slice_fusion.near), channel_id=1, source_target_pairs={{0,8},{8,0},{4,12},{12,4},{1,9},{9,1},{5,13},{13,5},{2,10},{10,2},... | collective-permute-start | bytes 49160 | tf_op jit(solution)/shard_map/ppermute | solution.py:213
  37.6 1.4 %collective-permute-start.13 = (f32[2,128,128]{2,1,0:T(8,128)S(1)}, f32[2,128,128]{2,1,0:T(8,128)S(1)}, u32[]{:S(2)}, u32[]{:S(2)}) collective-permute-start(f32[2,128,128]{2,1,0:T(8,128)S(1)} %add.19.total), channel_id=1, source_target_pairs={{0,1},{1,0},{2,3},{3,2},{4,5},{5,4},{6,7},{7,6},{8,9},{9,8},{10,11... | collective-permute-start | bytes 393224 | tf_op jit(solution)/shard_map/ppermute | solution.py:219

commit v5 on v4

--- a/solution.py
+++ b/solution.py
@@ -23,18 +23,16 @@
     return high, (x - high.astype(F32)).astype(BF16)
 
 
-def left_terms(x):
-    high, low = split(x)
-    return jnp.concatenate([high, high, low], axis=1)
-
-
-def right_terms(x):
-    high, low = split(x)
-    return jnp.concatenate([high, low, high], axis=0)
-
-
-def times(a, b):
-    return lax.dot_general(a, b, (((1,), (0,)), ((), ())), preferred_element_type=F32)
+def times(a, x):
+    n = x.shape[1]
+    parts = jnp.concatenate(split(x), axis=1)
+    both = lax.dot_general(
+        a,
+        jnp.concatenate([parts, parts], axis=0),
+        (((1,), (0,)), ((), ())),
+        preferred_element_type=F32,
+    )
+    return both[:, n:] + both[:, :n]
 
 
 def times_turned(a, b):
@@ -85,12 +83,12 @@
     channels, rows, _ = left.shape
     slots, _, inner = halfway.shape
     cols = inner // channels
-    factors[...] = left_terms(left[...].reshape(channels * rows, rows))
+    factors[...] = jnp.concatenate(split(left[...].reshape(channels * rows, rows)), axis=1)
     for k in range(slots):
         b = slot_column(k, sector)
         valid[k] = block_valid(left_sizes, right_sizes, pairs, sector, b, rows, cols)
         vector[k] = wave[:, columns(b, cols)] * valid[k]
-    part = times(factors[...], right_terms(channel_row(vector)))
+    part = times(factors[...], channel_row(vector))
     for k in range(slots):
         for w in range(channels):
             halfway[k, :, w * cols : (w + 1) * cols] = part[
@@ -109,7 +107,7 @@
     channels = factors.shape[0] // rows
     for k, slot in enumerate(slots):
         image[k] = (own[k] + other[k]) * valid[slot]
-    half = times(factors[...], right_terms(channel_row(image)))
+    half = times(factors[...], channel_row(image))
     partials = []
     for k in range(len(slots)):
         here = half[:, k * cols : (k + 1) * cols].reshape(channels, rows, cols)
@@ -164,15 +162,16 @@
 
 def scalar_body(groups, cells, near, far, scalars):
     def everyone(read):
-        lanes = (read(near, 0) + read(near, 16)) + (read(far, 0) + read(far, 16))
-        return jnp.sum(lanes)
+        lanes = (read(near, 0) + read(near, 8)) + (read(far, 0) + read(far, 8))
+        return jnp.sum(lanes, axis=1, keepdims=True)
 
     def every_group(row):
         return lambda s, at: sum(
             s[at + row + 3 * g : at + row + 3 * g + 1, :] for g in range(groups)
         )
 
-    value = everyone(every_group(0)) / (everyone(every_group(1)) + TINY)
+    both = everyone(lambda s, at: s[at : at + 2, :] + s[at + 3 : at + 5, :])
+    value = both[0:1, :] / (both[1:2, :] + TINY)
 
     def rest_of(s, at):
         total = every_group(2)(s, at)
@@ -182,8 +181,9 @@
             total += (ratio - value) * (ratio - value) * c
         return total
 
-    row = lax.broadcasted_iota(jnp.int32, scalars.shape, 0)
-    scalars[...] = jnp.where(row == 0, value, 1.0 / jnp.sqrt(everyone(rest_of) / cells + TINY))
+    scale = 1.0 / jnp.sqrt(everyone(rest_of) / cells + TINY)
+    scalars[0:1, :] = jnp.broadcast_to(value, (1, scalars.shape[1]))
+    scalars[1:2, :] = jnp.broadcast_to(scale, (1, scalars.shape[1]))
 
 
 def last_body(groups, valid, scalars, total, others, *refs):
@@ -234,7 +234,7 @@
         [
             shape(sectors, rows, cols),
             shape(sectors, rows, channels * cols),
-            shape(channels * rows, 3 * rows, of=BF16),
+            shape(channels * rows, 2 * rows, of=BF16),
             shape(sectors, rows, cols),
         ],
         3,
@@ -255,7 +255,7 @@
     three = chip_sum(partials((3,), after(halfway, two), right_far))
     image_early, second_early, sums = call(
         functools.partial(early_body, EARLY),
-        [shape(3, rows, cols), shape(3, rows, cols), shape(16, cols)],
+        [shape(3, rows, cols), shape(3, rows, cols), shape(8, cols)],
         0,
         8,
     )(
@@ -270,7 +270,7 @@
     )
     image_late, keep, send, sums = call(
         functools.partial(late_body, EARLY, LATE),
-        [shape(1, rows, cols), shape(2, rows, cols), shape(2, rows, cols), shape(16, cols)],
+        [shape(1, rows, cols), shape(2, rows, cols), shape(2, rows, cols), shape(8, cols)],
         0,
         8,
     )(three, across(three), valid, factors, vector, sums, second_early, right_far)

time: 40 us -> 40 us (level)
  transfers between devices with their start and end apart: 14 -> 14, of which waited for: 11 -> 11; matrix products, arithmetic and copies ran while one was open for 0% -> 0% of each run, Pallas kernels for 8% -> 7%
where the time goes in v5:
time: 40 us; the launch traced here: 39.8 us
  starting transfers between devices  19.2 us (48%)
  waiting for transfers between devices  11.7 us (29%)
  Pallas kernels  4.19 us (10%)
  local copies, waits for them, and re-layouts  3.9 us (10%)
  between operations  0.75 us (2%)
    ppermute x3, starting transfers between devices, near(): return lax.ppermute(x, 'sector', [(0, 1), (1, 0), (2, 3), (3, 2)])  6.16 us
    ppermute x4, starting transfers between devices, across(): return lax.ppermute(x, 'mpo', [(0, 2), (1, 3), (2, 0), (3, 1)])  5.2 us
    ppermute x1, starting transfers between devices, mirror(): return lax.ppermute(x, 'sector', [(0, 3), (3, 0), (1, 2), (2, 1)])  5.11 us
    ppermute x5, waiting for transfers between devices, core(): return lax.ppermute(x, 'mpo', [(0, 1), (1, 0), (2, 3), (3, 2)])  4.01 us
    unnamed x13, local copies, waits for them, and re-layouts  3.9 us
    ppermute x4, waiting for transfers between devices, across(): return lax.ppermute(x, 'mpo', [(0, 2), (1, 3), (2, 0), (3, 1)])  3.64 us
    ppermute x1, waiting for transfers between devices, mirror(): return lax.ppermute(x, 'sector', [(0, 3), (3, 0), (1, 2), (2, 1)])  2.44 us
    ppermute x1, starting transfers between devices, far(): return lax.ppermute(x, 'sector', [(0, 2), (2, 0), (1, 3), (3, 1)])  2.18 us
  transfers between devices with their start and end apart: 14, of which 11 were waited for; matrix products, arithmetic and copies ran while one was open for 0% of the time, Pallas kernels for 7%

profile of v5, /device:TPU:0, one launch (start us, length us, event | category | flops | bytes accessed | tf_op | source)
XLA Modules:
  0.0 39.8 jit_solution(7397447027199363483)
XLA Ops:
  0.6 0.0 copy-start
  0.6 5.1 %collective-permute-start = (f32[4,128,128]{2,1,0:T(8,128)}, f32[4,128,128]{2,1,0:T(8,128)S(1)}, u32[]{:S(2)}, u32[]{:S(2)}) collective-permute-start(f32[4,128,128]{2,1,0:T(8,128)} %refs_0_.3), channel_id=1, source_target_pairs={{0,12},{12,0},{4,8},{8,4},{1,13},{13,1},{5,9},{9,5},{2,14},{14,2},... | collective-permute-start | bytes 786440 | tf_op jit(solution)/shard_map/ppermute | solution.py:216
  5.8 0.0 collective-permute-start.2
  5.8 0.0 copy-start.1
  5.8 0.9 %copy-done.1 = f32[128,512]{1,0:T(8,128)S(1)} copy-done((f32[128,512]{1,0:T(8,128)S(1)}, f32[128,512]{1,0:T(8,128)}, u32[]{:S(2)}) %copy-start.1) | copy-done | bytes 262168
  6.7 0.0 copy-start.2
  6.7 0.9 %copy-done.2 = f32[4,128,128]{2,1,0:T(8,128)S(1)} copy-done((f32[4,128,128]{2,1,0:T(8,128)S(1)}, f32[4,128,128]{2,1,0:T(8,128)}, u32[]{:S(2)}) %copy-start.2) | copy-done | bytes 262168
  7.7 0.0 copy-start.3
  7.7 0.7 %copy-done.3 = s32[4,4]{1,0:T(4,128)S(1)} copy-done((s32[4,4]{1,0:T(4,128)S(1)}, s32[4,4]{1,0:T(4,128)}, u32[]{:S(2)}) %copy-start.3) | copy-done | bytes 88
  8.3 0.0 copy-start.4
  8.3 0.7 %copy-done.4 = s32[4]{0:T(128)S(1)} copy-done((s32[4]{0:T(128)S(1)}, s32[4]{0:T(128)}, u32[]{:S(2)}) %copy-start.4) | copy-done | bytes 40
  9.0 0.0 copy-start.5
  9.0 0.7 %copy-done.5 = s32[4]{0:T(128)S(1)} copy-done((s32[4]{0:T(128)S(1)}, s32[4]{0:T(128)}, u32[]{:S(2)}) %copy-start.5) | copy-done | bytes 40
  9.7 1.1 %shard_map.77 = (f32[4,128,128]{2,1,0:T(8,128)S(1)}, f32[4,128,512]{2,1,0:T(8,128)S(1)}, bf16[512,256]{1,0:T(8,128)(2,1)S(1)}, f32[4,128,128]{2,1,0:T(8,128)S(1)}) custom-call(s32[4]{0:T(128)S(1)} %copy-done.4, s32[4]{0:T(128)S(1)} %copy-done.5, s32[4,4]{1,0:T(4,128)S(1)} %copy-done.3, f32[128,512]{1,0:T(8,128)S(1)} %copy-done.1, f32[4,128,128]{2,1,0:T(8,128)S(1)} %copy-done.2), custom_call_target="tpu_custom_call" | custom-call | tf_op jit(solution)/shard_map/pallas_call | solution.py:232
  10.7 2.4 %collective-permute-done.refs_1_.refs_2_ = f32[4,128,128]{2,1,0:T(8,128)S(1)} collective-permute-done((f32[4,128,128]{2,1,0:T(8,128)}, f32[4,128,128]{2,1,0:T(8,128)S(1)}, u32[]{:S(2)}, u32[]{:S(2)}) %collective-permute-start) | collective-permute-done | bytes 262176 | tf_op jit(solution)/shard_map/ppermute | solution.py:216
  13.2 4.4 %collective-permute-start.4 = (f32[4,128,128]{2,1,0:T(8,128)S(1)}, f32[4,128,128]{2,1,0:T(8,128)S(1)}, u32[]{:S(2)}, u32[]{:S(2)}) collective-permute-start(f32[4,128,128]{2,1,0:T(8,128)S(1)} %collective-permute-done.refs_1_.refs_2_), channel_id=1, source_target_pairs={{0,4},{4,0},{8,12},{12,8},{1,5},{5,1},{9,13},{13,9},{2,6},{6,2},{1... | collective-permute-start | bytes 786440 | tf_op jit(solution)/shard_map/ppermute | solution.py:210
  17.6 0.0 copy-done
  17.6 0.3 shard_map.78
  17.9 0.1 collective-permute-start.1
  18.0 1.2 %collective-permute-done.1 = f32[1,128,128]{2,1,0:T(8,128)S(1)} collective-permute-done((f32[1,128,128]{2,1,0:T(8,128)S(1)}, f32[1,128,128]{2,1,0:T(8,128)S(1)}, u32[]{:S(2)}, u32[]{:S(2)}) %collective-permute-start.1) | collective-permute-done | bytes 65568 | tf_op jit(solution)/shard_map/ppermute | solution.py:219
  19.2 0.0 collective-permute-done.2.refs_0_.refs_1_
  19.2 0.4 shard_map.79
  19.6 0.2 collective-permute-start.3
  19.8 1.2 %collective-permute-done.3 = f32[2,128,128]{2,1,0:T(8,128)S(1)} collective-permute-done((f32[2,128,128]{2,1,0:T(8,128)S(1)}, f32[2,128,128]{2,1,0:T(8,128)S(1)}, u32[]{:S(2)}, u32[]{:S(2)}) %collective-permute-start.3) | collective-permute-done | bytes 131104 | tf_op jit(solution)/shard_map/ppermute | solution.py:219
  21.0 1.6 %collective-permute-start.8 = (f32[2,128,128]{2,1,0:T(8,128)S(1)}, f32[2,128,128]{2,1,0:T(8,128)S(1)}, u32[]{:S(2)}, u32[]{:S(2)}) collective-permute-start(f32[2,128,128]{2,1,0:T(8,128)S(1)} %add.16), channel_id=1, source_target_pairs={{0,2},{1,3},{2,0},{3,1},{4,6},{5,7},{6,4},{7,5},{8,10},{9,11},{10,... | collective-permute-start | bytes 393224 | tf_op jit(solution)/shard_map/ppermute | solution.py:222
  22.6 0.5 %collective-permute-start.7 = (f32[1,128,128]{2,1,0:T(8,128)S(1)}, f32[1,128,128]{2,1,0:T(8,128)S(1)}, u32[]{:S(2)}, u32[]{:S(2)}) collective-permute-start(f32[1,128,128]{2,1,0:T(8,128)S(1)} %add.15), channel_id=1, source_target_pairs={{0,2},{1,3},{2,0},{3,1},{4,6},{5,7},{6,4},{7,5},{8,10},{9,11},{10,... | collective-permute-start | bytes 196616 | tf_op jit(solution)/shard_map/ppermute | solution.py:222
  23.1 0.5 %collective-permute-done.4.refs_0_ = f32[4,128,128]{2,1,0:T(8,128)S(1)} collective-permute-done((f32[4,128,128]{2,1,0:T(8,128)S(1)}, f32[4,128,128]{2,1,0:T(8,128)S(1)}, u32[]{:S(2)}, u32[]{:S(2)}) %collective-permute-start.4) | collective-permute-done | bytes 262176 | tf_op jit(solution)/shard_map/ppermute | solution.py:210
  23.6 0.3 shard_map.80
  23.9 0.1 collective-permute-start.5
  24.0 1.2 %collective-permute-done.5 = f32[1,128,128]{2,1,0:T(8,128)S(1)} collective-permute-done((f32[1,128,128]{2,1,0:T(8,128)S(1)}, f32[1,128,128]{2,1,0:T(8,128)S(1)}, u32[]{:S(2)}, u32[]{:S(2)}) %collective-permute-start.5) | collective-permute-done | bytes 65568 | tf_op jit(solution)/shard_map/ppermute | solution.py:219
  25.2 1.6 %collective-permute-start.6 = (f32[1,128,128]{2,1,0:T(8,128)S(1)}, f32[1,128,128]{2,1,0:T(8,128)S(1)}, u32[]{:S(2)}, u32[]{:S(2)}) collective-permute-start(f32[1,128,128]{2,1,0:T(8,128)S(1)} %add.17.own), channel_id=1, source_target_pairs={{0,2},{1,3},{2,0},{3,1},{4,6},{5,7},{6,4},{7,5},{8,10},{9,11},{10,... | collective-permute-start | bytes 196616 | tf_op jit(solution)/shard_map/ppermute | solution.py:222
  26.8 1.3 %collective-permute-done.7 = f32[1,128,128]{2,1,0:T(8,128)S(1)} collective-permute-done((f32[1,128,128]{2,1,0:T(8,128)S(1)}, f32[1,128,128]{2,1,0:T(8,128)S(1)}, u32[]{:S(2)}, u32[]{:S(2)}) %collective-permute-start.7) | collective-permute-done | bytes 65568 | tf_op jit(solution)/shard_map/ppermute | solution.py:222
  28.0 0.0 collective-permute-done.8
  28.1 0.7 %shard_map.81 = (f32[3,128,128]{2,1,0:T(8,128)S(1)}, f32[3,128,128]{2,1,0:T(8,128)S(1)}, f32[8,128]{1,0:T(8,128)S(1)}) custom-call(f32[3,128,128]{2,1,0:T(8,128)S(1)} %pad_maximum_fusion.own, f32[3,128,128]{2,1,0:T(8,128)S(1)} %pad_maximum_fusion.1.other, f32[4,128,128]{2,1,0:T(8,128)S(1)} %get-tuple-element.17.valid, ...), custom_call_target="tpu_custom_call" | custom-call | tf_op jit(solution)/shard_map/pallas_call | solution.py:256
  28.7 0.8 %collective-permute-done.6.other = f32[1,128,128]{2,1,0:T(8,128)S(1)} collective-permute-done((f32[1,128,128]{2,1,0:T(8,128)S(1)}, f32[1,128,128]{2,1,0:T(8,128)S(1)}, u32[]{:S(2)}, u32[]{:S(2)}) %collective-permute-start.6) | collective-permute-done | bytes 65568 | tf_op jit(solution)/shard_map/ppermute | solution.py:222
  29.5 0.5 %shard_map.82 = (f32[1,128,128]{2,1,0:T(8,128)S(1)}, f32[2,128,128]{2,1,0:T(8,128)S(1)}, f32[2,128,128]{2,1,0:T(8,128)S(1)}, f32[8,128]{1,0:T(8,128)S(1)}) custom-call(f32[1,128,128]{2,1,0:T(8,128)S(1)} %add.17.own, f32[1,128,128]{2,1,0:T(8,128)S(1)} %collective-permute-done.6.other, f32[4,128,128]{2,1,0:T(8,128)S(1)} %get-tuple-element.17.valid, ...), custom_call_target="tpu_custom_call" | custom-call | tf_op jit(solution)/shard_map/pallas_call | solution.py:271
  30.1 0.1 collective-permute-start.11
  30.1 1.7 %collective-permute-start.9 = (f32[8,128]{1,0:T(8,128)S(1)}, f32[8,128]{1,0:T(8,128)S(1)}, u32[]{:S(2)}, u32[]{:S(2)}) collective-permute-start(f32[8,128]{1,0:T(8,128)S(1)} %get-tuple-element.27), channel_id=1, source_target_pairs={{0,4},{4,0},{8,12},{12,8},{1,5},{5,1},{9,13},{13,9},{2,6},{6,2},{1... | collective-permute-start | bytes 12296 | tf_op jit(solution)/shard_map/ppermute | solution.py:210
  31.9 0.0 collective-permute-done.11
  31.9 1.6 %collective-permute-start.12 = (f32[2,128,128]{2,1,0:T(8,128)S(1)}, f32[2,128,128]{2,1,0:T(8,128)S(1)}, u32[]{:S(2)}, u32[]{:S(2)}) collective-permute-start(f32[2,128,128]{2,1,0:T(8,128)S(1)} %add.18), channel_id=1, source_target_pairs={{0,2},{1,3},{2,0},{3,1},{4,6},{5,7},{6,4},{7,5},{8,10},{9,11},{10,... | collective-permute-start | bytes 393224 | tf_op jit(solution)/shard_map/ppermute | solution.py:222
  33.5 0.3 collective-permute-done.9
  33.8 2.2 %collective-permute-start.10 = (f32[16,128]{1,0:T(8,128)S(1)}, f32[16,128]{1,0:T(8,128)S(1)}, u32[]{:S(2)}, u32[]{:S(2)}) collective-permute-start(f32[16,128]{1,0:T(8,128)S(1)} %constant_dynamic-update-slice_fusion.near), channel_id=1, source_target_pairs={{0,8},{8,0},{4,12},{12,4},{1,9},{9,1},{5,13},{13,5},{2,10},{10,2},... | collective-permute-start | bytes 24584 | tf_op jit(solution)/shard_map/ppermute | solution.py:213
  36.0 1.5 %collective-permute-done.12 = f32[2,128,128]{2,1,0:T(8,128)S(1)} collective-permute-done((f32[2,128,128]{2,1,0:T(8,128)S(1)}, f32[2,128,128]{2,1,0:T(8,128)S(1)}, u32[]{:S(2)}, u32[]{:S(2)}) %collective-permute-start.12) | collective-permute-done | bytes 131104 | tf_op jit(solution)/shard_map/ppermute | solution.py:222
  37.6 0.1 collective-permute-start.13
  37.6 0.7 %collective-permute-done.10.far = f32[16,128]{1,0:T(8,128)S(1)} collective-permute-done((f32[16,128]{1,0:T(8,128)S(1)}, f32[16,128]{1,0:T(8,128)S(1)}, u32[]{:S(2)}, u32[]{:S(2)}) %collective-permute-start.10) | collective-permute-done | bytes 8224 | tf_op jit(solution)/shard_map/ppermute | solution.py:213
  38.4 0.3 shard_map.83.scalars
  38.6 0.4 collective-permute-done.13.others
  39.0 0.8 %shard_map.84 = (f32[128,512]{1,0:T(8,128)}, f32[1]{0:T(128)}) custom-call(f32[4,128,128]{2,1,0:T(8,128)S(1)} %get-tuple-element.17.valid, f32[8,128]{1,0:T(8,128)S(1)} %shard_map.83.scalars, f32[2,128,128]{2,1,0:T(8,128)S(1)} %add.19.total, f32[2,128,128]{2,1,0:T(8,128)S(1)} %collective-permute-done.13.others, ...), custom_call_target="tpu_custom_call" | custom-call | tf_op jit(solution)/shard_map/pallas_call | solution.py:286
  (9 shorter events, 0.1 us)
Async XLA Ops:
  0.6 17.0 %copy-start = (f32[4,128,128]{2,1,0:T(8,128)S(1)}, f32[4,128,128]{2,1,0:T(8,128)}, u32[]{:S(2)}) copy-start(f32[4,128,128]{2,1,0:T(8,128)} %refs_0_.3) | copy-start | bytes 786436
  0.6 12.5 %collective-permute-start = (f32[4,128,128]{2,1,0:T(8,128)}, f32[4,128,128]{2,1,0:T(8,128)S(1)}, u32[]{:S(2)}, u32[]{:S(2)}) collective-permute-start(f32[4,128,128]{2,1,0:T(8,128)} %refs_0_.3), channel_id=1, source_target_pairs={{0,12},{12,0},{4,8},{8,4},{1,13},{13,1},{5,9},{9,5},{2,14},{14,2},... | collective-permute-start | bytes 786440 | tf_op jit(solution)/shard_map/ppermute | solution.py:216
  5.8 13.5 %collective-permute-start.2 = (f32[4,128,128]{2,1,0:T(8,128)}, f32[4,128,128]{2,1,0:T(8,128)S(1)}, u32[]{:S(2)}, u32[]{:S(2)}) collective-permute-start(f32[4,128,128]{2,1,0:T(8,128)} %refs_0_.3), channel_id=1, source_target_pairs={{0,4},{4,0},{8,12},{12,8},{1,5},{5,1},{9,13},{13,9},{2,6},{6,2},{1... | collective-permute-start | bytes 786440 | tf_op jit(solution)/shard_map/ppermute | solution.py:210
  5.8 1.0 %copy-start.1 = (f32[128,512]{1,0:T(8,128)S(1)}, f32[128,512]{1,0:T(8,128)}, u32[]{:S(2)}) copy-start(f32[128,512]{1,0:T(8,128)} %wave.1) | copy-start | bytes 786436
  6.7 0.9 %copy-start.2 = (f32[4,128,128]{2,1,0:T(8,128)S(1)}, f32[4,128,128]{2,1,0:T(8,128)}, u32[]{:S(2)}) copy-start(f32[4,128,128]{2,1,0:T(8,128)} %left.1) | copy-start | bytes 786436
  7.7 0.7 %copy-start.3 = (s32[4,4]{1,0:T(4,128)S(1)}, s32[4,4]{1,0:T(4,128)}, u32[]{:S(2)}) copy-start(s32[4,4]{1,0:T(4,128)} %pairs.1) | copy-start | bytes 196
  8.3 0.7 %copy-start.4 = (s32[4]{0:T(128)S(1)}, s32[4]{0:T(128)}, u32[]{:S(2)}) copy-start(s32[4]{0:T(128)} %left_sizes.1) | copy-start | bytes 52
  9.0 0.7 %copy-start.5 = (s32[4]{0:T(128)S(1)}, s32[4]{0:T(128)}, u32[]{:S(2)}) copy-start(s32[4]{0:T(128)} %right_sizes.1) | copy-start | bytes 52
  13.2 10.4 %collective-permute-start.4 = (f32[4,128,128]{2,1,0:T(8,128)S(1)}, f32[4,128,128]{2,1,0:T(8,128)S(1)}, u32[]{:S(2)}, u32[]{:S(2)}) collective-permute-start(f32[4,128,128]{2,1,0:T(8,128)S(1)} %collective-permute-done.refs_1_.refs_2_), channel_id=1, source_target_pairs={{0,4},{4,0},{8,12},{12,8},{1,5},{5,1},{9,13},{13,9},{2,6},{6,2},{1... | collective-permute-start | bytes 786440 | tf_op jit(solution)/shard_map/ppermute | solution.py:210
  17.9 1.3 %collective-permute-start.1 = (f32[1,128,128]{2,1,0:T(8,128)S(1)}, f32[1,128,128]{2,1,0:T(8,128)S(1)}, u32[]{:S(2)}, u32[]{:S(2)}) collective-permute-start(f32[1,128,128]{2,1,0:T(8,128)S(1)} %shard_map.78), channel_id=1, source_target_pairs={{0,1},{1,0},{2,3},{3,2},{4,5},{5,4},{6,7},{7,6},{8,9},{9,8},{10,11... | collective-permute-start | bytes 196616 | tf_op jit(solution)/shard_map/ppermute | solution.py:219
  19.6 1.4 %collective-permute-start.3 = (f32[2,128,128]{2,1,0:T(8,128)S(1)}, f32[2,128,128]{2,1,0:T(8,128)S(1)}, u32[]{:S(2)}, u32[]{:S(2)}) collective-permute-start(f32[2,128,128]{2,1,0:T(8,128)S(1)} %shard_map.79), channel_id=1, source_target_pairs={{0,1},{1,0},{2,3},{3,2},{4,5},{5,4},{6,7},{7,6},{8,9},{9,8},{10,11... | collective-permute-start | bytes 393224 | tf_op jit(solution)/shard_map/ppermute | solution.py:219
  21.0 7.0 %collective-permute-start.8 = (f32[2,128,128]{2,1,0:T(8,128)S(1)}, f32[2,128,128]{2,1,0:T(8,128)S(1)}, u32[]{:S(2)}, u32[]{:S(2)}) collective-permute-start(f32[2,128,128]{2,1,0:T(8,128)S(1)} %add.16), channel_id=1, source_target_pairs={{0,2},{1,3},{2,0},{3,1},{4,6},{5,7},{6,4},{7,5},{8,10},{9,11},{10,... | collective-permute-start | bytes 393224 | tf_op jit(solution)/shard_map/ppermute | solution.py:222
  22.6 5.5 %collective-permute-start.7 = (f32[1,128,128]{2,1,0:T(8,128)S(1)}, f32[1,128,128]{2,1,0:T(8,128)S(1)}, u32[]{:S(2)}, u32[]{:S(2)}) collective-permute-start(f32[1,128,128]{2,1,0:T(8,128)S(1)} %add.15), channel_id=1, source_target_pairs={{0,2},{1,3},{2,0},{3,1},{4,6},{5,7},{6,4},{7,5},{8,10},{9,11},{10,... | collective-permute-start | bytes 196616 | tf_op jit(solution)/shard_map/ppermute | solution.py:222
  23.9 1.3 %collective-permute-start.5 = (f32[1,128,128]{2,1,0:T(8,128)S(1)}, f32[1,128,128]{2,1,0:T(8,128)S(1)}, u32[]{:S(2)}, u32[]{:S(2)}) collective-permute-start(f32[1,128,128]{2,1,0:T(8,128)S(1)} %shard_map.80), channel_id=1, source_target_pairs={{0,1},{1,0},{2,3},{3,2},{4,5},{5,4},{6,7},{7,6},{8,9},{9,8},{10,11... | collective-permute-start | bytes 196616 | tf_op jit(solution)/shard_map/ppermute | solution.py:219
  25.2 4.3 %collective-permute-start.6 = (f32[1,128,128]{2,1,0:T(8,128)S(1)}, f32[1,128,128]{2,1,0:T(8,128)S(1)}, u32[]{:S(2)}, u32[]{:S(2)}) collective-permute-start(f32[1,128,128]{2,1,0:T(8,128)S(1)} %add.17.own), channel_id=1, source_target_pairs={{0,2},{1,3},{2,0},{3,1},{4,6},{5,7},{6,4},{7,5},{8,10},{9,11},{10,... | collective-permute-start | bytes 196616 | tf_op jit(solution)/shard_map/ppermute | solution.py:222
  30.1 1.8 %collective-permute-start.11 = (f32[2,128,128]{2,1,0:T(8,128)S(1)}, f32[2,128,128]{2,1,0:T(8,128)S(1)}, u32[]{:S(2)}, u32[]{:S(2)}) collective-permute-start(f32[2,128,128]{2,1,0:T(8,128)S(1)} %get-tuple-element.29), channel_id=1, source_target_pairs={{0,1},{1,0},{2,3},{3,2},{4,5},{5,4},{6,7},{7,6},{8,9},{9,8},{10,11... | collective-permute-start | bytes 393224 | tf_op jit(solution)/shard_map/ppermute | solution.py:219
  30.1 3.7 %collective-permute-start.9 = (f32[8,128]{1,0:T(8,128)S(1)}, f32[8,128]{1,0:T(8,128)S(1)}, u32[]{:S(2)}, u32[]{:S(2)}) collective-permute-start(f32[8,128]{1,0:T(8,128)S(1)} %get-tuple-element.27), channel_id=1, source_target_pairs={{0,4},{4,0},{8,12},{12,8},{1,5},{5,1},{9,13},{13,9},{2,6},{6,2},{1... | collective-permute-start | bytes 12296 | tf_op jit(solution)/shard_map/ppermute | solution.py:210
  31.9 5.6 %collective-permute-start.12 = (f32[2,128,128]{2,1,0:T(8,128)S(1)}, f32[2,128,128]{2,1,0:T(8,128)S(1)}, u32[]{:S(2)}, u32[]{:S(2)}) collective-permute-start(f32[2,128,128]{2,1,0:T(8,128)S(1)} %add.18), channel_id=1, source_target_pairs={{0,2},{1,3},{2,0},{3,1},{4,6},{5,7},{6,4},{7,5},{8,10},{9,11},{10,... | collective-permute-start | bytes 393224 | tf_op jit(solution)/shard_map/ppermute | solution.py:222
  33.8 4.5 %collective-permute-start.10 = (f32[16,128]{1,0:T(8,128)S(1)}, f32[16,128]{1,0:T(8,128)S(1)}, u32[]{:S(2)}, u32[]{:S(2)}) collective-permute-start(f32[16,128]{1,0:T(8,128)S(1)} %constant_dynamic-update-slice_fusion.near), channel_id=1, source_target_pairs={{0,8},{8,0},{4,12},{12,4},{1,9},{9,1},{5,13},{13,5},{2,10},{10,2},... | collective-permute-start | bytes 24584 | tf_op jit(solution)/shard_map/ppermute | solution.py:213
  37.6 1.4 %collective-permute-start.13 = (f32[2,128,128]{2,1,0:T(8,128)S(1)}, f32[2,128,128]{2,1,0:T(8,128)S(1)}, u32[]{:S(2)}, u32[]{:S(2)}) collective-permute-start(f32[2,128,128]{2,1,0:T(8,128)S(1)} %add.19.total), channel_id=1, source_target_pairs={{0,1},{1,0},{2,3},{3,2},{4,5},{5,4},{6,7},{7,6},{8,9},{9,8},{10,11... | collective-permute-start | bytes 393224 | tf_op jit(solution)/shard_map/ppermute | solution.py:219

commit v6 on v5

--- a/solution.py
+++ b/solution.py
@@ -20,30 +20,46 @@
 
 def split(x):
     high = x.astype(BF16)
-    return high, (x - high.astype(F32)).astype(BF16)
-
-
-def times(a, x):
-    n = x.shape[1]
-    parts = jnp.concatenate(split(x), axis=1)
-    both = lax.dot_general(
-        a,
-        jnp.concatenate([parts, parts], axis=0),
-        (((1,), (0,)), ((), ())),
-        preferred_element_type=F32,
-    )
-    return both[:, n:] + both[:, :n]
+    rest = x - high.astype(F32)
+    middle = rest.astype(BF16)
+    return high, middle, (rest - middle.astype(F32)).astype(BF16)
+
+
+def matmul(a, b, turned=False):
+    return lax.dot_general(
+        a, b, (((1,), (1 if turned else 0,)), ((), ())), preferred_element_type=F32
+    )
+
+
+def left_parts(a):
+    high, middle, low = split(a)
+    return jnp.concatenate([middle, high, low], axis=1)
+
+
+def times(parts, x):
+    depth, n = x.shape
+    high, middle, low = split(x)
+    large = jnp.concatenate([high, middle], axis=1)
+    large = matmul(parts[:, : 2 * depth], jnp.concatenate([large, large], axis=0))
+    small = matmul(parts[:, depth:], jnp.concatenate([low, high], axis=0))
+    return (small + large[:, n:]) + large[:, :n]
 
 
 def times_turned(a, b):
     m, n = a.shape[0], b.shape[0]
-    both = lax.dot_general(
-        jnp.concatenate(split(a), axis=0),
-        jnp.concatenate(split(b), axis=0),
-        (((1,), (1,)), ((), ())),
-        preferred_element_type=F32,
-    )
-    return (both[m:, n:] + (both[m:, :n] + both[:m, n:])) + both[:m, :n]
+    a_high, a_middle, a_low = split(a)
+    b_high, b_middle, b_low = split(b)
+    large = matmul(
+        jnp.concatenate([a_high, a_middle], axis=0),
+        jnp.concatenate([b_high, b_middle], axis=0),
+        turned=True,
+    )
+    small = matmul(
+        jnp.concatenate([a_high, a_low], axis=1),
+        jnp.concatenate([b_low, b_high], axis=1),
+        turned=True,
+    )
+    return ((small + large[m:, n:]) + (large[m:, :n] + large[:m, n:])) + large[:m, :n]
 
 
 def block_valid(left_sizes, right_sizes, pairs, a, b, rows, cols):
@@ -83,7 +99,7 @@
     channels, rows, _ = left.shape
     slots, _, inner = halfway.shape
     cols = inner // channels
-    factors[...] = jnp.concatenate(split(left[...].reshape(channels * rows, rows)), axis=1)
+    factors[...] = left_parts(left[...].reshape(channels * rows, rows))
     for k in range(slots):
         b = slot_column(k, sector)
         valid[k] = block_valid(left_sizes, right_sizes, pairs, sector, b, rows, cols)
@@ -100,6 +116,10 @@
     out = refs[-1]
     for k, slot in enumerate(slots):
         out[k] = times_turned(halfway[slot], channel_row(refs[k]))
+
+
+def ratio_of(cross, square):
+    return jnp.where(square > 0, cross / jnp.where(square > 0, square, 1.0), 0.0)
 
 
 def second_images(slots, own, other, valid, factors, rights, image):
@@ -123,13 +143,14 @@
         v = vector[slot]
         cross += jnp.sum(v * image[k], axis=0, keepdims=True)
         square += jnp.sum(v * v, axis=0, keepdims=True)
-    ratio = jnp.where(square > 0, cross / jnp.where(square > 0, square, 1.0), 0.0)
+    both = jnp.sum(jnp.concatenate([cross, square], axis=0), axis=1, keepdims=True)
+    both = jnp.broadcast_to(both, (2, cols))
+    ratio = ratio_of(both[0:1], both[1:2])
     rest = jnp.zeros((1, cols), F32)
     for k, slot in enumerate(slots):
         away = image[k] - ratio * vector[slot]
         rest += jnp.sum(away * away, axis=0, keepdims=True)
-    sums[at : at + 1, :] = cross
-    sums[at + 1 : at + 2, :] = square
+    sums[at : at + 2, :] = both
     sums[at + 2 : at + 3, :] = rest
 
 
@@ -162,28 +183,24 @@
 
 def scalar_body(groups, cells, near, far, scalars):
     def everyone(read):
-        lanes = (read(near, 0) + read(near, 8)) + (read(far, 0) + read(far, 8))
-        return jnp.sum(lanes, axis=1, keepdims=True)
+        return (read(near, 0) + read(near, 8)) + (read(far, 0) + read(far, 8))
 
     def every_group(row):
-        return lambda s, at: sum(
-            s[at + row + 3 * g : at + row + 3 * g + 1, :] for g in range(groups)
-        )
-
-    both = everyone(lambda s, at: s[at : at + 2, :] + s[at + 3 : at + 5, :])
-    value = both[0:1, :] / (both[1:2, :] + TINY)
-
-    def rest_of(s, at):
-        total = every_group(2)(s, at)
+        return lambda s, at: sum(s[at + row + 3 * g : at + row + 3 * g + 1, :] for g in range(groups))
+
+    value = everyone(every_group(0)) / (everyone(every_group(1)) + TINY)
+
+    def gaps(s, at):
+        total = 0.0
         for row in range(at, at + 3 * groups, 3):
-            c = s[row + 1 : row + 2, :]
-            ratio = jnp.where(c > 0, s[row : row + 1, :] / jnp.where(c > 0, c, 1.0), 0.0)
-            total += (ratio - value) * (ratio - value) * c
+            square = s[row + 1 : row + 2, :]
+            gap = ratio_of(s[row : row + 1, :], square) - value
+            total += gap * (gap * square)
         return total
 
-    scale = 1.0 / jnp.sqrt(everyone(rest_of) / cells + TINY)
-    scalars[0:1, :] = jnp.broadcast_to(value, (1, scalars.shape[1]))
-    scalars[1:2, :] = jnp.broadcast_to(scale, (1, scalars.shape[1]))
+    rest = jnp.sum(everyone(every_group(2)), axis=1, keepdims=True) + everyone(gaps)
+    scalars[0:1, :] = value
+    scalars[1:2, :] = 1.0 / jnp.sqrt(rest / cells + TINY)
 
 
 def last_body(groups, valid, scalars, total, others, *refs):
@@ -234,7 +251,7 @@
         [
             shape(sectors, rows, cols),
             shape(sectors, rows, channels * cols),
-            shape(channels * rows, 2 * rows, of=BF16),
+            shape(channels * rows, 3 * rows, of=BF16),
             shape(sectors, rows, cols),
         ],
         3,

time: 40 us -> 40.2 us (level)
  Pallas kernels: 4.19 us -> 4.97 us
  waiting for transfers between devices: 11.7 us -> 11.2 us
  transfers between devices with their start and end apart: 14 -> 14, of which waited for: 11 -> 11; matrix products, arithmetic and copies ran while one was open for 0% -> 0% of each run, Pallas kernels for 7% -> 9%
where the time goes in v6:
time: 40.2 us; the launch traced here: 40 us
  starting transfers between devices  19.1 us (48%)
  waiting for transfers between devices  11.2 us (28%)
  Pallas kernels  4.97 us (12%)
  local copies, waits for them, and re-layouts  3.9 us (10%)
  between operations  0.75 us (2%)
    ppermute x3, starting transfers between devices, near(): return lax.ppermute(x, 'sector', [(0, 1), (1, 0), (2, 3), (3, 2)])  6.13 us
    ppermute x4, starting transfers between devices, across(): return lax.ppermute(x, 'mpo', [(0, 2), (1, 3), (2, 0), (3, 1)])  5.21 us
    ppermute x1, starting transfers between devices, mirror(): return lax.ppermute(x, 'sector', [(0, 3), (3, 0), (1, 2), (2, 1)])  5.11 us
    ppermute x5, waiting for transfers between devices, core(): return lax.ppermute(x, 'mpo', [(0, 1), (1, 0), (2, 3), (3, 2)])  4.14 us
    unnamed x13, local copies, waits for them, and re-layouts  3.9 us
    ppermute x4, waiting for transfers between devices, across(): return lax.ppermute(x, 'mpo', [(0, 2), (1, 3), (2, 0), (3, 1)])  3.3 us
    ppermute x1, waiting for transfers between devices, mirror(): return lax.ppermute(x, 'sector', [(0, 3), (3, 0), (1, 2), (2, 1)])  2.3 us
    ppermute x1, starting transfers between devices, far(): return lax.ppermute(x, 'sector', [(0, 2), (2, 0), (1, 3), (3, 1)])  2.15 us
  transfers between devices with their start and end apart: 14, of which 11 were waited for; matrix products, arithmetic and copies ran while one was open for 0% of the time, Pallas kernels for 9%

profile of v6, /device:TPU:0, one launch (start us, length us, event | category | flops | bytes accessed | tf_op | source)
XLA Modules:
  0.0 40.0 jit_solution(16081039062225042497)
XLA Ops:
  0.6 0.0 copy-start
  0.6 5.1 %collective-permute-start = (f32[4,128,128]{2,1,0:T(8,128)}, f32[4,128,128]{2,1,0:T(8,128)S(1)}, u32[]{:S(2)}, u32[]{:S(2)}) collective-permute-start(f32[4,128,128]{2,1,0:T(8,128)} %refs_0_.3), channel_id=1, source_target_pairs={{0,12},{12,0},{4,8},{8,4},{1,13},{13,1},{5,9},{9,5},{2,14},{14,2},... | collective-permute-start | bytes 786440 | tf_op jit(solution)/shard_map/ppermute | solution.py:233
  5.8 0.0 collective-permute-start.2
  5.8 0.0 copy-start.1
  5.8 0.9 %copy-done.1 = f32[128,512]{1,0:T(8,128)S(1)} copy-done((f32[128,512]{1,0:T(8,128)S(1)}, f32[128,512]{1,0:T(8,128)}, u32[]{:S(2)}) %copy-start.1) | copy-done | bytes 262168
  6.7 0.0 copy-start.2
  6.7 0.9 %copy-done.2 = f32[4,128,128]{2,1,0:T(8,128)S(1)} copy-done((f32[4,128,128]{2,1,0:T(8,128)S(1)}, f32[4,128,128]{2,1,0:T(8,128)}, u32[]{:S(2)}) %copy-start.2) | copy-done | bytes 262168
  7.7 0.0 copy-start.3
  7.7 0.7 %copy-done.3 = s32[4,4]{1,0:T(4,128)S(1)} copy-done((s32[4,4]{1,0:T(4,128)S(1)}, s32[4,4]{1,0:T(4,128)}, u32[]{:S(2)}) %copy-start.3) | copy-done | bytes 88
  8.3 0.0 copy-start.4
  8.3 0.7 %copy-done.4 = s32[4]{0:T(128)S(1)} copy-done((s32[4]{0:T(128)S(1)}, s32[4]{0:T(128)}, u32[]{:S(2)}) %copy-start.4) | copy-done | bytes 40
  9.0 0.0 copy-start.5
  9.0 0.7 %copy-done.5 = s32[4]{0:T(128)S(1)} copy-done((s32[4]{0:T(128)S(1)}, s32[4]{0:T(128)}, u32[]{:S(2)}) %copy-start.5) | copy-done | bytes 40
  9.7 1.2 %shard_map.77 = (f32[4,128,128]{2,1,0:T(8,128)S(1)}, f32[4,128,512]{2,1,0:T(8,128)S(1)}, bf16[512,384]{1,0:T(8,128)(2,1)S(1)}, f32[4,128,128]{2,1,0:T(8,128)S(1)}) custom-call(s32[4]{0:T(128)S(1)} %copy-done.4, s32[4]{0:T(128)S(1)} %copy-done.5, s32[4,4]{1,0:T(4,128)S(1)} %copy-done.3, f32[128,512]{1,0:T(8,128)S(1)} %copy-done.1, f32[4,128,128]{2,1,0:T(8,128)S(1)} %copy-done.2), custom_call_target="tpu_custom_call" | custom-call | tf_op jit(solution)/shard_map/pallas_call | solution.py:249
  10.9 2.3 %collective-permute-done.refs_1_.refs_2_ = f32[4,128,128]{2,1,0:T(8,128)S(1)} collective-permute-done((f32[4,128,128]{2,1,0:T(8,128)}, f32[4,128,128]{2,1,0:T(8,128)S(1)}, u32[]{:S(2)}, u32[]{:S(2)}) %collective-permute-start) | collective-permute-done | bytes 262176 | tf_op jit(solution)/shard_map/ppermute | solution.py:233
  13.2 4.4 %collective-permute-start.4 = (f32[4,128,128]{2,1,0:T(8,128)S(1)}, f32[4,128,128]{2,1,0:T(8,128)S(1)}, u32[]{:S(2)}, u32[]{:S(2)}) collective-permute-start(f32[4,128,128]{2,1,0:T(8,128)S(1)} %collective-permute-done.refs_1_.refs_2_), channel_id=1, source_target_pairs={{0,4},{4,0},{8,12},{12,8},{1,5},{5,1},{9,13},{13,9},{2,6},{6,2},{1... | collective-permute-start | bytes 786440 | tf_op jit(solution)/shard_map/ppermute | solution.py:227
  17.6 0.0 copy-done
  17.6 0.3 shard_map.78
  17.9 0.1 collective-permute-start.1
  18.0 1.2 %collective-permute-done.1 = f32[1,128,128]{2,1,0:T(8,128)S(1)} collective-permute-done((f32[1,128,128]{2,1,0:T(8,128)S(1)}, f32[1,128,128]{2,1,0:T(8,128)S(1)}, u32[]{:S(2)}, u32[]{:S(2)}) %collective-permute-start.1) | collective-permute-done | bytes 65568 | tf_op jit(solution)/shard_map/ppermute | solution.py:236
  19.3 0.0 collective-permute-done.2.refs_0_.refs_1_
  19.3 0.5 %shard_map.79 = f32[2,128,128]{2,1,0:T(8,128)S(1)} custom-call(f32[4,128,512]{2,1,0:T(8,128)S(1)} %get-tuple-element.21.halfway, f32[4,128,128]{2,1,0:T(8,128)S(1)} %collective-permute-done.2.refs_0_.refs_1_, f32[4,128,128]{2,1,0:T(8,128)S(1)} %collective-permute-done.refs_1_.refs_2_), custom_call_target="tpu_custom_call" | custom-call | tf_op jit(solution)/shard_map/pallas_call | solution.py:263
  19.8 0.2 collective-permute-start.3
  20.0 1.2 %collective-permute-done.3 = f32[2,128,128]{2,1,0:T(8,128)S(1)} collective-permute-done((f32[2,128,128]{2,1,0:T(8,128)S(1)}, f32[2,128,128]{2,1,0:T(8,128)S(1)}, u32[]{:S(2)}, u32[]{:S(2)}) %collective-permute-start.3) | collective-permute-done | bytes 131104 | tf_op jit(solution)/shard_map/ppermute | solution.py:236
  21.2 1.6 %collective-permute-start.8 = (f32[2,128,128]{2,1,0:T(8,128)S(1)}, f32[2,128,128]{2,1,0:T(8,128)S(1)}, u32[]{:S(2)}, u32[]{:S(2)}) collective-permute-start(f32[2,128,128]{2,1,0:T(8,128)S(1)} %add.16), channel_id=1, source_target_pairs={{0,2},{1,3},{2,0},{3,1},{4,6},{5,7},{6,4},{7,5},{8,10},{9,11},{10,... | collective-permute-start | bytes 393224 | tf_op jit(solution)/shard_map/ppermute | solution.py:239
  22.8 0.5 %collective-permute-start.7 = (f32[1,128,128]{2,1,0:T(8,128)S(1)}, f32[1,128,128]{2,1,0:T(8,128)S(1)}, u32[]{:S(2)}, u32[]{:S(2)}) collective-permute-start(f32[1,128,128]{2,1,0:T(8,128)S(1)} %add.15), channel_id=1, source_target_pairs={{0,2},{1,3},{2,0},{3,1},{4,6},{5,7},{6,4},{7,5},{8,10},{9,11},{10,... | collective-permute-start | bytes 196616 | tf_op jit(solution)/shard_map/ppermute | solution.py:239
  23.3 0.3 collective-permute-done.4.refs_0_
  23.6 0.3 shard_map.80
  23.9 0.1 collective-permute-start.5
  24.0 1.2 %collective-permute-done.5 = f32[1,128,128]{2,1,0:T(8,128)S(1)} collective-permute-done((f32[1,128,128]{2,1,0:T(8,128)S(1)}, f32[1,128,128]{2,1,0:T(8,128)S(1)}, u32[]{:S(2)}, u32[]{:S(2)}) %collective-permute-start.5) | collective-permute-done | bytes 65568 | tf_op jit(solution)/shard_map/ppermute | solution.py:236
  25.3 1.6 %collective-permute-start.6 = (f32[1,128,128]{2,1,0:T(8,128)S(1)}, f32[1,128,128]{2,1,0:T(8,128)S(1)}, u32[]{:S(2)}, u32[]{:S(2)}) collective-permute-start(f32[1,128,128]{2,1,0:T(8,128)S(1)} %add.17.own), channel_id=1, source_target_pairs={{0,2},{1,3},{2,0},{3,1},{4,6},{5,7},{6,4},{7,5},{8,10},{9,11},{10,... | collective-permute-start | bytes 196616 | tf_op jit(solution)/shard_map/ppermute | solution.py:239
  26.8 1.5 %collective-permute-done.7 = f32[1,128,128]{2,1,0:T(8,128)S(1)} collective-permute-done((f32[1,128,128]{2,1,0:T(8,128)S(1)}, f32[1,128,128]{2,1,0:T(8,128)S(1)}, u32[]{:S(2)}, u32[]{:S(2)}) %collective-permute-start.7) | collective-permute-done | bytes 65568 | tf_op jit(solution)/shard_map/ppermute | solution.py:239
  28.3 0.0 collective-permute-done.8
  28.3 1.0 %shard_map.81 = (f32[3,128,128]{2,1,0:T(8,128)S(1)}, f32[3,128,128]{2,1,0:T(8,128)S(1)}, f32[8,128]{1,0:T(8,128)S(1)}) custom-call(f32[3,128,128]{2,1,0:T(8,128)S(1)} %pad_maximum_fusion.own, f32[3,128,128]{2,1,0:T(8,128)S(1)} %pad_maximum_fusion.1.other, f32[4,128,128]{2,1,0:T(8,128)S(1)} %get-tuple-element.17.valid, ...), custom_call_target="tpu_custom_call" | custom-call | tf_op jit(solution)/shard_map/pallas_call | solution.py:273
  29.4 0.3 collective-permute-done.6.other
  29.6 0.7 %shard_map.82 = (f32[1,128,128]{2,1,0:T(8,128)S(1)}, f32[2,128,128]{2,1,0:T(8,128)S(1)}, f32[2,128,128]{2,1,0:T(8,128)S(1)}, f32[8,128]{1,0:T(8,128)S(1)}) custom-call(f32[1,128,128]{2,1,0:T(8,128)S(1)} %add.17.own, f32[1,128,128]{2,1,0:T(8,128)S(1)} %collective-permute-done.6.other, f32[4,128,128]{2,1,0:T(8,128)S(1)} %get-tuple-element.17.valid, ...), custom_call_target="tpu_custom_call" | custom-call | tf_op jit(solution)/shard_map/pallas_call | solution.py:288
  30.3 0.1 collective-permute-start.11
  30.4 1.7 %collective-permute-start.9 = (f32[8,128]{1,0:T(8,128)S(1)}, f32[8,128]{1,0:T(8,128)S(1)}, u32[]{:S(2)}, u32[]{:S(2)}) collective-permute-start(f32[8,128]{1,0:T(8,128)S(1)} %get-tuple-element.27), channel_id=1, source_target_pairs={{0,4},{4,0},{8,12},{12,8},{1,5},{5,1},{9,13},{13,9},{2,6},{6,2},{1... | collective-permute-start | bytes 12296 | tf_op jit(solution)/shard_map/ppermute | solution.py:227
  32.1 0.0 collective-permute-done.11
  32.1 1.6 %collective-permute-start.12 = (f32[2,128,128]{2,1,0:T(8,128)S(1)}, f32[2,128,128]{2,1,0:T(8,128)S(1)}, u32[]{:S(2)}, u32[]{:S(2)}) collective-permute-start(f32[2,128,128]{2,1,0:T(8,128)S(1)} %add.18), channel_id=1, source_target_pairs={{0,2},{1,3},{2,0},{3,1},{4,6},{5,7},{6,4},{7,5},{8,10},{9,11},{10,... | collective-permute-start | bytes 393224 | tf_op jit(solution)/shard_map/ppermute | solution.py:239
  33.7 0.4 collective-permute-done.9
  34.1 2.1 %collective-permute-start.10 = (f32[16,128]{1,0:T(8,128)S(1)}, f32[16,128]{1,0:T(8,128)S(1)}, u32[]{:S(2)}, u32[]{:S(2)}) collective-permute-start(f32[16,128]{1,0:T(8,128)S(1)} %constant_dynamic-update-slice_fusion.near), channel_id=1, source_target_pairs={{0,8},{8,0},{4,12},{12,4},{1,9},{9,1},{5,13},{13,5},{2,10},{10,2},... | collective-permute-start | bytes 24584 | tf_op jit(solution)/shard_map/ppermute | solution.py:230
  36.2 1.5 %collective-permute-done.12 = f32[2,128,128]{2,1,0:T(8,128)S(1)} collective-permute-done((f32[2,128,128]{2,1,0:T(8,128)S(1)}, f32[2,128,128]{2,1,0:T(8,128)S(1)}, u32[]{:S(2)}, u32[]{:S(2)}) %collective-permute-start.12) | collective-permute-done | bytes 131104 | tf_op jit(solution)/shard_map/ppermute | solution.py:239
  37.8 0.1 collective-permute-start.13
  37.9 0.8 %collective-permute-done.10.far = f32[16,128]{1,0:T(8,128)S(1)} collective-permute-done((f32[16,128]{1,0:T(8,128)S(1)}, f32[16,128]{1,0:T(8,128)S(1)}, u32[]{:S(2)}, u32[]{:S(2)}) %collective-permute-start.10) | collective-permute-done | bytes 8224 | tf_op jit(solution)/shard_map/ppermute | solution.py:230
  38.6 0.1 shard_map.83.scalars
  38.7 0.5 %collective-permute-done.13.others = f32[2,128,128]{2,1,0:T(8,128)S(1)} collective-permute-done((f32[2,128,128]{2,1,0:T(8,128)S(1)}, f32[2,128,128]{2,1,0:T(8,128)S(1)}, u32[]{:S(2)}, u32[]{:S(2)}) %collective-permute-start.13) | collective-permute-done | bytes 131104 | tf_op jit(solution)/shard_map/ppermute | solution.py:236
  39.2 0.8 %shard_map.84 = (f32[128,512]{1,0:T(8,128)}, f32[1]{0:T(128)}) custom-call(f32[4,128,128]{2,1,0:T(8,128)S(1)} %get-tuple-element.17.valid, f32[8,128]{1,0:T(8,128)S(1)} %shard_map.83.scalars, f32[2,128,128]{2,1,0:T(8,128)S(1)} %add.19.total, f32[2,128,128]{2,1,0:T(8,128)S(1)} %collective-permute-done.13.others, ...), custom_call_target="tpu_custom_call" | custom-call | tf_op jit(solution)/shard_map/pallas_call | solution.py:303
  (9 shorter events, 0.1 us)
Async XLA Ops:
  0.6 17.0 %copy-start = (f32[4,128,128]{2,1,0:T(8,128)S(1)}, f32[4,128,128]{2,1,0:T(8,128)}, u32[]{:S(2)}) copy-start(f32[4,128,128]{2,1,0:T(8,128)} %refs_0_.3) | copy-start | bytes 786436
  0.6 12.5 %collective-permute-start = (f32[4,128,128]{2,1,0:T(8,128)}, f32[4,128,128]{2,1,0:T(8,128)S(1)}, u32[]{:S(2)}, u32[]{:S(2)}) collective-permute-start(f32[4,128,128]{2,1,0:T(8,128)} %refs_0_.3), channel_id=1, source_target_pairs={{0,12},{12,0},{4,8},{8,4},{1,13},{13,1},{5,9},{9,5},{2,14},{14,2},... | collective-permute-start | bytes 786440 | tf_op jit(solution)/shard_map/ppermute | solution.py:233
  5.8 13.5 %collective-permute-start.2 = (f32[4,128,128]{2,1,0:T(8,128)}, f32[4,128,128]{2,1,0:T(8,128)S(1)}, u32[]{:S(2)}, u32[]{:S(2)}) collective-permute-start(f32[4,128,128]{2,1,0:T(8,128)} %refs_0_.3), channel_id=1, source_target_pairs={{0,4},{4,0},{8,12},{12,8},{1,5},{5,1},{9,13},{13,9},{2,6},{6,2},{1... | collective-permute-start | bytes 786440 | tf_op jit(solution)/shard_map/ppermute | solution.py:227
  5.8 1.0 %copy-start.1 = (f32[128,512]{1,0:T(8,128)S(1)}, f32[128,512]{1,0:T(8,128)}, u32[]{:S(2)}) copy-start(f32[128,512]{1,0:T(8,128)} %wave.1) | copy-start | bytes 786436
  6.7 0.9 %copy-start.2 = (f32[4,128,128]{2,1,0:T(8,128)S(1)}, f32[4,128,128]{2,1,0:T(8,128)}, u32[]{:S(2)}) copy-start(f32[4,128,128]{2,1,0:T(8,128)} %left.1) | copy-start | bytes 786436
  7.7 0.7 %copy-start.3 = (s32[4,4]{1,0:T(4,128)S(1)}, s32[4,4]{1,0:T(4,128)}, u32[]{:S(2)}) copy-start(s32[4,4]{1,0:T(4,128)} %pairs.1) | copy-start | bytes 196
  8.3 0.7 %copy-start.4 = (s32[4]{0:T(128)S(1)}, s32[4]{0:T(128)}, u32[]{:S(2)}) copy-start(s32[4]{0:T(128)} %left_sizes.1) | copy-start | bytes 52
  9.0 0.7 %copy-start.5 = (s32[4]{0:T(128)S(1)}, s32[4]{0:T(128)}, u32[]{:S(2)}) copy-start(s32[4]{0:T(128)} %right_sizes.1) | copy-start | bytes 52
  13.2 10.4 %collective-permute-start.4 = (f32[4,128,128]{2,1,0:T(8,128)S(1)}, f32[4,128,128]{2,1,0:T(8,128)S(1)}, u32[]{:S(2)}, u32[]{:S(2)}) collective-permute-start(f32[4,128,128]{2,1,0:T(8,128)S(1)} %collective-permute-done.refs_1_.refs_2_), channel_id=1, source_target_pairs={{0,4},{4,0},{8,12},{12,8},{1,5},{5,1},{9,13},{13,9},{2,6},{6,2},{1... | collective-permute-start | bytes 786440 | tf_op jit(solution)/shard_map/ppermute | solution.py:227
  17.9 1.3 %collective-permute-start.1 = (f32[1,128,128]{2,1,0:T(8,128)S(1)}, f32[1,128,128]{2,1,0:T(8,128)S(1)}, u32[]{:S(2)}, u32[]{:S(2)}) collective-permute-start(f32[1,128,128]{2,1,0:T(8,128)S(1)} %shard_map.78), channel_id=1, source_target_pairs={{0,1},{1,0},{2,3},{3,2},{4,5},{5,4},{6,7},{7,6},{8,9},{9,8},{10,11... | collective-permute-start | bytes 196616 | tf_op jit(solution)/shard_map/ppermute | solution.py:236
  19.8 1.4 %collective-permute-start.3 = (f32[2,128,128]{2,1,0:T(8,128)S(1)}, f32[2,128,128]{2,1,0:T(8,128)S(1)}, u32[]{:S(2)}, u32[]{:S(2)}) collective-permute-start(f32[2,128,128]{2,1,0:T(8,128)S(1)} %shard_map.79), channel_id=1, source_target_pairs={{0,1},{1,0},{2,3},{3,2},{4,5},{5,4},{6,7},{7,6},{8,9},{9,8},{10,11... | collective-permute-start | bytes 393224 | tf_op jit(solution)/shard_map/ppermute | solution.py:236
  21.2 7.1 %collective-permute-start.8 = (f32[2,128,128]{2,1,0:T(8,128)S(1)}, f32[2,128,128]{2,1,0:T(8,128)S(1)}, u32[]{:S(2)}, u32[]{:S(2)}) collective-permute-start(f32[2,128,128]{2,1,0:T(8,128)S(1)} %add.16), channel_id=1, source_target_pairs={{0,2},{1,3},{2,0},{3,1},{4,6},{5,7},{6,4},{7,5},{8,10},{9,11},{10,... | collective-permute-start | bytes 393224 | tf_op jit(solution)/shard_map/ppermute | solution.py:239
  22.8 5.5 %collective-permute-start.7 = (f32[1,128,128]{2,1,0:T(8,128)S(1)}, f32[1,128,128]{2,1,0:T(8,128)S(1)}, u32[]{:S(2)}, u32[]{:S(2)}) collective-permute-start(f32[1,128,128]{2,1,0:T(8,128)S(1)} %add.15), channel_id=1, source_target_pairs={{0,2},{1,3},{2,0},{3,1},{4,6},{5,7},{6,4},{7,5},{8,10},{9,11},{10,... | collective-permute-start | bytes 196616 | tf_op jit(solution)/shard_map/ppermute | solution.py:239
  23.9 1.3 %collective-permute-start.5 = (f32[1,128,128]{2,1,0:T(8,128)S(1)}, f32[1,128,128]{2,1,0:T(8,128)S(1)}, u32[]{:S(2)}, u32[]{:S(2)}) collective-permute-start(f32[1,128,128]{2,1,0:T(8,128)S(1)} %shard_map.80), channel_id=1, source_target_pairs={{0,1},{1,0},{2,3},{3,2},{4,5},{5,4},{6,7},{7,6},{8,9},{9,8},{10,11... | collective-permute-start | bytes 196616 | tf_op jit(solution)/shard_map/ppermute | solution.py:236
  25.3 4.4 %collective-permute-start.6 = (f32[1,128,128]{2,1,0:T(8,128)S(1)}, f32[1,128,128]{2,1,0:T(8,128)S(1)}, u32[]{:S(2)}, u32[]{:S(2)}) collective-permute-start(f32[1,128,128]{2,1,0:T(8,128)S(1)} %add.17.own), channel_id=1, source_target_pairs={{0,2},{1,3},{2,0},{3,1},{4,6},{5,7},{6,4},{7,5},{8,10},{9,11},{10,... | collective-permute-start | bytes 196616 | tf_op jit(solution)/shard_map/ppermute | solution.py:239
  30.3 1.8 %collective-permute-start.11 = (f32[2,128,128]{2,1,0:T(8,128)S(1)}, f32[2,128,128]{2,1,0:T(8,128)S(1)}, u32[]{:S(2)}, u32[]{:S(2)}) collective-permute-start(f32[2,128,128]{2,1,0:T(8,128)S(1)} %get-tuple-element.29), channel_id=1, source_target_pairs={{0,1},{1,0},{2,3},{3,2},{4,5},{5,4},{6,7},{7,6},{8,9},{9,8},{10,11... | collective-permute-start | bytes 393224 | tf_op jit(solution)/shard_map/ppermute | solution.py:236
  30.4 3.7 %collective-permute-start.9 = (f32[8,128]{1,0:T(8,128)S(1)}, f32[8,128]{1,0:T(8,128)S(1)}, u32[]{:S(2)}, u32[]{:S(2)}) collective-permute-start(f32[8,128]{1,0:T(8,128)S(1)} %get-tuple-element.27), channel_id=1, source_target_pairs={{0,4},{4,0},{8,12},{12,8},{1,5},{5,1},{9,13},{13,9},{2,6},{6,2},{1... | collective-permute-start | bytes 12296 | tf_op jit(solution)/shard_map/ppermute | solution.py:227
  32.1 5.6 %collective-permute-start.12 = (f32[2,128,128]{2,1,0:T(8,128)S(1)}, f32[2,128,128]{2,1,0:T(8,128)S(1)}, u32[]{:S(2)}, u32[]{:S(2)}) collective-permute-start(f32[2,128,128]{2,1,0:T(8,128)S(1)} %add.18), channel_id=1, source_target_pairs={{0,2},{1,3},{2,0},{3,1},{4,6},{5,7},{6,4},{7,5},{8,10},{9,11},{10,... | collective-permute-start | bytes 393224 | tf_op jit(solution)/shard_map/ppermute | solution.py:239
  34.1 4.5 %collective-permute-start.10 = (f32[16,128]{1,0:T(8,128)S(1)}, f32[16,128]{1,0:T(8,128)S(1)}, u32[]{:S(2)}, u32[]{:S(2)}) collective-permute-start(f32[16,128]{1,0:T(8,128)S(1)} %constant_dynamic-update-slice_fusion.near), channel_id=1, source_target_pairs={{0,8},{8,0},{4,12},{12,4},{1,9},{9,1},{5,13},{13,5},{2,10},{10,2},... | collective-permute-start | bytes 24584 | tf_op jit(solution)/shard_map/ppermute | solution.py:230
  37.8 1.4 %collective-permute-start.13 = (f32[2,128,128]{2,1,0:T(8,128)S(1)}, f32[2,128,128]{2,1,0:T(8,128)S(1)}, u32[]{:S(2)}, u32[]{:S(2)}) collective-permute-start(f32[2,128,128]{2,1,0:T(8,128)S(1)} %add.19.total), channel_id=1, source_target_pairs={{0,1},{1,0},{2,3},{3,2},{4,5},{5,4},{6,7},{7,6},{8,9},{9,8},{10,11... | collective-permute-start | bytes 393224 | tf_op jit(solution)/shard_map/ppermute | solution.py:236

commit v7 on v6

--- a/solution.py
+++ b/solution.py
@@ -122,14 +122,17 @@
     return jnp.where(square > 0, cross / jnp.where(square > 0, square, 1.0), 0.0)
 
 
-def second_images(slots, own, other, valid, factors, rights, image):
-    _, rows, cols = own.shape
-    channels = factors.shape[0] // rows
+def first_images(slots, own, other, valid, image):
     for k, slot in enumerate(slots):
         image[k] = (own[k] + other[k]) * valid[slot]
+
+
+def second_images(factors, rights, image):
+    slots, rows, cols = image.shape
+    channels = factors.shape[0] // rows
     half = times(factors[...], channel_row(image))
     partials = []
-    for k in range(len(slots)):
+    for k in range(slots):
         here = half[:, k * cols : (k + 1) * cols].reshape(channels, rows, cols)
         partials.append(times_turned(channel_row(here), channel_row(rights[k])))
     return partials
@@ -156,29 +159,24 @@
 
 def early_body(slots, own, other, valid, factors, vector, *refs):
     image, partial, sums = refs[-3:]
-    parts = second_images(slots, own, other, valid, factors, refs[:-3], image)
-    for k, part in enumerate(parts):
-        partial[k] = part
+    first_images(slots, own, other, valid, image)
     sums[...] = jnp.zeros_like(sums)
     write_sums(slots, vector, image, sums, 0)
+    for k, part in enumerate(second_images(factors, refs[:-3], image)):
+        partial[k] = part
 
 
 def late_body(early, slots, own, other, valid, factors, vector, sums_before, before, *refs):
     image, keep, send, sums = refs[-4:]
-    me = lax.axis_index("mpo") % 2
-    parts = second_images(slots, own, other, valid, factors, refs[:-4], image)
-    everything = {slot: before[k] for k, slot in enumerate(early)}
-    everything.update(zip(slots, parts))
-    for half in (0, 1):
-
-        @pl.when(me == half)
-        def _():
-            for k in (0, 1):
-                keep[k] = everything[2 * half + k]
-                send[k] = everything[2 * (1 - half) + k]
-
+    first = lax.axis_index("mpo") % 2 == 0
+    first_images(slots, own, other, valid, image)
     sums[...] = sums_before[...]
     write_sums(slots, vector, image, sums, 3)
+    everything = {slot: before[k] for k, slot in enumerate(early)}
+    everything.update(zip(slots, second_images(factors, refs[:-4], image)))
+    for k in (0, 1):
+        keep[k] = jnp.where(first, everything[k], everything[2 + k])
+        send[k] = jnp.where(first, everything[2 + k], everything[k])
 
 
 def scalar_body(groups, cells, near, far, scalars):

time: 40.2 us -> 40.1 us (level)
  no operation moved by 1% of the time
where the time goes in v7:
time: 40.1 us; the launch traced here: 39.9 us
  starting transfers between devices  19.1 us (48%)
  waiting for transfers between devices  11.2 us (28%)
  Pallas kernels  4.84 us (12%)
  local copies, waits for them, and re-layouts  3.9 us (10%)
  between operations  0.76 us (2%)
    ppermute x3, starting transfers between devices, near(): return lax.ppermute(x, 'sector', [(0, 1), (1, 0), (2, 3), (3, 2)])  6.13 us
    ppermute x4, starting transfers between devices, across(): return lax.ppermute(x, 'mpo', [(0, 2), (1, 3), (2, 0), (3, 1)])  5.21 us
    ppermute x1, starting transfers between devices, mirror(): return lax.ppermute(x, 'sector', [(0, 3), (3, 0), (1, 2), (2, 1)])  5.11 us
    ppermute x5, waiting for transfers between devices, core(): return lax.ppermute(x, 'mpo', [(0, 1), (1, 0), (2, 3), (3, 2)])  4.14 us
    unnamed x13, local copies, waits for them, and re-layouts  3.9 us
    ppermute x4, waiting for transfers between devices, across(): return lax.ppermute(x, 'mpo', [(0, 2), (1, 3), (2, 0), (3, 1)])  3.29 us
    ppermute x1, waiting for transfers between devices, mirror(): return lax.ppermute(x, 'sector', [(0, 3), (3, 0), (1, 2), (2, 1)])  2.3 us
    ppermute x1, starting transfers between devices, far(): return lax.ppermute(x, 'sector', [(0, 2), (2, 0), (1, 3), (3, 1)])  2.14 us
  transfers between devices with their start and end apart: 14, of which 11 were waited for; matrix products, arithmetic and copies ran while one was open for 0% of the time, Pallas kernels for 9%

profile of v7, /device:TPU:0, one launch (start us, length us, event | category | flops | bytes accessed | tf_op | source)
XLA Modules:
  0.0 39.9 jit_solution(4855161161388418957)
XLA Ops:
  0.6 0.0 copy-start
  0.6 5.1 %collective-permute-start = (f32[4,128,128]{2,1,0:T(8,128)}, f32[4,128,128]{2,1,0:T(8,128)S(1)}, u32[]{:S(2)}, u32[]{:S(2)}) collective-permute-start(f32[4,128,128]{2,1,0:T(8,128)} %refs_0_.3), channel_id=1, source_target_pairs={{0,12},{12,0},{4,8},{8,4},{1,13},{13,1},{5,9},{9,5},{2,14},{14,2},... | collective-permute-start | bytes 786440 | tf_op jit(solution)/shard_map/ppermute | solution.py:231
  5.8 0.0 collective-permute-start.2
  5.8 0.0 copy-start.1
  5.8 0.9 %copy-done.1 = f32[128,512]{1,0:T(8,128)S(1)} copy-done((f32[128,512]{1,0:T(8,128)S(1)}, f32[128,512]{1,0:T(8,128)}, u32[]{:S(2)}) %copy-start.1) | copy-done | bytes 262168
  6.7 0.0 copy-start.2
  6.7 0.9 %copy-done.2 = f32[4,128,128]{2,1,0:T(8,128)S(1)} copy-done((f32[4,128,128]{2,1,0:T(8,128)S(1)}, f32[4,128,128]{2,1,0:T(8,128)}, u32[]{:S(2)}) %copy-start.2) | copy-done | bytes 262168
  7.7 0.0 copy-start.3
  7.7 0.7 %copy-done.3 = s32[4,4]{1,0:T(4,128)S(1)} copy-done((s32[4,4]{1,0:T(4,128)S(1)}, s32[4,4]{1,0:T(4,128)}, u32[]{:S(2)}) %copy-start.3) | copy-done | bytes 88
  8.3 0.0 copy-start.4
  8.3 0.7 %copy-done.4 = s32[4]{0:T(128)S(1)} copy-done((s32[4]{0:T(128)S(1)}, s32[4]{0:T(128)}, u32[]{:S(2)}) %copy-start.4) | copy-done | bytes 40
  9.0 0.0 copy-start.5
  9.0 0.7 %copy-done.5 = s32[4]{0:T(128)S(1)} copy-done((s32[4]{0:T(128)S(1)}, s32[4]{0:T(128)}, u32[]{:S(2)}) %copy-start.5) | copy-done | bytes 40
  9.7 1.2 %shard_map.77 = (f32[4,128,128]{2,1,0:T(8,128)S(1)}, f32[4,128,512]{2,1,0:T(8,128)S(1)}, bf16[512,384]{1,0:T(8,128)(2,1)S(1)}, f32[4,128,128]{2,1,0:T(8,128)S(1)}) custom-call(s32[4]{0:T(128)S(1)} %copy-done.4, s32[4]{0:T(128)S(1)} %copy-done.5, s32[4,4]{1,0:T(4,128)S(1)} %copy-done.3, f32[128,512]{1,0:T(8,128)S(1)} %copy-done.1, f32[4,128,128]{2,1,0:T(8,128)S(1)} %copy-done.2), custom_call_target="tpu_custom_call" | custom-call | tf_op jit(solution)/shard_map/pallas_call | solution.py:247
  10.9 2.3 %collective-permute-done.refs_1_.refs_2_ = f32[4,128,128]{2,1,0:T(8,128)S(1)} collective-permute-done((f32[4,128,128]{2,1,0:T(8,128)}, f32[4,128,128]{2,1,0:T(8,128)S(1)}, u32[]{:S(2)}, u32[]{:S(2)}) %collective-permute-start) | collective-permute-done | bytes 262176 | tf_op jit(solution)/shard_map/ppermute | solution.py:231
  13.2 4.4 %collective-permute-start.4 = (f32[4,128,128]{2,1,0:T(8,128)S(1)}, f32[4,128,128]{2,1,0:T(8,128)S(1)}, u32[]{:S(2)}, u32[]{:S(2)}) collective-permute-start(f32[4,128,128]{2,1,0:T(8,128)S(1)} %collective-permute-done.refs_1_.refs_2_), channel_id=1, source_target_pairs={{0,4},{4,0},{8,12},{12,8},{1,5},{5,1},{9,13},{13,9},{2,6},{6,2},{1... | collective-permute-start | bytes 786440 | tf_op jit(solution)/shard_map/ppermute | solution.py:225
  17.6 0.0 copy-done
  17.6 0.3 shard_map.78
  17.9 0.1 collective-permute-start.1
  18.0 1.2 %collective-permute-done.1 = f32[1,128,128]{2,1,0:T(8,128)S(1)} collective-permute-done((f32[1,128,128]{2,1,0:T(8,128)S(1)}, f32[1,128,128]{2,1,0:T(8,128)S(1)}, u32[]{:S(2)}, u32[]{:S(2)}) %collective-permute-start.1) | collective-permute-done | bytes 65568 | tf_op jit(solution)/shard_map/ppermute | solution.py:234
  19.3 0.0 collective-permute-done.2.refs_0_.refs_1_
  19.3 0.5 %shard_map.79 = f32[2,128,128]{2,1,0:T(8,128)S(1)} custom-call(f32[4,128,512]{2,1,0:T(8,128)S(1)} %get-tuple-element.21.halfway, f32[4,128,128]{2,1,0:T(8,128)S(1)} %collective-permute-done.2.refs_0_.refs_1_, f32[4,128,128]{2,1,0:T(8,128)S(1)} %collective-permute-done.refs_1_.refs_2_), custom_call_target="tpu_custom_call" | custom-call | tf_op jit(solution)/shard_map/pallas_call | solution.py:261
  19.8 0.2 collective-permute-start.3
  20.0 1.2 %collective-permute-done.3 = f32[2,128,128]{2,1,0:T(8,128)S(1)} collective-permute-done((f32[2,128,128]{2,1,0:T(8,128)S(1)}, f32[2,128,128]{2,1,0:T(8,128)S(1)}, u32[]{:S(2)}, u32[]{:S(2)}) %collective-permute-start.3) | collective-permute-done | bytes 131104 | tf_op jit(solution)/shard_map/ppermute | solution.py:234
  21.2 1.6 %collective-permute-start.8 = (f32[2,128,128]{2,1,0:T(8,128)S(1)}, f32[2,128,128]{2,1,0:T(8,128)S(1)}, u32[]{:S(2)}, u32[]{:S(2)}) collective-permute-start(f32[2,128,128]{2,1,0:T(8,128)S(1)} %add.16), channel_id=1, source_target_pairs={{0,2},{1,3},{2,0},{3,1},{4,6},{5,7},{6,4},{7,5},{8,10},{9,11},{10,... | collective-permute-start | bytes 393224 | tf_op jit(solution)/shard_map/ppermute | solution.py:237
  22.8 0.5 %collective-permute-start.7 = (f32[1,128,128]{2,1,0:T(8,128)S(1)}, f32[1,128,128]{2,1,0:T(8,128)S(1)}, u32[]{:S(2)}, u32[]{:S(2)}) collective-permute-start(f32[1,128,128]{2,1,0:T(8,128)S(1)} %add.15), channel_id=1, source_target_pairs={{0,2},{1,3},{2,0},{3,1},{4,6},{5,7},{6,4},{7,5},{8,10},{9,11},{10,... | collective-permute-start | bytes 196616 | tf_op jit(solution)/shard_map/ppermute | solution.py:237
  23.3 0.3 collective-permute-done.4.refs_0_
  23.6 0.3 shard_map.80
  23.9 0.1 collective-permute-start.5
  24.0 1.2 %collective-permute-done.5 = f32[1,128,128]{2,1,0:T(8,128)S(1)} collective-permute-done((f32[1,128,128]{2,1,0:T(8,128)S(1)}, f32[1,128,128]{2,1,0:T(8,128)S(1)}, u32[]{:S(2)}, u32[]{:S(2)}) %collective-permute-start.5) | collective-permute-done | bytes 65568 | tf_op jit(solution)/shard_map/ppermute | solution.py:234
  25.3 1.6 %collective-permute-start.6 = (f32[1,128,128]{2,1,0:T(8,128)S(1)}, f32[1,128,128]{2,1,0:T(8,128)S(1)}, u32[]{:S(2)}, u32[]{:S(2)}) collective-permute-start(f32[1,128,128]{2,1,0:T(8,128)S(1)} %add.17.own), channel_id=1, source_target_pairs={{0,2},{1,3},{2,0},{3,1},{4,6},{5,7},{6,4},{7,5},{8,10},{9,11},{10,... | collective-permute-start | bytes 196616 | tf_op jit(solution)/shard_map/ppermute | solution.py:237
  26.8 1.5 %collective-permute-done.7 = f32[1,128,128]{2,1,0:T(8,128)S(1)} collective-permute-done((f32[1,128,128]{2,1,0:T(8,128)S(1)}, f32[1,128,128]{2,1,0:T(8,128)S(1)}, u32[]{:S(2)}, u32[]{:S(2)}) %collective-permute-start.7) | collective-permute-done | bytes 65568 | tf_op jit(solution)/shard_map/ppermute | solution.py:237
  28.3 0.0 collective-permute-done.8
  28.3 1.0 %shard_map.81 = (f32[3,128,128]{2,1,0:T(8,128)S(1)}, f32[3,128,128]{2,1,0:T(8,128)S(1)}, f32[8,128]{1,0:T(8,128)S(1)}) custom-call(f32[3,128,128]{2,1,0:T(8,128)S(1)} %pad_maximum_fusion.own, f32[3,128,128]{2,1,0:T(8,128)S(1)} %pad_maximum_fusion.1.other, f32[4,128,128]{2,1,0:T(8,128)S(1)} %get-tuple-element.17.valid, ...), custom_call_target="tpu_custom_call" | custom-call | tf_op jit(solution)/shard_map/pallas_call | solution.py:271
  29.4 0.3 collective-permute-done.6.other
  29.6 0.5 %shard_map.82 = (f32[1,128,128]{2,1,0:T(8,128)S(1)}, f32[2,128,128]{2,1,0:T(8,128)S(1)}, f32[2,128,128]{2,1,0:T(8,128)S(1)}, f32[8,128]{1,0:T(8,128)S(1)}) custom-call(f32[1,128,128]{2,1,0:T(8,128)S(1)} %add.17.own, f32[1,128,128]{2,1,0:T(8,128)S(1)} %collective-permute-done.6.other, f32[4,128,128]{2,1,0:T(8,128)S(1)} %get-tuple-element.17.valid, ...), custom_call_target="tpu_custom_call" | custom-call | tf_op jit(solution)/shard_map/pallas_call | solution.py:286
  30.2 0.1 collective-permute-start.11
  30.3 1.7 %collective-permute-start.9 = (f32[8,128]{1,0:T(8,128)S(1)}, f32[8,128]{1,0:T(8,128)S(1)}, u32[]{:S(2)}, u32[]{:S(2)}) collective-permute-start(f32[8,128]{1,0:T(8,128)S(1)} %get-tuple-element.27), channel_id=1, source_target_pairs={{0,4},{4,0},{8,12},{12,8},{1,5},{5,1},{9,13},{13,9},{2,6},{6,2},{1... | collective-permute-start | bytes 12296 | tf_op jit(solution)/shard_map/ppermute | solution.py:225
  32.0 0.0 collective-permute-done.11
  32.0 1.6 %collective-permute-start.12 = (f32[2,128,128]{2,1,0:T(8,128)S(1)}, f32[2,128,128]{2,1,0:T(8,128)S(1)}, u32[]{:S(2)}, u32[]{:S(2)}) collective-permute-start(f32[2,128,128]{2,1,0:T(8,128)S(1)} %add.18), channel_id=1, source_target_pairs={{0,2},{1,3},{2,0},{3,1},{4,6},{5,7},{6,4},{7,5},{8,10},{9,11},{10,... | collective-permute-start | bytes 393224 | tf_op jit(solution)/shard_map/ppermute | solution.py:237
  33.6 0.4 collective-permute-done.9
  33.9 2.1 %collective-permute-start.10 = (f32[16,128]{1,0:T(8,128)S(1)}, f32[16,128]{1,0:T(8,128)S(1)}, u32[]{:S(2)}, u32[]{:S(2)}) collective-permute-start(f32[16,128]{1,0:T(8,128)S(1)} %constant_dynamic-update-slice_fusion.near), channel_id=1, source_target_pairs={{0,8},{8,0},{4,12},{12,4},{1,9},{9,1},{5,13},{13,5},{2,10},{10,2},... | collective-permute-start | bytes 24584 | tf_op jit(solution)/shard_map/ppermute | solution.py:228
  36.1 1.6 %collective-permute-done.12 = f32[2,128,128]{2,1,0:T(8,128)S(1)} collective-permute-done((f32[2,128,128]{2,1,0:T(8,128)S(1)}, f32[2,128,128]{2,1,0:T(8,128)S(1)}, u32[]{:S(2)}, u32[]{:S(2)}) %collective-permute-start.12) | collective-permute-done | bytes 131104 | tf_op jit(solution)/shard_map/ppermute | solution.py:237
  37.7 0.1 collective-permute-start.13
  37.7 0.8 %collective-permute-done.10.far = f32[16,128]{1,0:T(8,128)S(1)} collective-permute-done((f32[16,128]{1,0:T(8,128)S(1)}, f32[16,128]{1,0:T(8,128)S(1)}, u32[]{:S(2)}, u32[]{:S(2)}) %collective-permute-start.10) | collective-permute-done | bytes 8224 | tf_op jit(solution)/shard_map/ppermute | solution.py:228
  38.5 0.1 shard_map.83.scalars
  38.6 0.5 %collective-permute-done.13.others = f32[2,128,128]{2,1,0:T(8,128)S(1)} collective-permute-done((f32[2,128,128]{2,1,0:T(8,128)S(1)}, f32[2,128,128]{2,1,0:T(8,128)S(1)}, u32[]{:S(2)}, u32[]{:S(2)}) %collective-permute-start.13) | collective-permute-done | bytes 131104 | tf_op jit(solution)/shard_map/ppermute | solution.py:234
  39.1 0.8 %shard_map.84 = (f32[128,512]{1,0:T(8,128)}, f32[1]{0:T(128)}) custom-call(f32[4,128,128]{2,1,0:T(8,128)S(1)} %get-tuple-element.17.valid, f32[8,128]{1,0:T(8,128)S(1)} %shard_map.83.scalars, f32[2,128,128]{2,1,0:T(8,128)S(1)} %add.19.total, f32[2,128,128]{2,1,0:T(8,128)S(1)} %collective-permute-done.13.others, ...), custom_call_target="tpu_custom_call" | custom-call | tf_op jit(solution)/shard_map/pallas_call | solution.py:301
  (9 shorter events, 0.1 us)
Async XLA Ops:
  0.6 17.0 %copy-start = (f32[4,128,128]{2,1,0:T(8,128)S(1)}, f32[4,128,128]{2,1,0:T(8,128)}, u32[]{:S(2)}) copy-start(f32[4,128,128]{2,1,0:T(8,128)} %refs_0_.3) | copy-start | bytes 786436
  0.6 12.5 %collective-permute-start = (f32[4,128,128]{2,1,0:T(8,128)}, f32[4,128,128]{2,1,0:T(8,128)S(1)}, u32[]{:S(2)}, u32[]{:S(2)}) collective-permute-start(f32[4,128,128]{2,1,0:T(8,128)} %refs_0_.3), channel_id=1, source_target_pairs={{0,12},{12,0},{4,8},{8,4},{1,13},{13,1},{5,9},{9,5},{2,14},{14,2},... | collective-permute-start | bytes 786440 | tf_op jit(solution)/shard_map/ppermute | solution.py:231
  5.8 13.5 %collective-permute-start.2 = (f32[4,128,128]{2,1,0:T(8,128)}, f32[4,128,128]{2,1,0:T(8,128)S(1)}, u32[]{:S(2)}, u32[]{:S(2)}) collective-permute-start(f32[4,128,128]{2,1,0:T(8,128)} %refs_0_.3), channel_id=1, source_target_pairs={{0,4},{4,0},{8,12},{12,8},{1,5},{5,1},{9,13},{13,9},{2,6},{6,2},{1... | collective-permute-start | bytes 786440 | tf_op jit(solution)/shard_map/ppermute | solution.py:225
  5.8 1.0 %copy-start.1 = (f32[128,512]{1,0:T(8,128)S(1)}, f32[128,512]{1,0:T(8,128)}, u32[]{:S(2)}) copy-start(f32[128,512]{1,0:T(8,128)} %wave.1) | copy-start | bytes 786436
  6.7 0.9 %copy-start.2 = (f32[4,128,128]{2,1,0:T(8,128)S(1)}, f32[4,128,128]{2,1,0:T(8,128)}, u32[]{:S(2)}) copy-start(f32[4,128,128]{2,1,0:T(8,128)} %left.1) | copy-start | bytes 786436
  7.7 0.7 %copy-start.3 = (s32[4,4]{1,0:T(4,128)S(1)}, s32[4,4]{1,0:T(4,128)}, u32[]{:S(2)}) copy-start(s32[4,4]{1,0:T(4,128)} %pairs.1) | copy-start | bytes 196
  8.3 0.7 %copy-start.4 = (s32[4]{0:T(128)S(1)}, s32[4]{0:T(128)}, u32[]{:S(2)}) copy-start(s32[4]{0:T(128)} %left_sizes.1) | copy-start | bytes 52
  9.0 0.7 %copy-start.5 = (s32[4]{0:T(128)S(1)}, s32[4]{0:T(128)}, u32[]{:S(2)}) copy-start(s32[4]{0:T(128)} %right_sizes.1) | copy-start | bytes 52
  13.2 10.4 %collective-permute-start.4 = (f32[4,128,128]{2,1,0:T(8,128)S(1)}, f32[4,128,128]{2,1,0:T(8,128)S(1)}, u32[]{:S(2)}, u32[]{:S(2)}) collective-permute-start(f32[4,128,128]{2,1,0:T(8,128)S(1)} %collective-permute-done.refs_1_.refs_2_), channel_id=1, source_target_pairs={{0,4},{4,0},{8,12},{12,8},{1,5},{5,1},{9,13},{13,9},{2,6},{6,2},{1... | collective-permute-start | bytes 786440 | tf_op jit(solution)/shard_map/ppermute | solution.py:225
  17.9 1.3 %collective-permute-start.1 = (f32[1,128,128]{2,1,0:T(8,128)S(1)}, f32[1,128,128]{2,1,0:T(8,128)S(1)}, u32[]{:S(2)}, u32[]{:S(2)}) collective-permute-start(f32[1,128,128]{2,1,0:T(8,128)S(1)} %shard_map.78), channel_id=1, source_target_pairs={{0,1},{1,0},{2,3},{3,2},{4,5},{5,4},{6,7},{7,6},{8,9},{9,8},{10,11... | collective-permute-start | bytes 196616 | tf_op jit(solution)/shard_map/ppermute | solution.py:234
  19.8 1.4 %collective-permute-start.3 = (f32[2,128,128]{2,1,0:T(8,128)S(1)}, f32[2,128,128]{2,1,0:T(8,128)S(1)}, u32[]{:S(2)}, u32[]{:S(2)}) collective-permute-start(f32[2,128,128]{2,1,0:T(8,128)S(1)} %shard_map.79), channel_id=1, source_target_pairs={{0,1},{1,0},{2,3},{3,2},{4,5},{5,4},{6,7},{7,6},{8,9},{9,8},{10,11... | collective-permute-start | bytes 393224 | tf_op jit(solution)/shard_map/ppermute | solution.py:234
  21.2 7.1 %collective-permute-start.8 = (f32[2,128,128]{2,1,0:T(8,128)S(1)}, f32[2,128,128]{2,1,0:T(8,128)S(1)}, u32[]{:S(2)}, u32[]{:S(2)}) collective-permute-start(f32[2,128,128]{2,1,0:T(8,128)S(1)} %add.16), channel_id=1, source_target_pairs={{0,2},{1,3},{2,0},{3,1},{4,6},{5,7},{6,4},{7,5},{8,10},{9,11},{10,... | collective-permute-start | bytes 393224 | tf_op jit(solution)/shard_map/ppermute | solution.py:237
  22.8 5.5 %collective-permute-start.7 = (f32[1,128,128]{2,1,0:T(8,128)S(1)}, f32[1,128,128]{2,1,0:T(8,128)S(1)}, u32[]{:S(2)}, u32[]{:S(2)}) collective-permute-start(f32[1,128,128]{2,1,0:T(8,128)S(1)} %add.15), channel_id=1, source_target_pairs={{0,2},{1,3},{2,0},{3,1},{4,6},{5,7},{6,4},{7,5},{8,10},{9,11},{10,... | collective-permute-start | bytes 196616 | tf_op jit(solution)/shard_map/ppermute | solution.py:237
  23.9 1.3 %collective-permute-start.5 = (f32[1,128,128]{2,1,0:T(8,128)S(1)}, f32[1,128,128]{2,1,0:T(8,128)S(1)}, u32[]{:S(2)}, u32[]{:S(2)}) collective-permute-start(f32[1,128,128]{2,1,0:T(8,128)S(1)} %shard_map.80), channel_id=1, source_target_pairs={{0,1},{1,0},{2,3},{3,2},{4,5},{5,4},{6,7},{7,6},{8,9},{9,8},{10,11... | collective-permute-start | bytes 196616 | tf_op jit(solution)/shard_map/ppermute | solution.py:234
  25.3 4.4 %collective-permute-start.6 = (f32[1,128,128]{2,1,0:T(8,128)S(1)}, f32[1,128,128]{2,1,0:T(8,128)S(1)}, u32[]{:S(2)}, u32[]{:S(2)}) collective-permute-start(f32[1,128,128]{2,1,0:T(8,128)S(1)} %add.17.own), channel_id=1, source_target_pairs={{0,2},{1,3},{2,0},{3,1},{4,6},{5,7},{6,4},{7,5},{8,10},{9,11},{10,... | collective-permute-start | bytes 196616 | tf_op jit(solution)/shard_map/ppermute | solution.py:237
  30.2 1.8 %collective-permute-start.11 = (f32[2,128,128]{2,1,0:T(8,128)S(1)}, f32[2,128,128]{2,1,0:T(8,128)S(1)}, u32[]{:S(2)}, u32[]{:S(2)}) collective-permute-start(f32[2,128,128]{2,1,0:T(8,128)S(1)} %get-tuple-element.29), channel_id=1, source_target_pairs={{0,1},{1,0},{2,3},{3,2},{4,5},{5,4},{6,7},{7,6},{8,9},{9,8},{10,11... | collective-permute-start | bytes 393224 | tf_op jit(solution)/shard_map/ppermute | solution.py:234
  30.3 3.7 %collective-permute-start.9 = (f32[8,128]{1,0:T(8,128)S(1)}, f32[8,128]{1,0:T(8,128)S(1)}, u32[]{:S(2)}, u32[]{:S(2)}) collective-permute-start(f32[8,128]{1,0:T(8,128)S(1)} %get-tuple-element.27), channel_id=1, source_target_pairs={{0,4},{4,0},{8,12},{12,8},{1,5},{5,1},{9,13},{13,9},{2,6},{6,2},{1... | collective-permute-start | bytes 12296 | tf_op jit(solution)/shard_map/ppermute | solution.py:225
  32.0 5.6 %collective-permute-start.12 = (f32[2,128,128]{2,1,0:T(8,128)S(1)}, f32[2,128,128]{2,1,0:T(8,128)S(1)}, u32[]{:S(2)}, u32[]{:S(2)}) collective-permute-start(f32[2,128,128]{2,1,0:T(8,128)S(1)} %add.18), channel_id=1, source_target_pairs={{0,2},{1,3},{2,0},{3,1},{4,6},{5,7},{6,4},{7,5},{8,10},{9,11},{10,... | collective-permute-start | bytes 393224 | tf_op jit(solution)/shard_map/ppermute | solution.py:237
  33.9 4.5 %collective-permute-start.10 = (f32[16,128]{1,0:T(8,128)S(1)}, f32[16,128]{1,0:T(8,128)S(1)}, u32[]{:S(2)}, u32[]{:S(2)}) collective-permute-start(f32[16,128]{1,0:T(8,128)S(1)} %constant_dynamic-update-slice_fusion.near), channel_id=1, source_target_pairs={{0,8},{8,0},{4,12},{12,4},{1,9},{9,1},{5,13},{13,5},{2,10},{10,2},... | collective-permute-start | bytes 24584 | tf_op jit(solution)/shard_map/ppermute | solution.py:228
  37.7 1.4 %collective-permute-start.13 = (f32[2,128,128]{2,1,0:T(8,128)S(1)}, f32[2,128,128]{2,1,0:T(8,128)S(1)}, u32[]{:S(2)}, u32[]{:S(2)}) collective-permute-start(f32[2,128,128]{2,1,0:T(8,128)S(1)} %add.19.total), channel_id=1, source_target_pairs={{0,1},{1,0},{2,3},{3,2},{4,5},{5,4},{6,7},{7,6},{8,9},{9,8},{10,11... | collective-permute-start | bytes 393224 | tf_op jit(solution)/shard_map/ppermute | solution.py:234

commit v8 on v7

--- a/solution.py
+++ b/solution.py
@@ -94,7 +94,7 @@
     return jnp.concatenate([blocks[w] for w in range(blocks.shape[0])], axis=1)
 
 
-def half_body(left_sizes, right_sizes, pairs, wave, left, vector, halfway, factors, valid):
+def half_body(left_sizes, right_sizes, pairs, wave, left, right, vector, halfway, factors, valid, own):
     sector = lax.axis_index("sector")
     channels, rows, _ = left.shape
     slots, _, inner = halfway.shape
@@ -110,6 +110,7 @@
             halfway[k, :, w * cols : (w + 1) * cols] = part[
                 w * rows : (w + 1) * rows, k * cols : (k + 1) * cols
             ]
+    own[0] = times_turned(halfway[0], channel_row(right))
 
 
 def first_body(slots, halfway, *refs):
@@ -244,17 +245,18 @@
 
     right_near = near(right)
     right_mirror = mirror(right)
-    vector, halfway, factors, valid = call(
+    vector, halfway, factors, valid, own = call(
         half_body,
         [
             shape(sectors, rows, cols),
             shape(sectors, rows, channels * cols),
             shape(channels * rows, 3 * rows, of=BF16),
             shape(sectors, rows, cols),
+            shape(1, rows, cols),
         ],
         3,
-        2,
-    )(left_sizes, right_sizes, pairs, wave, left)
+        3,
+    )(left_sizes, right_sizes, pairs, wave, left, right)
     right_far = near(after(right_mirror, halfway))
 
     def partials(slots, halfway, *rights):
@@ -265,7 +267,7 @@
     def chip_sum(x):
         return x + core(x)
 
-    one = chip_sum(after(partials((0,), halfway, right), right_mirror))
+    one = chip_sum(after(own, right_mirror))
     two = chip_sum(partials((1, 2), after(halfway, one), right_near, right_mirror))
     three = chip_sum(partials((3,), after(halfway, two), right_far))
     image_early, second_early, sums = call(

time: 40.1 us -> 40.1 us (level)
  local copies, waits for them, and re-layouts: 3.9 us -> 4.91 us
  waiting for transfers between devices: 11.2 us -> 10.3 us
    ppermute x1, waiting for transfers between devices: 2.3 us -> 1.09 us  [mirror(): return lax.ppermute(x, 'sector', [(0, 3), (3, 0), (1, 2), (2, 1)])]
    unnamed x13 -> x15, local copies, waits for them, and re-layouts: 3.9 us -> 4.91 us
    pallas_call x3 -> x2, Pallas kernels: 1.15 us -> 0.82 us  [partials(): call(functools.partial(first_body, slots), [shape(len(slots), rows, cols)...]
where the time goes in v8:
time: 40.1 us; the launch traced here: 39.8 us
  starting transfers between devices  19.1 us (48%)
  waiting for transfers between devices  10.3 us (26%)
  local copies, waits for them, and re-layouts  4.91 us (12%)
  Pallas kernels  4.71 us (12%)
  between operations  0.75 us (2%)
    ppermute x3, starting transfers between devices, near(): return lax.ppermute(x, 'sector', [(0, 1), (1, 0), (2, 3), (3, 2)])  6.16 us
    ppermute x4, starting transfers between devices, across(): return lax.ppermute(x, 'mpo', [(0, 2), (1, 3), (2, 0), (3, 1)])  5.21 us
    ppermute x1, starting transfers between devices, mirror(): return lax.ppermute(x, 'sector', [(0, 3), (3, 0), (1, 2), (2, 1)])  5.11 us
    unnamed x15, local copies, waits for them, and re-layouts  4.91 us
    ppermute x5, waiting for transfers between devices, core(): return lax.ppermute(x, 'mpo', [(0, 1), (1, 0), (2, 3), (3, 2)])  4.17 us
    ppermute x4, waiting for transfers between devices, across(): return lax.ppermute(x, 'mpo', [(0, 2), (1, 3), (2, 0), (3, 1)])  3.24 us
    ppermute x1, starting transfers between devices, far(): return lax.ppermute(x, 'sector', [(0, 2), (2, 0), (1, 3), (3, 1)])  2.18 us
    pallas_call x1, Pallas kernels, line_device(): call(half_body, [shape(sectors, rows, cols), shape(sectors, rows, channel...  1.43 us
  transfers between devices with their start and end apart: 14, of which 11 were waited for; matrix products, arithmetic and copies ran while one was open for 0% of the time, Pallas kernels for 9%

profile of v8, /device:TPU:0, one launch (start us, length us, event | category | flops | bytes accessed | tf_op | source)
XLA Modules:
  0.0 39.8 jit_solution(8622988808346739792)
XLA Ops:
  0.6 5.1 %collective-permute-start = (f32[4,128,128]{2,1,0:T(8,128)}, f32[4,128,128]{2,1,0:T(8,128)S(1)}, u32[]{:S(2)}, u32[]{:S(2)}) collective-permute-start(f32[4,128,128]{2,1,0:T(8,128)} %refs_0_.1), channel_id=1, source_target_pairs={{0,12},{12,0},{4,8},{8,4},{1,13},{13,1},{5,9},{9,5},{2,14},{14,2},... | collective-permute-start | bytes 786440 | tf_op jit(solution)/shard_map/ppermute | solution.py:232
  5.7 0.0 collective-permute-start.2
  5.7 0.0 copy-start
  5.8 1.0 %copy-done = f32[4,128,128]{2,1,0:T(8,128)S(1)} copy-done((f32[4,128,128]{2,1,0:T(8,128)S(1)}, f32[4,128,128]{2,1,0:T(8,128)}, u32[]{:S(2)}) %copy-start) | copy-done | bytes 262168
  6.8 0.0 copy-start.2
  6.8 0.9 %copy-done.2 = f32[128,512]{1,0:T(8,128)S(1)} copy-done((f32[128,512]{1,0:T(8,128)S(1)}, f32[128,512]{1,0:T(8,128)}, u32[]{:S(2)}) %copy-start.2) | copy-done | bytes 262168
  7.7 0.0 copy-start.3
  7.7 0.9 %copy-done.3 = f32[4,128,128]{2,1,0:T(8,128)S(1)} copy-done((f32[4,128,128]{2,1,0:T(8,128)S(1)}, f32[4,128,128]{2,1,0:T(8,128)}, u32[]{:S(2)}) %copy-start.3) | copy-done | bytes 262168
  8.7 0.0 copy-start.4
  8.7 0.7 %copy-done.4 = s32[4,4]{1,0:T(4,128)S(1)} copy-done((s32[4,4]{1,0:T(4,128)S(1)}, s32[4,4]{1,0:T(4,128)}, u32[]{:S(2)}) %copy-start.4) | copy-done | bytes 88
  9.3 0.0 copy-start.5
  9.3 0.7 %copy-done.5 = s32[4]{0:T(128)S(1)} copy-done((s32[4]{0:T(128)S(1)}, s32[4]{0:T(128)}, u32[]{:S(2)}) %copy-start.5) | copy-done | bytes 40
  10.0 0.7 %copy-done.6 = s32[4]{0:T(128)S(1)} copy-done((s32[4]{0:T(128)S(1)}, s32[4]{0:T(128)}, u32[]{:S(2)}) %copy-start.6) | copy-done | bytes 40
  10.7 1.4 %shard_map.77 = (f32[4,128,128]{2,1,0:T(8,128)S(1)}, f32[4,128,512]{2,1,0:T(8,128)S(1)}, bf16[512,384]{1,0:T(8,128)(2,1)S(1)}, f32[4,128,128]{2,1,0:T(8,128)S(1)}, f32[1,128,128]{2,1,0:T(8,128)S(1)}) custom-call(s32[4]{0:T(128)S(1)} %copy-done.5, s32[4]{0:T(128)S(1)} %copy-done.6, s32[4,4]{1,0:T(4,128)S(1)} %copy-done.4, f32[128,512]{1,0:T(8,128)S(1)} %copy-done.2, ...), custom_call_target="tpu_custom_call" | custom-call | tf_op jit(solution)/shard_map/pallas_call | solution.py:248
  12.1 1.1 %collective-permute-done.refs_1_.refs_2_ = f32[4,128,128]{2,1,0:T(8,128)S(1)} collective-permute-done((f32[4,128,128]{2,1,0:T(8,128)}, f32[4,128,128]{2,1,0:T(8,128)S(1)}, u32[]{:S(2)}, u32[]{:S(2)}) %collective-permute-start) | collective-permute-done | bytes 262176 | tf_op jit(solution)/shard_map/ppermute | solution.py:232
  13.2 4.4 %collective-permute-start.4 = (f32[4,128,128]{2,1,0:T(8,128)S(1)}, f32[4,128,128]{2,1,0:T(8,128)S(1)}, u32[]{:S(2)}, u32[]{:S(2)}) collective-permute-start(f32[4,128,128]{2,1,0:T(8,128)S(1)} %collective-permute-done.refs_1_.refs_2_), channel_id=1, source_target_pairs={{0,4},{4,0},{8,12},{12,8},{1,5},{5,1},{9,13},{13,9},{2,6},{6,2},{1... | collective-permute-start | bytes 786440 | tf_op jit(solution)/shard_map/ppermute | solution.py:226
  17.6 0.0 collective-permute-start.1
  17.6 1.3 %collective-permute-done.1 = f32[1,128,128]{2,1,0:T(8,128)S(1)} collective-permute-done((f32[1,128,128]{2,1,0:T(8,128)S(1)}, f32[1,128,128]{2,1,0:T(8,128)S(1)}, u32[]{:S(2)}, u32[]{:S(2)}) %collective-permute-start.1) | collective-permute-done | bytes 65568 | tf_op jit(solution)/shard_map/ppermute | solution.py:235
  18.9 0.0 collective-permute-done.2.refs_0_.refs_1_
  18.9 0.5 %shard_map.78 = f32[2,128,128]{2,1,0:T(8,128)S(1)} custom-call(f32[4,128,512]{2,1,0:T(8,128)S(1)} %get-tuple-element.23.halfway, f32[4,128,128]{2,1,0:T(8,128)S(1)} %collective-permute-done.2.refs_0_.refs_1_, f32[4,128,128]{2,1,0:T(8,128)S(1)} %collective-permute-done.refs_1_.refs_2_), custom_call_target="tpu_custom_call" | custom-call | tf_op jit(solution)/shard_map/pallas_call | solution.py:263
  19.4 0.2 collective-permute-start.3
  19.6 1.2 %collective-permute-done.3 = f32[2,128,128]{2,1,0:T(8,128)S(1)} collective-permute-done((f32[2,128,128]{2,1,0:T(8,128)S(1)}, f32[2,128,128]{2,1,0:T(8,128)S(1)}, u32[]{:S(2)}, u32[]{:S(2)}) %collective-permute-start.3) | collective-permute-done | bytes 131104 | tf_op jit(solution)/shard_map/ppermute | solution.py:235
  20.8 1.5 %collective-permute-start.8 = (f32[2,128,128]{2,1,0:T(8,128)S(1)}, f32[2,128,128]{2,1,0:T(8,128)S(1)}, u32[]{:S(2)}, u32[]{:S(2)}) collective-permute-start(f32[2,128,128]{2,1,0:T(8,128)S(1)} %add.16), channel_id=1, source_target_pairs={{0,2},{1,3},{2,0},{3,1},{4,6},{5,7},{6,4},{7,5},{8,10},{9,11},{10,... | collective-permute-start | bytes 393224 | tf_op jit(solution)/shard_map/ppermute | solution.py:238
  22.3 0.5 %collective-permute-start.7 = (f32[1,128,128]{2,1,0:T(8,128)S(1)}, f32[1,128,128]{2,1,0:T(8,128)S(1)}, u32[]{:S(2)}, u32[]{:S(2)}) collective-permute-start(f32[1,128,128]{2,1,0:T(8,128)S(1)} %add.15), channel_id=1, source_target_pairs={{0,2},{1,3},{2,0},{3,1},{4,6},{5,7},{6,4},{7,5},{8,10},{9,11},{10,... | collective-permute-start | bytes 196616 | tf_op jit(solution)/shard_map/ppermute | solution.py:238
  22.9 0.7 %collective-permute-done.4.refs_0_ = f32[4,128,128]{2,1,0:T(8,128)S(1)} collective-permute-done((f32[4,128,128]{2,1,0:T(8,128)S(1)}, f32[4,128,128]{2,1,0:T(8,128)S(1)}, u32[]{:S(2)}, u32[]{:S(2)}) %collective-permute-start.4) | collective-permute-done | bytes 262176 | tf_op jit(solution)/shard_map/ppermute | solution.py:226
  23.6 0.3 shard_map.79
  23.9 0.1 collective-permute-start.5
  24.0 0.0 copy-start.1
  24.1 1.2 %collective-permute-done.5 = f32[1,128,128]{2,1,0:T(8,128)S(1)} collective-permute-done((f32[1,128,128]{2,1,0:T(8,128)S(1)}, f32[1,128,128]{2,1,0:T(8,128)S(1)}, u32[]{:S(2)}, u32[]{:S(2)}) %collective-permute-start.5) | collective-permute-done | bytes 65568 | tf_op jit(solution)/shard_map/ppermute | solution.py:235
  25.3 1.6 %collective-permute-start.6 = (f32[1,128,128]{2,1,0:T(8,128)S(1)}, f32[1,128,128]{2,1,0:T(8,128)S(1)}, u32[]{:S(2)}, u32[]{:S(2)}) collective-permute-start(f32[1,128,128]{2,1,0:T(8,128)S(1)} %add.17.own), channel_id=1, source_target_pairs={{0,2},{1,3},{2,0},{3,1},{4,6},{5,7},{6,4},{7,5},{8,10},{9,11},{10,... | collective-permute-start | bytes 196616 | tf_op jit(solution)/shard_map/ppermute | solution.py:238
  26.8 1.0 %collective-permute-done.7 = f32[1,128,128]{2,1,0:T(8,128)S(1)} collective-permute-done((f32[1,128,128]{2,1,0:T(8,128)S(1)}, f32[1,128,128]{2,1,0:T(8,128)S(1)}, u32[]{:S(2)}, u32[]{:S(2)}) %collective-permute-start.7) | collective-permute-done | bytes 65568 | tf_op jit(solution)/shard_map/ppermute | solution.py:238
  27.8 0.0 collective-permute-done.8
  27.8 0.0 copy-done.1
  27.9 1.0 %shard_map.80 = (f32[3,128,128]{2,1,0:T(8,128)S(1)}, f32[3,128,128]{2,1,0:T(8,128)S(1)}, f32[8,128]{1,0:T(8,128)S(1)}) custom-call(f32[3,128,128]{2,1,0:T(8,128)S(1)} %pad_maximum_fusion.own, f32[3,128,128]{2,1,0:T(8,128)S(1)} %pad_maximum_fusion.1.other, f32[4,128,128]{2,1,0:T(8,128)S(1)} %get-tuple-element.18.valid, ...), custom_call_target="tpu_custom_call" | custom-call | tf_op jit(solution)/shard_map/pallas_call | solution.py:273
  28.9 0.7 %collective-permute-done.6.other = f32[1,128,128]{2,1,0:T(8,128)S(1)} collective-permute-done((f32[1,128,128]{2,1,0:T(8,128)S(1)}, f32[1,128,128]{2,1,0:T(8,128)S(1)}, u32[]{:S(2)}, u32[]{:S(2)}) %collective-permute-start.6) | collective-permute-done | bytes 65568 | tf_op jit(solution)/shard_map/ppermute | solution.py:238
  29.6 0.5 %shard_map.81 = (f32[1,128,128]{2,1,0:T(8,128)S(1)}, f32[2,128,128]{2,1,0:T(8,128)S(1)}, f32[2,128,128]{2,1,0:T(8,128)S(1)}, f32[8,128]{1,0:T(8,128)S(1)}) custom-call(f32[1,128,128]{2,1,0:T(8,128)S(1)} %add.17.own, f32[1,128,128]{2,1,0:T(8,128)S(1)} %collective-permute-done.6.other, f32[4,128,128]{2,1,0:T(8,128)S(1)} %get-tuple-element.18.valid, ...), custom_call_target="tpu_custom_call" | custom-call | tf_op jit(solution)/shard_map/pallas_call | solution.py:288
  30.1 0.1 collective-permute-start.11
  30.2 1.7 %collective-permute-start.9 = (f32[8,128]{1,0:T(8,128)S(1)}, f32[8,128]{1,0:T(8,128)S(1)}, u32[]{:S(2)}, u32[]{:S(2)}) collective-permute-start(f32[8,128]{1,0:T(8,128)S(1)} %get-tuple-element.29), channel_id=1, source_target_pairs={{0,4},{4,0},{8,12},{12,8},{1,5},{5,1},{9,13},{13,9},{2,6},{6,2},{1... | collective-permute-start | bytes 12296 | tf_op jit(solution)/shard_map/ppermute | solution.py:226
  32.0 0.0 collective-permute-done.11
  32.0 1.6 %collective-permute-start.12 = (f32[2,128,128]{2,1,0:T(8,128)S(1)}, f32[2,128,128]{2,1,0:T(8,128)S(1)}, u32[]{:S(2)}, u32[]{:S(2)}) collective-permute-start(f32[2,128,128]{2,1,0:T(8,128)S(1)} %add.18), channel_id=1, source_target_pairs={{0,2},{1,3},{2,0},{3,1},{4,6},{5,7},{6,4},{7,5},{8,10},{9,11},{10,... | collective-permute-start | bytes 393224 | tf_op jit(solution)/shard_map/ppermute | solution.py:238
  33.5 0.3 collective-permute-done.9
  33.9 2.2 %collective-permute-start.10 = (f32[16,128]{1,0:T(8,128)S(1)}, f32[16,128]{1,0:T(8,128)S(1)}, u32[]{:S(2)}, u32[]{:S(2)}) collective-permute-start(f32[16,128]{1,0:T(8,128)S(1)} %constant_dynamic-update-slice_fusion.near), channel_id=1, source_target_pairs={{0,8},{8,0},{4,12},{12,4},{1,9},{9,1},{5,13},{13,5},{2,10},{10,2},... | collective-permute-start | bytes 24584 | tf_op jit(solution)/shard_map/ppermute | solution.py:229
  36.1 1.5 %collective-permute-done.12 = f32[2,128,128]{2,1,0:T(8,128)S(1)} collective-permute-done((f32[2,128,128]{2,1,0:T(8,128)S(1)}, f32[2,128,128]{2,1,0:T(8,128)S(1)}, u32[]{:S(2)}, u32[]{:S(2)}) %collective-permute-start.12) | collective-permute-done | bytes 131104 | tf_op jit(solution)/shard_map/ppermute | solution.py:238
  37.6 0.1 collective-permute-start.13
  37.7 0.7 %collective-permute-done.10.far = f32[16,128]{1,0:T(8,128)S(1)} collective-permute-done((f32[16,128]{1,0:T(8,128)S(1)}, f32[16,128]{1,0:T(8,128)S(1)}, u32[]{:S(2)}, u32[]{:S(2)}) %collective-permute-start.10) | collective-permute-done | bytes 8224 | tf_op jit(solution)/shard_map/ppermute | solution.py:229
  38.4 0.1 shard_map.82.scalars
  38.5 0.5 %collective-permute-done.13.others = f32[2,128,128]{2,1,0:T(8,128)S(1)} collective-permute-done((f32[2,128,128]{2,1,0:T(8,128)S(1)}, f32[2,128,128]{2,1,0:T(8,128)S(1)}, u32[]{:S(2)}, u32[]{:S(2)}) %collective-permute-start.13) | collective-permute-done | bytes 131104 | tf_op jit(solution)/shard_map/ppermute | solution.py:235
  39.1 0.8 %shard_map.83 = (f32[128,512]{1,0:T(8,128)}, f32[1]{0:T(128)}) custom-call(f32[4,128,128]{2,1,0:T(8,128)S(1)} %get-tuple-element.18.valid, f32[8,128]{1,0:T(8,128)S(1)} %shard_map.82.scalars, f32[2,128,128]{2,1,0:T(8,128)S(1)} %add.19.total, f32[2,128,128]{2,1,0:T(8,128)S(1)} %collective-permute-done.13.others, ...), custom_call_target="tpu_custom_call" | custom-call | tf_op jit(solution)/shard_map/pallas_call | solution.py:303
  (10 shorter events, 0.1 us)
Async XLA Ops:
  0.6 12.6 %collective-permute-start = (f32[4,128,128]{2,1,0:T(8,128)}, f32[4,128,128]{2,1,0:T(8,128)S(1)}, u32[]{:S(2)}, u32[]{:S(2)}) collective-permute-start(f32[4,128,128]{2,1,0:T(8,128)} %refs_0_.1), channel_id=1, source_target_pairs={{0,12},{12,0},{4,8},{8,4},{1,13},{13,1},{5,9},{9,5},{2,14},{14,2},... | collective-permute-start | bytes 786440 | tf_op jit(solution)/shard_map/ppermute | solution.py:232
  5.7 13.1 %collective-permute-start.2 = (f32[4,128,128]{2,1,0:T(8,128)}, f32[4,128,128]{2,1,0:T(8,128)S(1)}, u32[]{:S(2)}, u32[]{:S(2)}) collective-permute-start(f32[4,128,128]{2,1,0:T(8,128)} %refs_0_.1), channel_id=1, source_target_pairs={{0,4},{4,0},{8,12},{12,8},{1,5},{5,1},{9,13},{13,9},{2,6},{6,2},{1... | collective-permute-start | bytes 786440 | tf_op jit(solution)/shard_map/ppermute | solution.py:226
  5.7 1.0 %copy-start = (f32[4,128,128]{2,1,0:T(8,128)S(1)}, f32[4,128,128]{2,1,0:T(8,128)}, u32[]{:S(2)}) copy-start(f32[4,128,128]{2,1,0:T(8,128)} %refs_0_.1) | copy-start | bytes 786436
  6.8 0.9 %copy-start.2 = (f32[128,512]{1,0:T(8,128)S(1)}, f32[128,512]{1,0:T(8,128)}, u32[]{:S(2)}) copy-start(f32[128,512]{1,0:T(8,128)} %wave.1) | copy-start | bytes 786436
  7.7 0.9 %copy-start.3 = (f32[4,128,128]{2,1,0:T(8,128)S(1)}, f32[4,128,128]{2,1,0:T(8,128)}, u32[]{:S(2)}) copy-start(f32[4,128,128]{2,1,0:T(8,128)} %left.1) | copy-start | bytes 786436
  8.7 0.7 %copy-start.4 = (s32[4,4]{1,0:T(4,128)S(1)}, s32[4,4]{1,0:T(4,128)}, u32[]{:S(2)}) copy-start(s32[4,4]{1,0:T(4,128)} %pairs.1) | copy-start | bytes 196
  9.3 0.7 %copy-start.5 = (s32[4]{0:T(128)S(1)}, s32[4]{0:T(128)}, u32[]{:S(2)}) copy-start(s32[4]{0:T(128)} %left_sizes.1) | copy-start | bytes 52
  10.0 0.7 %copy-start.6 = (s32[4]{0:T(128)S(1)}, s32[4]{0:T(128)}, u32[]{:S(2)}) copy-start(s32[4]{0:T(128)} %right_sizes.1) | copy-start | bytes 52
  13.2 10.4 %collective-permute-start.4 = (f32[4,128,128]{2,1,0:T(8,128)S(1)}, f32[4,128,128]{2,1,0:T(8,128)S(1)}, u32[]{:S(2)}, u32[]{:S(2)}) collective-permute-start(f32[4,128,128]{2,1,0:T(8,128)S(1)} %collective-permute-done.refs_1_.refs_2_), channel_id=1, source_target_pairs={{0,4},{4,0},{8,12},{12,8},{1,5},{5,1},{9,13},{13,9},{2,6},{6,2},{1... | collective-permute-start | bytes 786440 | tf_op jit(solution)/shard_map/ppermute | solution.py:226
  17.6 1.3 %collective-permute-start.1 = (f32[1,128,128]{2,1,0:T(8,128)S(1)}, f32[1,128,128]{2,1,0:T(8,128)S(1)}, u32[]{:S(2)}, u32[]{:S(2)}) collective-permute-start(f32[1,128,128]{2,1,0:T(8,128)S(1)} %get-tuple-element.21), channel_id=1, source_target_pairs={{0,1},{1,0},{2,3},{3,2},{4,5},{5,4},{6,7},{7,6},{8,9},{9,8},{10,11... | collective-permute-start | bytes 196616 | tf_op jit(solution)/shard_map/ppermute | solution.py:235
  19.4 1.4 %collective-permute-start.3 = (f32[2,128,128]{2,1,0:T(8,128)S(1)}, f32[2,128,128]{2,1,0:T(8,128)S(1)}, u32[]{:S(2)}, u32[]{:S(2)}) collective-permute-start(f32[2,128,128]{2,1,0:T(8,128)S(1)} %shard_map.78), channel_id=1, source_target_pairs={{0,1},{1,0},{2,3},{3,2},{4,5},{5,4},{6,7},{7,6},{8,9},{9,8},{10,11... | collective-permute-start | bytes 393224 | tf_op jit(solution)/shard_map/ppermute | solution.py:235
  20.8 7.0 %collective-permute-start.8 = (f32[2,128,128]{2,1,0:T(8,128)S(1)}, f32[2,128,128]{2,1,0:T(8,128)S(1)}, u32[]{:S(2)}, u32[]{:S(2)}) collective-permute-start(f32[2,128,128]{2,1,0:T(8,128)S(1)} %add.16), channel_id=1, source_target_pairs={{0,2},{1,3},{2,0},{3,1},{4,6},{5,7},{6,4},{7,5},{8,10},{9,11},{10,... | collective-permute-start | bytes 393224 | tf_op jit(solution)/shard_map/ppermute | solution.py:238
  22.3 5.5 %collective-permute-start.7 = (f32[1,128,128]{2,1,0:T(8,128)S(1)}, f32[1,128,128]{2,1,0:T(8,128)S(1)}, u32[]{:S(2)}, u32[]{:S(2)}) collective-permute-start(f32[1,128,128]{2,1,0:T(8,128)S(1)} %add.15), channel_id=1, source_target_pairs={{0,2},{1,3},{2,0},{3,1},{4,6},{5,7},{6,4},{7,5},{8,10},{9,11},{10,... | collective-permute-start | bytes 196616 | tf_op jit(solution)/shard_map/ppermute | solution.py:238
  23.9 1.3 %collective-permute-start.5 = (f32[1,128,128]{2,1,0:T(8,128)S(1)}, f32[1,128,128]{2,1,0:T(8,128)S(1)}, u32[]{:S(2)}, u32[]{:S(2)}) collective-permute-start(f32[1,128,128]{2,1,0:T(8,128)S(1)} %shard_map.79), channel_id=1, source_target_pairs={{0,1},{1,0},{2,3},{3,2},{4,5},{5,4},{6,7},{7,6},{8,9},{9,8},{10,11... | collective-permute-start | bytes 196616 | tf_op jit(solution)/shard_map/ppermute | solution.py:235
  24.0 3.8 %copy-start.1 = (f32[4,128,128]{2,1,0:T(8,128)S(1)}, f32[4,128,128]{2,1,0:T(8,128)}, u32[]{:S(2)}) copy-start(f32[4,128,128]{2,1,0:T(8,128)} %refs_0_.1) | copy-start | bytes 786436
  25.3 4.3 %collective-permute-start.6 = (f32[1,128,128]{2,1,0:T(8,128)S(1)}, f32[1,128,128]{2,1,0:T(8,128)S(1)}, u32[]{:S(2)}, u32[]{:S(2)}) collective-permute-start(f32[1,128,128]{2,1,0:T(8,128)S(1)} %add.17.own), channel_id=1, source_target_pairs={{0,2},{1,3},{2,0},{3,1},{4,6},{5,7},{6,4},{7,5},{8,10},{9,11},{10,... | collective-permute-start | bytes 196616 | tf_op jit(solution)/shard_map/ppermute | solution.py:238
  30.1 1.8 %collective-permute-start.11 = (f32[2,128,128]{2,1,0:T(8,128)S(1)}, f32[2,128,128]{2,1,0:T(8,128)S(1)}, u32[]{:S(2)}, u32[]{:S(2)}) collective-permute-start(f32[2,128,128]{2,1,0:T(8,128)S(1)} %get-tuple-element.31), channel_id=1, source_target_pairs={{0,1},{1,0},{2,3},{3,2},{4,5},{5,4},{6,7},{7,6},{8,9},{9,8},{10,11... | collective-permute-start | bytes 393224 | tf_op jit(solution)/shard_map/ppermute | solution.py:235
  30.2 3.7 %collective-permute-start.9 = (f32[8,128]{1,0:T(8,128)S(1)}, f32[8,128]{1,0:T(8,128)S(1)}, u32[]{:S(2)}, u32[]{:S(2)}) collective-permute-start(f32[8,128]{1,0:T(8,128)S(1)} %get-tuple-element.29), channel_id=1, source_target_pairs={{0,4},{4,0},{8,12},{12,8},{1,5},{5,1},{9,13},{13,9},{2,6},{6,2},{1... | collective-permute-start | bytes 12296 | tf_op jit(solution)/shard_map/ppermute | solution.py:226
  32.0 5.6 %collective-permute-start.12 = (f32[2,128,128]{2,1,0:T(8,128)S(1)}, f32[2,128,128]{2,1,0:T(8,128)S(1)}, u32[]{:S(2)}, u32[]{:S(2)}) collective-permute-start(f32[2,128,128]{2,1,0:T(8,128)S(1)} %add.18), channel_id=1, source_target_pairs={{0,2},{1,3},{2,0},{3,1},{4,6},{5,7},{6,4},{7,5},{8,10},{9,11},{10,... | collective-permute-start | bytes 393224 | tf_op jit(solution)/shard_map/ppermute | solution.py:238
  33.9 4.5 %collective-permute-start.10 = (f32[16,128]{1,0:T(8,128)S(1)}, f32[16,128]{1,0:T(8,128)S(1)}, u32[]{:S(2)}, u32[]{:S(2)}) collective-permute-start(f32[16,128]{1,0:T(8,128)S(1)} %constant_dynamic-update-slice_fusion.near), channel_id=1, source_target_pairs={{0,8},{8,0},{4,12},{12,4},{1,9},{9,1},{5,13},{13,5},{2,10},{10,2},... | collective-permute-start | bytes 24584 | tf_op jit(solution)/shard_map/ppermute | solution.py:229
  37.6 1.4 %collective-permute-start.13 = (f32[2,128,128]{2,1,0:T(8,128)S(1)}, f32[2,128,128]{2,1,0:T(8,128)S(1)}, u32[]{:S(2)}, u32[]{:S(2)}) collective-permute-start(f32[2,128,128]{2,1,0:T(8,128)S(1)} %add.19.total), channel_id=1, source_target_pairs={{0,1},{1,0},{2,3},{3,2},{4,5},{5,4},{6,7},{7,6},{8,9},{9,8},{10,11... | collective-permute-start | bytes 393224 | tf_op jit(solution)/shard_map/ppermute | solution.py:235

commit v9 on v7

--- a/solution.py
+++ b/solution.py
@@ -179,7 +179,7 @@
         send[k] = jnp.where(first, everything[2 + k], everything[k])
 
 
-def scalar_body(groups, cells, near, far, scalars):
+def scalar_body(groups, cells, near, far, valid, total, early, late, scalars, done):
     def everyone(read):
         return (read(near, 0) + read(near, 8)) + (read(far, 0) + read(far, 8))
 
@@ -198,7 +198,12 @@
 
     rest = jnp.sum(everyone(every_group(2)), axis=1, keepdims=True) + everyone(gaps)
     scalars[0:1, :] = value
-    scalars[1:2, :] = 1.0 / jnp.sqrt(rest / cells + TINY)
+    scale = 1.0 / jnp.sqrt(rest / cells + TINY)
+    scalars[1:2, :] = scale
+    me = lax.axis_index("mpo") % 2
+    for k, image in enumerate((early[2], late[0])):
+        image = jnp.where(me == 0, early[k], image)
+        done[k] = (total[k] * valid[2 * me + k] - value * image) * scale
 
 
 def last_body(groups, valid, scalars, total, others, *refs):
@@ -211,8 +216,8 @@
     for slots, image in zip(groups, refs[:-2]):
         for k, slot in enumerate(slots):
             b = slot_column(slot, sector)
-            second = jnp.where(me == slot // 2, total[slot % 2], others[slot % 2])
-            product[:, columns(b, cols)] = (second * valid[slot] - value * image[k]) * scale
+            other = (others[slot % 2] * valid[slot] - value * image[k]) * scale
+            product[:, columns(b, cols)] = jnp.where(me == slot // 2, total[slot % 2], other)
 
 
 def line_device(wave, left, right, left_sizes, right_sizes, pairs):
@@ -295,16 +300,20 @@
     sums_far = far(sums_near)
     total = mine + across(mine)
     others = core(total)
-    (scalars,) = call(
-        functools.partial(scalar_body, 2, cells), [shape(8, cols)], 0, 2, flops=3_000_000_000
-    )(sums_near, sums_far)
+    scalars, done = call(
+        functools.partial(scalar_body, 2, cells),
+        [shape(8, cols), shape(2, rows, cols)],
+        0,
+        6,
+        flops=3_000_000_000,
+    )(sums_near, sums_far, valid, total, image_early, image_late)
     product, ritz = pl.pallas_call(
         functools.partial(last_body, (EARLY, LATE)),
         out_shape=[shape(rows, sectors * cols), shape(1)],
         in_specs=[VMEM] * 6,
         out_specs=[VMEM, SMEM],
         compiler_params=PARAMS,
-    )(valid, scalars, total, others, image_early, image_late)
+    )(valid, scalars, done, others, image_early, image_late)
     return product, ritz
 
 

time: 40.1 us -> 40.1 us (level)
  no operation moved by 1% of the time
where the time goes in v9:
time: 40.1 us; the launch traced here: 39.9 us
  starting transfers between devices  19.1 us (48%)
  waiting for transfers between devices  11.1 us (28%)
  Pallas kernels  4.85 us (12%)
  local copies, waits for them, and re-layouts  3.9 us (10%)
  between operations  0.76 us (2%)
    ppermute x3, starting transfers between devices, near(): return lax.ppermute(x, 'sector', [(0, 1), (1, 0), (2, 3), (3, 2)])  6.13 us
    ppermute x4, starting transfers between devices, across(): return lax.ppermute(x, 'mpo', [(0, 2), (1, 3), (2, 0), (3, 1)])  5.21 us
    ppermute x1, starting transfers between devices, mirror(): return lax.ppermute(x, 'sector', [(0, 3), (3, 0), (1, 2), (2, 1)])  5.11 us
    ppermute x5, waiting for transfers between devices, core(): return lax.ppermute(x, 'mpo', [(0, 1), (1, 0), (2, 3), (3, 2)])  4.11 us
    unnamed x13, local copies, waits for them, and re-layouts  3.9 us
    ppermute x4, waiting for transfers between devices, across(): return lax.ppermute(x, 'mpo', [(0, 2), (1, 3), (2, 0), (3, 1)])  3.29 us
    ppermute x1, waiting for transfers between devices, mirror(): return lax.ppermute(x, 'sector', [(0, 3), (3, 0), (1, 2), (2, 1)])  2.3 us
    ppermute x1, starting transfers between devices, far(): return lax.ppermute(x, 'sector', [(0, 2), (2, 0), (1, 3), (3, 1)])  2.14 us
  transfers between devices with their start and end apart: 14, of which 11 were waited for; matrix products, arithmetic and copies ran while one was open for 0% of the time, Pallas kernels for 9%

profile of v9, /device:TPU:0, one launch (start us, length us, event | category | flops | bytes accessed | tf_op | source)
XLA Modules:
  0.0 39.9 jit_solution(15189704935510436579)
XLA Ops:
  0.6 0.0 copy-start
  0.6 5.1 %collective-permute-start = (f32[4,128,128]{2,1,0:T(8,128)}, f32[4,128,128]{2,1,0:T(8,128)S(1)}, u32[]{:S(2)}, u32[]{:S(2)}) collective-permute-start(f32[4,128,128]{2,1,0:T(8,128)} %refs_0_.3), channel_id=1, source_target_pairs={{0,12},{12,0},{4,8},{8,4},{1,13},{13,1},{5,9},{9,5},{2,14},{14,2},... | collective-permute-start | bytes 786440 | tf_op jit(solution)/shard_map/ppermute | solution.py:236
  5.8 0.0 collective-permute-start.2
  5.8 0.0 copy-start.1
  5.8 0.9 %copy-done.1 = f32[128,512]{1,0:T(8,128)S(1)} copy-done((f32[128,512]{1,0:T(8,128)S(1)}, f32[128,512]{1,0:T(8,128)}, u32[]{:S(2)}) %copy-start.1) | copy-done | bytes 262168
  6.7 0.0 copy-start.2
  6.7 0.9 %copy-done.2 = f32[4,128,128]{2,1,0:T(8,128)S(1)} copy-done((f32[4,128,128]{2,1,0:T(8,128)S(1)}, f32[4,128,128]{2,1,0:T(8,128)}, u32[]{:S(2)}) %copy-start.2) | copy-done | bytes 262168
  7.7 0.0 copy-start.3
  7.7 0.7 %copy-done.3 = s32[4,4]{1,0:T(4,128)S(1)} copy-done((s32[4,4]{1,0:T(4,128)S(1)}, s32[4,4]{1,0:T(4,128)}, u32[]{:S(2)}) %copy-start.3) | copy-done | bytes 88
  8.3 0.0 copy-start.4
  8.3 0.7 %copy-done.4 = s32[4]{0:T(128)S(1)} copy-done((s32[4]{0:T(128)S(1)}, s32[4]{0:T(128)}, u32[]{:S(2)}) %copy-start.4) | copy-done | bytes 40
  9.0 0.0 copy-start.5
  9.0 0.7 %copy-done.5 = s32[4]{0:T(128)S(1)} copy-done((s32[4]{0:T(128)S(1)}, s32[4]{0:T(128)}, u32[]{:S(2)}) %copy-start.5) | copy-done | bytes 40
  9.7 1.2 %shard_map.77 = (f32[4,128,128]{2,1,0:T(8,128)S(1)}, f32[4,128,512]{2,1,0:T(8,128)S(1)}, bf16[512,384]{1,0:T(8,128)(2,1)S(1)}, f32[4,128,128]{2,1,0:T(8,128)S(1)}) custom-call(s32[4]{0:T(128)S(1)} %copy-done.4, s32[4]{0:T(128)S(1)} %copy-done.5, s32[4,4]{1,0:T(4,128)S(1)} %copy-done.3, f32[128,512]{1,0:T(8,128)S(1)} %copy-done.1, f32[4,128,128]{2,1,0:T(8,128)S(1)} %copy-done.2), custom_call_target="tpu_custom_call" | custom-call | tf_op jit(solution)/shard_map/pallas_call | solution.py:252
  10.9 2.3 %collective-permute-done.refs_1_.refs_2_ = f32[4,128,128]{2,1,0:T(8,128)S(1)} collective-permute-done((f32[4,128,128]{2,1,0:T(8,128)}, f32[4,128,128]{2,1,0:T(8,128)S(1)}, u32[]{:S(2)}, u32[]{:S(2)}) %collective-permute-start) | collective-permute-done | bytes 262176 | tf_op jit(solution)/shard_map/ppermute | solution.py:236
  13.2 4.4 %collective-permute-start.4 = (f32[4,128,128]{2,1,0:T(8,128)S(1)}, f32[4,128,128]{2,1,0:T(8,128)S(1)}, u32[]{:S(2)}, u32[]{:S(2)}) collective-permute-start(f32[4,128,128]{2,1,0:T(8,128)S(1)} %collective-permute-done.refs_1_.refs_2_), channel_id=1, source_target_pairs={{0,4},{4,0},{8,12},{12,8},{1,5},{5,1},{9,13},{13,9},{2,6},{6,2},{1... | collective-permute-start | bytes 786440 | tf_op jit(solution)/shard_map/ppermute | solution.py:230
  17.6 0.0 copy-done
  17.6 0.3 shard_map.78
  17.9 0.1 collective-permute-start.1
  18.0 1.2 %collective-permute-done.1 = f32[1,128,128]{2,1,0:T(8,128)S(1)} collective-permute-done((f32[1,128,128]{2,1,0:T(8,128)S(1)}, f32[1,128,128]{2,1,0:T(8,128)S(1)}, u32[]{:S(2)}, u32[]{:S(2)}) %collective-permute-start.1) | collective-permute-done | bytes 65568 | tf_op jit(solution)/shard_map/ppermute | solution.py:239
  19.3 0.0 collective-permute-done.2.refs_0_.refs_1_
  19.3 0.5 %shard_map.79 = f32[2,128,128]{2,1,0:T(8,128)S(1)} custom-call(f32[4,128,512]{2,1,0:T(8,128)S(1)} %get-tuple-element.23.halfway, f32[4,128,128]{2,1,0:T(8,128)S(1)} %collective-permute-done.2.refs_0_.refs_1_, f32[4,128,128]{2,1,0:T(8,128)S(1)} %collective-permute-done.refs_1_.refs_2_), custom_call_target="tpu_custom_call" | custom-call | tf_op jit(solution)/shard_map/pallas_call | solution.py:266
  19.8 0.2 collective-permute-start.3
  20.0 1.2 %collective-permute-done.3 = f32[2,128,128]{2,1,0:T(8,128)S(1)} collective-permute-done((f32[2,128,128]{2,1,0:T(8,128)S(1)}, f32[2,128,128]{2,1,0:T(8,128)S(1)}, u32[]{:S(2)}, u32[]{:S(2)}) %collective-permute-start.3) | collective-permute-done | bytes 131104 | tf_op jit(solution)/shard_map/ppermute | solution.py:239
  21.2 1.6 %collective-permute-start.8 = (f32[2,128,128]{2,1,0:T(8,128)S(1)}, f32[2,128,128]{2,1,0:T(8,128)S(1)}, u32[]{:S(2)}, u32[]{:S(2)}) collective-permute-start(f32[2,128,128]{2,1,0:T(8,128)S(1)} %add.16), channel_id=1, source_target_pairs={{0,2},{1,3},{2,0},{3,1},{4,6},{5,7},{6,4},{7,5},{8,10},{9,11},{10,... | collective-permute-start | bytes 393224 | tf_op jit(solution)/shard_map/ppermute | solution.py:242
  22.8 0.5 %collective-permute-start.7 = (f32[1,128,128]{2,1,0:T(8,128)S(1)}, f32[1,128,128]{2,1,0:T(8,128)S(1)}, u32[]{:S(2)}, u32[]{:S(2)}) collective-permute-start(f32[1,128,128]{2,1,0:T(8,128)S(1)} %add.15), channel_id=1, source_target_pairs={{0,2},{1,3},{2,0},{3,1},{4,6},{5,7},{6,4},{7,5},{8,10},{9,11},{10,... | collective-permute-start | bytes 196616 | tf_op jit(solution)/shard_map/ppermute | solution.py:242
  23.3 0.3 collective-permute-done.4.refs_0_
  23.6 0.3 shard_map.80
  23.9 0.1 collective-permute-start.5
  24.0 1.2 %collective-permute-done.5 = f32[1,128,128]{2,1,0:T(8,128)S(1)} collective-permute-done((f32[1,128,128]{2,1,0:T(8,128)S(1)}, f32[1,128,128]{2,1,0:T(8,128)S(1)}, u32[]{:S(2)}, u32[]{:S(2)}) %collective-permute-start.5) | collective-permute-done | bytes 65568 | tf_op jit(solution)/shard_map/ppermute | solution.py:239
  25.3 1.6 %collective-permute-start.6 = (f32[1,128,128]{2,1,0:T(8,128)S(1)}, f32[1,128,128]{2,1,0:T(8,128)S(1)}, u32[]{:S(2)}, u32[]{:S(2)}) collective-permute-start(f32[1,128,128]{2,1,0:T(8,128)S(1)} %add.17.own), channel_id=1, source_target_pairs={{0,2},{1,3},{2,0},{3,1},{4,6},{5,7},{6,4},{7,5},{8,10},{9,11},{10,... | collective-permute-start | bytes 196616 | tf_op jit(solution)/shard_map/ppermute | solution.py:242
  26.8 1.5 %collective-permute-done.7 = f32[1,128,128]{2,1,0:T(8,128)S(1)} collective-permute-done((f32[1,128,128]{2,1,0:T(8,128)S(1)}, f32[1,128,128]{2,1,0:T(8,128)S(1)}, u32[]{:S(2)}, u32[]{:S(2)}) %collective-permute-start.7) | collective-permute-done | bytes 65568 | tf_op jit(solution)/shard_map/ppermute | solution.py:242
  28.3 0.0 collective-permute-done.8
  28.3 1.0 %shard_map.81 = (f32[3,128,128]{2,1,0:T(8,128)S(1)}, f32[3,128,128]{2,1,0:T(8,128)S(1)}, f32[8,128]{1,0:T(8,128)S(1)}) custom-call(f32[3,128,128]{2,1,0:T(8,128)S(1)} %pad_maximum_fusion.own, f32[3,128,128]{2,1,0:T(8,128)S(1)} %pad_maximum_fusion.1.other, f32[4,128,128]{2,1,0:T(8,128)S(1)} %get-tuple-element.19.valid, ...), custom_call_target="tpu_custom_call" | custom-call | tf_op jit(solution)/shard_map/pallas_call | solution.py:276
  29.4 0.3 collective-permute-done.6.other
  29.6 0.5 %shard_map.82 = (f32[1,128,128]{2,1,0:T(8,128)S(1)}, f32[2,128,128]{2,1,0:T(8,128)S(1)}, f32[2,128,128]{2,1,0:T(8,128)S(1)}, f32[8,128]{1,0:T(8,128)S(1)}) custom-call(f32[1,128,128]{2,1,0:T(8,128)S(1)} %add.17.own, f32[1,128,128]{2,1,0:T(8,128)S(1)} %collective-permute-done.6.other, f32[4,128,128]{2,1,0:T(8,128)S(1)} %get-tuple-element.19.valid, ...), custom_call_target="tpu_custom_call" | custom-call | tf_op jit(solution)/shard_map/pallas_call | solution.py:291
  30.2 0.1 collective-permute-start.11
  30.3 1.7 %collective-permute-start.9 = (f32[8,128]{1,0:T(8,128)S(1)}, f32[8,128]{1,0:T(8,128)S(1)}, u32[]{:S(2)}, u32[]{:S(2)}) collective-permute-start(f32[8,128]{1,0:T(8,128)S(1)} %get-tuple-element.29), channel_id=1, source_target_pairs={{0,4},{4,0},{8,12},{12,8},{1,5},{5,1},{9,13},{13,9},{2,6},{6,2},{1... | collective-permute-start | bytes 12296 | tf_op jit(solution)/shard_map/ppermute | solution.py:230
  32.0 0.0 collective-permute-done.11
  32.0 1.6 %collective-permute-start.12 = (f32[2,128,128]{2,1,0:T(8,128)S(1)}, f32[2,128,128]{2,1,0:T(8,128)S(1)}, u32[]{:S(2)}, u32[]{:S(2)}) collective-permute-start(f32[2,128,128]{2,1,0:T(8,128)S(1)} %add.18), channel_id=1, source_target_pairs={{0,2},{1,3},{2,0},{3,1},{4,6},{5,7},{6,4},{7,5},{8,10},{9,11},{10,... | collective-permute-start | bytes 393224 | tf_op jit(solution)/shard_map/ppermute | solution.py:242
  33.6 0.4 collective-permute-done.9
  33.9 2.1 %collective-permute-start.10 = (f32[16,128]{1,0:T(8,128)S(1)}, f32[16,128]{1,0:T(8,128)S(1)}, u32[]{:S(2)}, u32[]{:S(2)}) collective-permute-start(f32[16,128]{1,0:T(8,128)S(1)} %constant_dynamic-update-slice_fusion.near), channel_id=1, source_target_pairs={{0,8},{8,0},{4,12},{12,4},{1,9},{9,1},{5,13},{13,5},{2,10},{10,2},... | collective-permute-start | bytes 24584 | tf_op jit(solution)/shard_map/ppermute | solution.py:233
  36.1 1.6 %collective-permute-done.12 = f32[2,128,128]{2,1,0:T(8,128)S(1)} collective-permute-done((f32[2,128,128]{2,1,0:T(8,128)S(1)}, f32[2,128,128]{2,1,0:T(8,128)S(1)}, u32[]{:S(2)}, u32[]{:S(2)}) %collective-permute-start.12) | collective-permute-done | bytes 131104 | tf_op jit(solution)/shard_map/ppermute | solution.py:242
  37.6 0.1 collective-permute-start.13
  37.7 0.8 %collective-permute-done.10.far = f32[16,128]{1,0:T(8,128)S(1)} collective-permute-done((f32[16,128]{1,0:T(8,128)S(1)}, f32[16,128]{1,0:T(8,128)S(1)}, u32[]{:S(2)}, u32[]{:S(2)}) %collective-permute-start.10) | collective-permute-done | bytes 8224 | tf_op jit(solution)/shard_map/ppermute | solution.py:233
  38.5 0.1 shard_map.83
  38.6 0.5 %collective-permute-done.13.others = f32[2,128,128]{2,1,0:T(8,128)S(1)} collective-permute-done((f32[2,128,128]{2,1,0:T(8,128)S(1)}, f32[2,128,128]{2,1,0:T(8,128)S(1)}, u32[]{:S(2)}, u32[]{:S(2)}) %collective-permute-start.13) | collective-permute-done | bytes 131104 | tf_op jit(solution)/shard_map/ppermute | solution.py:239
  39.1 0.8 %shard_map.84 = (f32[128,512]{1,0:T(8,128)}, f32[1]{0:T(128)}) custom-call(f32[4,128,128]{2,1,0:T(8,128)S(1)} %get-tuple-element.19.valid, f32[8,128]{1,0:T(8,128)S(1)} %get-tuple-element.34.scalars, f32[2,128,128]{2,1,0:T(8,128)S(1)} %get-tuple-element.35.total, f32[2,128,128]{2,1,0:T(8,128)S(1)} %collective-permute-done.13.others, ...), custom_call_target="tpu_custom_call" | custom-call | tf_op jit(solution)/shard_map/pallas_call | solution.py:310
  (9 shorter events, 0.1 us)
Async XLA Ops:
  0.6 17.0 %copy-start = (f32[4,128,128]{2,1,0:T(8,128)S(1)}, f32[4,128,128]{2,1,0:T(8,128)}, u32[]{:S(2)}) copy-start(f32[4,128,128]{2,1,0:T(8,128)} %refs_0_.3) | copy-start | bytes 786436
  0.6 12.5 %collective-permute-start = (f32[4,128,128]{2,1,0:T(8,128)}, f32[4,128,128]{2,1,0:T(8,128)S(1)}, u32[]{:S(2)}, u32[]{:S(2)}) collective-permute-start(f32[4,128,128]{2,1,0:T(8,128)} %refs_0_.3), channel_id=1, source_target_pairs={{0,12},{12,0},{4,8},{8,4},{1,13},{13,1},{5,9},{9,5},{2,14},{14,2},... | collective-permute-start | bytes 786440 | tf_op jit(solution)/shard_map/ppermute | solution.py:236
  5.8 13.5 %collective-permute-start.2 = (f32[4,128,128]{2,1,0:T(8,128)}, f32[4,128,128]{2,1,0:T(8,128)S(1)}, u32[]{:S(2)}, u32[]{:S(2)}) collective-permute-start(f32[4,128,128]{2,1,0:T(8,128)} %refs_0_.3), channel_id=1, source_target_pairs={{0,4},{4,0},{8,12},{12,8},{1,5},{5,1},{9,13},{13,9},{2,6},{6,2},{1... | collective-permute-start | bytes 786440 | tf_op jit(solution)/shard_map/ppermute | solution.py:230
  5.8 1.0 %copy-start.1 = (f32[128,512]{1,0:T(8,128)S(1)}, f32[128,512]{1,0:T(8,128)}, u32[]{:S(2)}) copy-start(f32[128,512]{1,0:T(8,128)} %wave.1) | copy-start | bytes 786436
  6.7 0.9 %copy-start.2 = (f32[4,128,128]{2,1,0:T(8,128)S(1)}, f32[4,128,128]{2,1,0:T(8,128)}, u32[]{:S(2)}) copy-start(f32[4,128,128]{2,1,0:T(8,128)} %left.1) | copy-start | bytes 786436
  7.7 0.7 %copy-start.3 = (s32[4,4]{1,0:T(4,128)S(1)}, s32[4,4]{1,0:T(4,128)}, u32[]{:S(2)}) copy-start(s32[4,4]{1,0:T(4,128)} %pairs.1) | copy-start | bytes 196
  8.3 0.7 %copy-start.4 = (s32[4]{0:T(128)S(1)}, s32[4]{0:T(128)}, u32[]{:S(2)}) copy-start(s32[4]{0:T(128)} %left_sizes.1) | copy-start | bytes 52
  9.0 0.7 %copy-start.5 = (s32[4]{0:T(128)S(1)}, s32[4]{0:T(128)}, u32[]{:S(2)}) copy-start(s32[4]{0:T(128)} %right_sizes.1) | copy-start | bytes 52
  13.2 10.4 %collective-permute-start.4 = (f32[4,128,128]{2,1,0:T(8,128)S(1)}, f32[4,128,128]{2,1,0:T(8,128)S(1)}, u32[]{:S(2)}, u32[]{:S(2)}) collective-permute-start(f32[4,128,128]{2,1,0:T(8,128)S(1)} %collective-permute-done.refs_1_.refs_2_), channel_id=1, source_target_pairs={{0,4},{4,0},{8,12},{12,8},{1,5},{5,1},{9,13},{13,9},{2,6},{6,2},{1... | collective-permute-start | bytes 786440 | tf_op jit(solution)/shard_map/ppermute | solution.py:230
  17.9 1.3 %collective-permute-start.1 = (f32[1,128,128]{2,1,0:T(8,128)S(1)}, f32[1,128,128]{2,1,0:T(8,128)S(1)}, u32[]{:S(2)}, u32[]{:S(2)}) collective-permute-start(f32[1,128,128]{2,1,0:T(8,128)S(1)} %shard_map.78), channel_id=1, source_target_pairs={{0,1},{1,0},{2,3},{3,2},{4,5},{5,4},{6,7},{7,6},{8,9},{9,8},{10,11... | collective-permute-start | bytes 196616 | tf_op jit(solution)/shard_map/ppermute | solution.py:239
  19.8 1.4 %collective-permute-start.3 = (f32[2,128,128]{2,1,0:T(8,128)S(1)}, f32[2,128,128]{2,1,0:T(8,128)S(1)}, u32[]{:S(2)}, u32[]{:S(2)}) collective-permute-start(f32[2,128,128]{2,1,0:T(8,128)S(1)} %shard_map.79), channel_id=1, source_target_pairs={{0,1},{1,0},{2,3},{3,2},{4,5},{5,4},{6,7},{7,6},{8,9},{9,8},{10,11... | collective-permute-start | bytes 393224 | tf_op jit(solution)/shard_map/ppermute | solution.py:239
  21.2 7.1 %collective-permute-start.8 = (f32[2,128,128]{2,1,0:T(8,128)S(1)}, f32[2,128,128]{2,1,0:T(8,128)S(1)}, u32[]{:S(2)}, u32[]{:S(2)}) collective-permute-start(f32[2,128,128]{2,1,0:T(8,128)S(1)} %add.16), channel_id=1, source_target_pairs={{0,2},{1,3},{2,0},{3,1},{4,6},{5,7},{6,4},{7,5},{8,10},{9,11},{10,... | collective-permute-start | bytes 393224 | tf_op jit(solution)/shard_map/ppermute | solution.py:242
  22.8 5.5 %collective-permute-start.7 = (f32[1,128,128]{2,1,0:T(8,128)S(1)}, f32[1,128,128]{2,1,0:T(8,128)S(1)}, u32[]{:S(2)}, u32[]{:S(2)}) collective-permute-start(f32[1,128,128]{2,1,0:T(8,128)S(1)} %add.15), channel_id=1, source_target_pairs={{0,2},{1,3},{2,0},{3,1},{4,6},{5,7},{6,4},{7,5},{8,10},{9,11},{10,... | collective-permute-start | bytes 196616 | tf_op jit(solution)/shard_map/ppermute | solution.py:242
  23.9 1.3 %collective-permute-start.5 = (f32[1,128,128]{2,1,0:T(8,128)S(1)}, f32[1,128,128]{2,1,0:T(8,128)S(1)}, u32[]{:S(2)}, u32[]{:S(2)}) collective-permute-start(f32[1,128,128]{2,1,0:T(8,128)S(1)} %shard_map.80), channel_id=1, source_target_pairs={{0,1},{1,0},{2,3},{3,2},{4,5},{5,4},{6,7},{7,6},{8,9},{9,8},{10,11... | collective-permute-start | bytes 196616 | tf_op jit(solution)/shard_map/ppermute | solution.py:239
  25.3 4.4 %collective-permute-start.6 = (f32[1,128,128]{2,1,0:T(8,128)S(1)}, f32[1,128,128]{2,1,0:T(8,128)S(1)}, u32[]{:S(2)}, u32[]{:S(2)}) collective-permute-start(f32[1,128,128]{2,1,0:T(8,128)S(1)} %add.17.own), channel_id=1, source_target_pairs={{0,2},{1,3},{2,0},{3,1},{4,6},{5,7},{6,4},{7,5},{8,10},{9,11},{10,... | collective-permute-start | bytes 196616 | tf_op jit(solution)/shard_map/ppermute | solution.py:242
  30.2 1.8 %collective-permute-start.11 = (f32[2,128,128]{2,1,0:T(8,128)S(1)}, f32[2,128,128]{2,1,0:T(8,128)S(1)}, u32[]{:S(2)}, u32[]{:S(2)}) collective-permute-start(f32[2,128,128]{2,1,0:T(8,128)S(1)} %get-tuple-element.31), channel_id=1, source_target_pairs={{0,1},{1,0},{2,3},{3,2},{4,5},{5,4},{6,7},{7,6},{8,9},{9,8},{10,11... | collective-permute-start | bytes 393224 | tf_op jit(solution)/shard_map/ppermute | solution.py:239
  30.3 3.7 %collective-permute-start.9 = (f32[8,128]{1,0:T(8,128)S(1)}, f32[8,128]{1,0:T(8,128)S(1)}, u32[]{:S(2)}, u32[]{:S(2)}) collective-permute-start(f32[8,128]{1,0:T(8,128)S(1)} %get-tuple-element.29), channel_id=1, source_target_pairs={{0,4},{4,0},{8,12},{12,8},{1,5},{5,1},{9,13},{13,9},{2,6},{6,2},{1... | collective-permute-start | bytes 12296 | tf_op jit(solution)/shard_map/ppermute | solution.py:230
  32.0 5.6 %collective-permute-start.12 = (f32[2,128,128]{2,1,0:T(8,128)S(1)}, f32[2,128,128]{2,1,0:T(8,128)S(1)}, u32[]{:S(2)}, u32[]{:S(2)}) collective-permute-start(f32[2,128,128]{2,1,0:T(8,128)S(1)} %add.18), channel_id=1, source_target_pairs={{0,2},{1,3},{2,0},{3,1},{4,6},{5,7},{6,4},{7,5},{8,10},{9,11},{10,... | collective-permute-start | bytes 393224 | tf_op jit(solution)/shard_map/ppermute | solution.py:242
  33.9 4.5 %collective-permute-start.10 = (f32[16,128]{1,0:T(8,128)S(1)}, f32[16,128]{1,0:T(8,128)S(1)}, u32[]{:S(2)}, u32[]{:S(2)}) collective-permute-start(f32[16,128]{1,0:T(8,128)S(1)} %constant_dynamic-update-slice_fusion.near), channel_id=1, source_target_pairs={{0,8},{8,0},{4,12},{12,4},{1,9},{9,1},{5,13},{13,5},{2,10},{10,2},... | collective-permute-start | bytes 24584 | tf_op jit(solution)/shard_map/ppermute | solution.py:233
  37.6 1.4 %collective-permute-start.13 = (f32[2,128,128]{2,1,0:T(8,128)S(1)}, f32[2,128,128]{2,1,0:T(8,128)S(1)}, u32[]{:S(2)}, u32[]{:S(2)}) collective-permute-start(f32[2,128,128]{2,1,0:T(8,128)S(1)} %add.19.total), channel_id=1, source_target_pairs={{0,1},{1,0},{2,3},{3,2},{4,5},{5,4},{6,7},{7,6},{8,9},{9,8},{10,11... | collective-permute-start | bytes 393224 | tf_op jit(solution)/shard_map/ppermute | solution.py:239
